TPU v7x, 128 devices: a whole 4x4x4 slice. The times are simulated.
128 devices in a mesh: member: 4 (over y), tile: 32 (over x, z, core).
Axes of the slice: x: 4, y: 4, z: 4, core: 2. Of those that a mesh axis runs over, the one named last changes fastest.
Arguments:
- alpha: float32 [80, 4, 64, 1440], P('member', None, 'tile'), may hold values from -6 to 6
- ensemble: bfloat16 [80, 4, 4, 64, 1440], P('member', None, None, 'tile'), may hold values from -6 to 6
- step_count: int32 [4], replicated, may hold values from 1 to 8
- obs_index: int32 [32, 32, 4, 1024], P('tile'), may hold values from 0 to 46079, as said below
- obs_weight: float32 [32, 32, 4, 1024], P('tile'), may hold values from 0 to 0.5
- obs_count: int32 [32, 32], P('tile'), may hold values from 0 to 1024
- obs_value: float32 [32, 32, 1024], P(None, 'tile'), may hold values from -6 to 6
- inv_var: float32 [32, 32, 1024], P(None, 'tile'), may hold values from 2 to 32
Outputs:
- gradient: float32 [80, 4, 64, 1440], P('member', None, 'tile')
- departure: float32 [32, 32, 1024], P('tile')
Inputs may be any that keep to these rules, and one draw needn't show every extreme that they name: `obs_index`: all four corners of a slot name one field and level; they are two neighbouring rows of the owner tile and two neighbouring columns, the column after the last being the first.
All inputs are finite; a program needn't handle non-finite values.
Results may differ from a plain program's by a relative error of at most 0.0003.
Values sent between devices are 32-bit elements; how exact they have to be, the bound alone decides.
No kernel may reach another device: no remote copies, remote signals or barrier semaphores. Data moves between devices by JAX's collectives and lax.ppermute only.
A program may use at most 64 MiB of HBM per device.

v0:
```python
import math

import jax
import jax.numpy as jnp
from jax import lax
from jax.sharding import PartitionSpec as P

KMAX = 8


def with_halo(value, sides, width):
    for axis, dim in sides:
        size, length = (lax.axis_size(axis), value.shape[dim])
        up = [(i, (i + 1) % size) for i in range(size - 1)]
        down = [(j, i) for i, j in up]
        last = lax.slice_in_dim(value, length - width, length, axis=dim)
        initial = lax.slice_in_dim(value, 0, width, axis=dim)
        before = lax.ppermute(last, axis, up)
        after = lax.ppermute(initial, axis, down)
        value = jnp.concatenate([before, value, after], axis=dim)
    return value


def laplace_step(value, padded, active):
    laplace = (
        padded[:, :, :-2]
        + padded[:, :, 2:]
        + jnp.roll(value, 1, 3)
        + jnp.roll(value, -1, 3)
        - 4.0 * value
    )
    return value + 0.2 * active[None, :, None, None] * laplace


def diffuse(field, step_count):
    value = field
    for step in range(KMAX):
        active = (step < step_count).astype(jnp.float32)
        padded = with_halo(value, (("tile", 2),), 1)
        value = laplace_step(value, padded, active)
    return value


def shards(alpha, ensemble, step_count, obs_index, obs_weight, obs_count, obs_value, inv_var):
    fields = ensemble.shape[1]
    levels, rows, columns = (alpha.shape[1], alpha.shape[2], alpha.shape[3])
    scale = 1.0 / math.sqrt(alpha.shape[0] * lax.axis_size("member") - 1)
    local = diffuse(alpha, step_count)
    partial_value = jnp.sum(ensemble.astype(jnp.float32) * local[:, None], axis=0)
    tile_index = obs_index[0]
    tile_weight = obs_weight[0]
    increment = lax.psum(partial_value, "member") * scale
    model_obs = jnp.sum(tile_weight * increment.reshape(-1)[tile_index], axis=1)
    at_source = lax.all_to_all(model_obs[None], "tile", split_axis=1, concat_axis=0, tiled=True)
    weighted = inv_var * (obs_value - at_source)
    returned = lax.all_to_all(weighted, "tile", split_axis=0, concat_axis=1, tiled=True)[0]
    live = jnp.arange(returned.shape[1], dtype=jnp.int32)[None, :] < obs_count[0][:, None]
    departure = jnp.where(live, returned, jnp.float32(0.0))
    spread = tile_weight * departure[:, None, :]
    adjoint = jax.ops.segment_sum(
        spread.ravel(), tile_index.ravel(), fields * levels * rows * columns
    )
    adjoint = adjoint.reshape(fields, levels, rows, columns)
    project = jnp.sum(ensemble.astype(jnp.float32) * adjoint[None], axis=1) * scale
    gradient = alpha - diffuse(project, step_count)
    return (gradient, departure[None])


def solution(mesh):
    return jax.shard_map(
        shards,
        mesh=mesh,
        in_specs=(
            P("member", None, "tile", None),
            P("member", None, None, "tile", None),
            P(),
            P("tile", None, None, None),
            P("tile", None, None, None),
            P("tile", None),
            P(None, "tile", None),
            P(None, "tile", None),
        ),
        out_specs=(P("member", None, "tile", None), P("tile", None, None)),
        check_vma=False,
    )
```

profile of v0, /device:TPU:1, one launch (start us, length us, event | category | flops | bytes accessed | tf_op | source)
XLA Modules:
  0.0 1828.1 jit_solution(565939133242376277)
XLA Ops:
  7.2 2.6 fusion.116
  10.0 4.9 collective-permute-start
  18.6 3.1 collective-permute-done
  22.3 4.1 collective-permute-done.1
  26.8 3.5 multiply_add_fusion.14
  33.6 2.7 collective-permute-start.3
  37.4 2.8 collective-permute-done.2
  40.7 4.3 collective-permute-done.3
  45.6 3.5 multiply_add_fusion.13
  55.8 3.1 collective-permute-done.4
  59.4 4.1 collective-permute-done.5
  64.0 3.5 multiply_add_fusion.12
  70.7 3.0 collective-permute-start.7
  77.9 4.7 collective-permute-done.7
  83.1 3.5 multiply_add_fusion.11
  93.3 3.1 collective-permute-done.8
  96.9 6.2 collective-permute-done.9
  103.6 3.5 multiply_add_fusion.10
  110.3 2.6 collective-permute-start.11
  114.1 2.9 collective-permute-done.10
  117.5 6.2 collective-permute-done.11
  124.2 3.5 multiply_add_fusion.9
  134.4 3.1 collective-permute-done.12
  138.0 6.2 collective-permute-done.13
  144.7 3.5 multiply_add_fusion.8
  151.4 2.7 collective-permute-start.15
  155.2 2.9 collective-permute-done.14
  158.6 6.2 collective-permute-done.15
  165.3 3.5 multiply_add_fusion.7
  168.8 2.8 fusion
  171.8 46.8 %all-reduce.2.cloned.1.call-done = f32[4,4,2,1440]{3,2,1,0:T(2,128)} async-done(((f32[4,4,2,1440]{3,2,1,0:T(2,128)}), f32[4,4,2,1440]{3,2,1,0:T(2,128)}) %all-reduce.2.cloned.1.call-update) | async-done | bytes 184336 | tf_op jit(solution)/shard_map/psum | solution.py:52
  219.8 724.9 %gather_fusion = f32[131072]{0:T(1024)S(1)} fusion(f32[46080]{0:T(1024)S(1)} %reshape.147, s32[131072]{0:T(1024)S(1)} %broadcast_clamp_fusion), kind=kCustom, calls=%fused_computation | custom fusion | bytes 1572864 | tf_op jit(solution)/shard_map/gather | solution.py:53
  945.5 17.3 all_to_all.21
  963.6 3.9 all-to-all-start.1
  968.4 6.9 all-to-all-done.1
  975.8 683.3 %scatter_custom_fusion = f32[46080]{0:T(1024)S(1)} fusion(s32[131072]{0:T(1024)} %bitcast.33, f32[131072]{0:T(1024)S(1)} %mul.292, f32[]{:T(128)} %constant.14.clone.1), kind=kCustom, calls=%fused_computation.131 | custom fusion | flops 131072 | bytes 184832 | tf_op jit(solution)/shard_map/scatter-add | solution.py:60
  1670.0 2.7 collective-permute-done.16
  1673.2 4.1 collective-permute-done.17
  1677.8 3.5 multiply_add_fusion.6
  1684.5 2.6 collective-permute-start.19
  1688.2 2.9 collective-permute-done.18
  1691.6 4.1 collective-permute-done.19
  1696.2 3.5 multiply_add_fusion.5
  1706.5 3.1 collective-permute-done.20
  1710.0 4.1 collective-permute-done.21
  1714.6 3.5 multiply_add_fusion.4
  1721.3 2.7 collective-permute-start.23
  1725.1 2.9 collective-permute-done.22
  1728.5 5.4 collective-permute-done.23
  1734.4 3.5 multiply_add_fusion.3
  1744.7 3.1 collective-permute-done.24
  1748.3 6.2 collective-permute-done.25
  1755.0 3.5 multiply_add_fusion.2
  1761.7 2.8 collective-permute-start.27
  1765.7 2.7 collective-permute-done.26
  1768.8 6.2 collective-permute-done.27
  1775.5 3.5 multiply_add_fusion.1
  1785.8 3.1 collective-permute-done.28
  1789.4 6.2 collective-permute-done.29
  1796.1 3.5 multiply_add_fusion
  1802.8 2.6 collective-permute-start.31
  1806.5 2.9 collective-permute-done.30
  1809.9 6.2 collective-permute-done.31
  1816.6 4.5 add_subtract_fusion
  (213 shorter events, 111.6 us)
Async XLA Ops:
  7.2 9.9 copy-start
  7.2 10.0 copy-start.26
  7.2 10.0 copy-start.5
  7.2 211.4 %all-reduce.2.cloned.1.call-start = ((), (), s32[]{:S(2)}) async-start(), calls=%async_computation.2 | async-start | bytes 393216 | tf_op jit(solution)/shard_map/psum | solution.py:52
  10.0 11.7 collective-permute-start
  15.1 11.2 collective-permute-start.1
  17.2 9.6 copy-start.11
  17.2 28.3 %copy-start.23 = (f32[4]{0:T(128)}, f32[4]{0:T(128)S(1)}, u32[]{:S(2)}) copy-start(f32[4]{0:T(128)S(1)} %get-tuple-element.107) | copy-start | bytes 52
  17.3 46.7 %copy-start.21 = (f32[4]{0:T(128)}, f32[4]{0:T(128)S(1)}, u32[]{:S(2)}) copy-start(f32[4]{0:T(128)S(1)} %get-tuple-element.106) | copy-start | bytes 52
  17.3 65.8 %copy-start.19 = (f32[4]{0:T(128)}, f32[4]{0:T(128)S(1)}, u32[]{:S(2)}) copy-start(f32[4]{0:T(128)S(1)} %get-tuple-element.105) | copy-start | bytes 52
  17.3 86.3 %copy-start.17 = (f32[4]{0:T(128)}, f32[4]{0:T(128)S(1)}, u32[]{:S(2)}) copy-start(f32[4]{0:T(128)S(1)} %get-tuple-element.104) | copy-start | bytes 52
  17.3 106.9 %copy-start.15 = (f32[4]{0:T(128)}, f32[4]{0:T(128)S(1)}, u32[]{:S(2)}) copy-start(f32[4]{0:T(128)S(1)} %get-tuple-element.103) | copy-start | bytes 52
  17.3 127.4 %copy-start.13 = (f32[4]{0:T(128)}, f32[4]{0:T(128)S(1)}, u32[]{:S(2)}) copy-start(f32[4]{0:T(128)S(1)} %get-tuple-element.109) | copy-start | bytes 52
  17.3 148.0 %copy-start.9 = (f32[4]{0:T(128)}, f32[4]{0:T(128)S(1)}, u32[]{:S(2)}) copy-start(f32[4]{0:T(128)S(1)} %get-tuple-element.102) | copy-start | bytes 52
  31.5 8.7 collective-permute-start.2
  33.6 11.5 collective-permute-start.3
  50.2 8.7 collective-permute-start.4
  52.3 11.2 collective-permute-start.5
  68.6 8.7 collective-permute-start.6
  70.7 11.8 collective-permute-start.7
  87.7 8.7 collective-permute-start.8
  89.8 13.3 collective-permute-start.9
  108.2 8.7 collective-permute-start.10
  110.3 13.3 collective-permute-start.11
  128.8 8.7 collective-permute-start.12
  130.9 13.3 collective-permute-start.13
  149.3 8.7 collective-permute-start.14
  151.4 13.3 collective-permute-start.15
  165.3 3.6 copy-start.2
  219.8 725.1 %copy-start.4 = (f32[1,32,4,1024]{3,2,1,0:T(4,128)S(1)}, f32[1,32,4,1024]{3,2,1,0:T(4,128)}, u32[]{:S(2)}) copy-start(f32[1,32,4,1024]{3,2,1,0:T(4,128)} %param.12) | copy-start | bytes 1572868
  944.7 18.1 copy-start.7
  944.7 18.1 copy-start.8
  944.9 22.6 %copy-start.6 = (s32[1,32,4,1024]{3,2,1,0:T(4,128)S(1)}, s32[1,32,4,1024]{3,2,1,0:T(4,128)}, u32[]{:S(2)}) copy-start(s32[1,32,4,1024]{3,2,1,0:T(4,128)} %param.11) | copy-start | bytes 1572868
  945.4 30.0 %copy-start.25 = (s32[1,32]{1,0:T(1,128)S(1)}, s32[1,32]{1,0:T(1,128)}, u32[]{:S(2)}) copy-start(s32[1,32]{1,0:T(1,128)} %param.13) | copy-start | bytes 388
  963.6 11.7 all-to-all-start.1
  975.6 683.9 %copy-start.3 = (bf16[20,4,4,2,1440]{4,3,2,1,0:T(2,128)(2,1)S(1)}, bf16[20,4,4,2,1440]{4,3,2,1,0:T(2,128)(2,1)}, u32[]{:S(2)}) copy-start(bf16[20,4,4,2,1440]{4,3,2,1,0:T(2,128)(2,1)} %param.9) | copy-start | bytes 5529604
  1663.5 9.3 collective-permute-start.16
  1666.1 11.2 collective-permute-start.17
  1670.0 7.8 copy-start.12
  1682.4 8.7 collective-permute-start.18
  1684.5 11.2 collective-permute-start.19
  1688.2 8.0 copy-start.24
  1700.8 8.7 collective-permute-start.20
  1702.9 11.2 collective-permute-start.21
  1706.4 8.2 copy-start.22
  1719.2 8.7 collective-permute-start.22
  1721.3 12.6 collective-permute-start.23
  1725.1 9.3 copy-start.20
  1739.0 8.7 collective-permute-start.24
  1741.1 13.3 collective-permute-start.25
  1744.7 10.3 copy-start.18
  1759.6 8.7 collective-permute-start.26
  1761.7 13.3 collective-permute-start.27
  1765.6 9.9 copy-start.16
  1780.1 8.7 collective-permute-start.28
  1782.2 13.3 collective-permute-start.29
  1785.8 10.3 copy-start.14
  1800.7 8.7 collective-permute-start.30
  1802.8 13.3 collective-permute-start.31
  1806.5 10.1 copy-start.1
  1806.5 10.1 copy-start.10
Sparse Core Ops, SparseCore 0:
  171.8 46.6 all-reduce.1
where the time goes:
time: 1840 us; the launch traced here: 1830 us
  local copies, waits for them, and re-layouts  783 us (43%)
  other arithmetic  749 us (41%)
  waiting for transfers between devices  185 us (10%)
  starting transfers between devices  78.4 us (4%)
    gather x2, local copies, waits for them, and re-layouts, shards(): model_obs = jnp.sum(tile_weight * increment.reshape(-1)[tile_index], axis=1)  725 us
    scatter-add x1, other arithmetic, shards(): jax.ops.segment_sum(spread.ravel(), tile_index.ravel(), fields * levels *...  683 us
    ppermute x16, waiting for transfers between devices, with_halo(): after = lax.ppermute(initial, axis, down)  84 us
    add x15, other arithmetic, laplace_step(): return value + 0.2 * active[None, :, None, None] * laplace  52.9 us
    ppermute x16, waiting for transfers between devices, with_halo(): before = lax.ppermute(last, axis, up)  46.9 us
    psum x1, waiting for transfers between devices, shards(): increment = lax.psum(partial_value, 'member') * scale  46.8 us
    ppermute x16, starting transfers between devices, with_halo(): after = lax.ppermute(initial, axis, down)  40.1 us
  transfers between devices with their start and end apart: 34, of which 34 were waited for; matrix products, arithmetic and copies ran while one was open for 2% of the time, Pallas kernels for 0%

commit v1 on v0

v1 whole, which is shorter than its diff:
```python
import math

import jax
import jax.numpy as jnp
from jax import lax
from jax.experimental import pallas as pl
from jax.experimental.pallas import tpu as pltpu
from jax.sharding import PartitionSpec as P

FLD, LEV, ROWS, LON = 4, 4, 2, 1440
TILES, SLOT, GROUP = 32, 1024, 20
LAT = TILES * ROWS
CH = FLD * LEV
KMAX = 8

PIECES = 5
MGRP = GROUP // PIECES
HALF = LON // 2
PIECE = HALF + 2 * KMAX
LANES = 128
LINE = -(-PIECES * PIECE // LANES)
COLS = -(-LON // LANES)
OBS_ROWS = SLOT // LANES
LINE_OBS = LINE + OBS_ROWS

CHUNK = 90
CHUNKS = LON // CHUNK
HI = CH * CHUNKS
LO = 96
BLOCK = 256
PER_SRC = SLOT // BLOCK
BLOCKS = TILES * PER_SRC

F32, BF16, I32 = jnp.float32, jnp.bfloat16, jnp.int32
VMEM = pl.BlockSpec(memory_space=pltpu.VMEM)
SMEM = pl.BlockSpec(memory_space=pltpu.SMEM)


def params(mib):
    return pltpu.CompilerParams(vmem_limit_bytes=mib * 1024 * 1024)


def lanes8():
    return lax.broadcasted_iota(I32, (8, LANES), 1)


def assemble(fetch, where_from, cache):
    value, start, last = None, 0, None
    segments = []
    for lane in range(LANES):
        src = where_from(lane)
        if src is None:
            continue
        key, tile, at = src
        this = (key, tile, (lane - at) % LANES)
        if this != last:
            segments.append((lane, this))
            last = this
    for start, (key, tile, shift) in segments:
        if (key, tile, shift) not in cache:
            x = fetch(key, tile)
            cache[key, tile, shift] = pltpu.roll(x, shift, 1) if shift else x
        x = cache[key, tile, shift]
        value = x if value is None else jnp.where(lanes8() >= start, x, value)
    return value


def pack_rows(fetch, store, line):
    for mgrp in range(MGRP):
        for half in range(2):
            cache = {}
            for j in range(LINE):

                def where_from(lane):
                    piece, at = divmod(j * LANES + lane, PIECE)
                    if piece >= PIECES:
                        return None
                    col = (at - KMAX + half * HALF) % LON
                    return (piece, col // LANES, col % LANES)

                tile = assemble(lambda piece, t: fetch(piece * MGRP + mgrp, t), where_from, cache)
                store((half * MGRP * 8 + mgrp * 8) * line + j, tile)


def unpack_tile(got_ref, member, t, cache):
    piece, mgrp = divmod(member, MGRP)

    def where_from(lane):
        col = t * LANES + lane
        if col >= LON:
            return None
        half, at = divmod(col, HALF)
        at += piece * PIECE + KMAX
        return (half, at // LANES, at % LANES)

    def fetch(half, j):
        return got_ref[pl.ds((half * MGRP * 8 + mgrp * 8) * LINE + j, 8, stride=LINE), :]

    return assemble(fetch, where_from, cache)


def pack_kernel(alpha_ref, value_ref, var_ref, out_ref):
    def fetch(member, t):
        return alpha_ref[member * 8 : member * 8 + 8, t * LANES : (t + 1) * LANES]

    def store(row, tile):
        out_ref[pl.ds(row, 8, stride=LINE_OBS), :] = tile

    pack_rows(fetch, store, LINE_OBS)
    for d in range(TILES):
        for r, ref in enumerate((value_ref, var_ref)):
            at = (d * 2 + r) * LINE_OBS + LINE
            out_ref[at : at + OBS_ROWS, :] = ref[d * OBS_ROWS : (d + 1) * OBS_ROWS, :]


def diffuse_body(steps_ref, in_ref, out_ref, buf, line):
    lat8 = LAT // 8
    for a in range(lat8):
        for j in range(LINE):
            buf[0, a, :, j * LANES : (j + 1) * LANES] = in_ref[pl.ds(a * line + j, 8, stride=8 * line), :]
    sub = lax.broadcasted_iota(I32, (8, LANES), 0)
    lane = lanes8()

    def step(k, carry):
        now, later = lax.rem(k, 2), lax.rem(k + 1, 2)
        old_right, cur = None, None
        for a in range(lat8):
            right = {}
            left = {}

            def tile(aa, j):
                return buf[now, aa, :, j * LANES : (j + 1) * LANES]

            x = [tile(a, j) for j in range(LINE)]
            right = [pltpu.roll(v, 1, 1) for v in x]
            left = [pltpu.roll(v, LANES - 1, 1) for v in x]
            for j in range(LINE):
                west = jnp.where(lane == 0, right[j - 1], right[j])
                east = jnp.where(lane == LANES - 1, left[(j + 1) % LINE], left[j])
                if a == 0:
                    north = jnp.where(sub == 0, 0.0, pltpu.roll(tile(lat8 - 1, j), 1, 0))
                else:
                    north = tile(a - 1, j)
                if a == lat8 - 1:
                    south = jnp.where(sub == 7, 0.0, pltpu.roll(tile(0, j), 7, 0))
                else:
                    south = tile(a + 1, j)
                laplace = ((north + south) + (west + east)) - 4.0 * x[j]
                buf[later, a, :, j * LANES : (j + 1) * LANES] = x[j] + 0.2 * laplace
        return carry

    count = steps_ref[0]
    lax.fori_loop(0, count, step, 0)
    end = lax.rem(count, 2)
    for a in range(lat8):
        for j in range(LINE):
            out_ref[pl.ds(a * LINE + j, 8, stride=8 * LINE), :] = buf[end, a, :, j * LANES : (j + 1) * LANES]


def diffuse_first_kernel(steps_ref, in_ref, out_ref, value_ref, var_ref, buf):
    diffuse_body(steps_ref, in_ref, out_ref, buf, LINE_OBS)
    for t in range(TILES):
        for r, ref in enumerate((value_ref, var_ref)):
            at = (t * 2 + r) * LINE_OBS + LINE
            ref[t * OBS_ROWS : (t + 1) * OBS_ROWS, :] = in_ref[at : at + OBS_ROWS, :]


def diffuse_kernel(steps_ref, in_ref, out_ref, buf):
    diffuse_body(steps_ref, in_ref, out_ref, buf, LINE)


def slots_kernel(index_ref, weight_ref, out_ref):
    def body(s, carry):
        index = index_ref[s]
        weight = weight_ref[s]
        at = index.astype(F32) + 0.5
        chan = jnp.floor(at * (1.0 / (ROWS * LON)))
        rest = at - chan * (ROWS * LON)
        below = rest > LON
        col = jnp.where(below, rest - LON, rest) - 0.5
        low, high = jnp.min(col, 0, keepdims=True), jnp.max(col, 0, keepdims=True)
        base = jnp.where(high - low > 1.5, high, low)
        chunk = jnp.floor((base + 0.5) * (1.0 / CHUNK))
        first = col == base
        rows = [chunk * CH + chan[0:1], base - chunk * CHUNK]
        for row in (jnp.logical_not(below), below):
            for column in (first, jnp.logical_not(first)):
                rows.append(jnp.sum(jnp.where(row & column, weight, 0.0), 0, keepdims=True))
        for k, row in enumerate(rows):
            out_ref[s, k : k + 1, :] = row
        return carry

    lax.fori_loop(0, TILES, body, 0)


def live_blocks(count_ref, list_ref, pad):
    def body(s, n):
        for j in range(PER_SRC):
            list_ref[n + j] = s * PER_SRC + j
        return n + lax.div(count_ref[s] + (BLOCK - 1), BLOCK)

    n = lax.fori_loop(0, TILES, body, 0)
    for j in range(pad):
        list_ref[n + j] = 0
    return n


def slot_rows(slot_ref, b):
    s = lax.div(b, PER_SRC)
    at = pl.multiple_of(lax.rem(b, PER_SRC) * BLOCK, BLOCK)
    return [slot_ref[s, k : k + 1, pl.ds(at, BLOCK)] for k in range(6)]


def one_hot(high):
    rows = lax.broadcasted_iota(I32, (HI, BLOCK), 0).astype(F32).astype(BF16)
    return jnp.where(rows == high.astype(BF16), jnp.ones((), BF16), jnp.zeros((), BF16))


def split(x):
    high = x.astype(BF16)
    return high, (x - high.astype(F32)).astype(BF16)


UNROLL = 2


def observe_kernel(scale, count_ref, got_ref, ens_ref, slot_ref, out_ref, inc_ref, table_ref, list_ref):
    for t in range(COLS):
        total = [jnp.zeros((8, LANES), F32) for f in range(FLD)]
        for m in range(GROUP):
            local = unpack_tile(got_ref, m, t, {})
            for pair in range(FLD // 2):
                ens = ens_ref[m, pair, :, t * LANES : (t + 1) * LANES].astype(F32)
                total[2 * pair] += ens[:8] * local
                total[2 * pair + 1] += ens[8:] * local
        for f in range(FLD):
            inc_ref[t, f * 8 : f * 8 + 8, :] = total[f] * scale
    for q in range(CHUNKS):
        for f in range(FLD):

            def where_from(lane):
                if lane > CHUNK:
                    return None
                col = (q * CHUNK + lane) % LON
                return (0, col // LANES, col % LANES)

            tile = assemble(lambda key, t: inc_ref[t, f * 8 : f * 8 + 8, :], where_from, {})
            table_ref[q * 32 + f * 8 : q * 32 + f * 8 + 8, :] = tile
    parts = []
    for r in range(ROWS):
        turned = table_ref[pl.ds(r, HI, stride=2), :].T
        parts.append(split(turned[:LO]))
    left = jnp.concatenate([parts[0][0], parts[1][0], parts[0][1], parts[1][1]], 0)

    out_ref[...] = jnp.zeros_like(out_ref)
    n = live_blocks(count_ref, list_ref, UNROLL)
    columns = lax.broadcasted_iota(I32, (LO, BLOCK), 0).astype(F32)

    def body(i, carry):
        for u in range(UNROLL):
            b = list_ref[i * UNROLL + u]
            high, low, w00, w01, w10, w11 = slot_rows(slot_ref, b)
            picked = jnp.dot(left, one_hot(high), preferred_element_type=F32)
            both = picked[: 2 * LO] + picked[2 * LO :]
            here, after = columns == low, columns == low + 1.0
            value = jnp.where(here, w00, jnp.where(after, w01, 0.0)) * both[:LO]
            value += jnp.where(here, w10, jnp.where(after, w11, 0.0)) * both[LO:]
            value = jnp.sum(value, 0, keepdims=True)
            for h in range(BLOCK // LANES):
                out_ref[pl.ds(b * (BLOCK // LANES) + h, 1), :] = value[:, h * LANES : (h + 1) * LANES]
        return carry

    lax.fori_loop(0, lax.div(n + UNROLL - 1, UNROLL), body, 0)


def adjoint_kernel(scale, count_ref, m0, m1, m2, m3, value_ref, var_ref, slot_ref, ens_ref, out_ref, dep_ref, acc_ref,
                   table_ref, adj_ref, proj_ref, list_ref):
    slot_at = lax.broadcasted_iota(I32, (OBS_ROWS, LANES), 0) * LANES + lax.broadcasted_iota(I32, (OBS_ROWS, LANES), 1)
    for s in range(TILES):
        at = slice(s * OBS_ROWS, (s + 1) * OBS_ROWS)
        model = (m0[at, :] + m1[at, :]) + (m2[at, :] + m3[at, :])
        weighted = var_ref[at, :] * (value_ref[at, :] - model)
        dep_ref[at, :] = jnp.where(slot_at < count_ref[s], weighted, 0.0)
    acc_ref[...] = jnp.zeros_like(acc_ref)
    n = live_blocks(count_ref, list_ref, UNROLL)
    columns = lax.broadcasted_iota(I32, (LO, BLOCK), 0).astype(F32).astype(BF16)

    def body(i, carry):
        total = acc_ref[...]
        for u in range(UNROLL):
            at = i * UNROLL + u
            b = list_ref[at]
            live = (at < n).astype(F32)
            high, low, w00, w01, w10, w11 = slot_rows(slot_ref, b)
            per = BLOCK // LANES
            dep = jnp.concatenate([dep_ref[pl.ds(b * per + h, 1), :] for h in range(per)], 1) * live
            here, after = columns == low.astype(BF16), columns == (low + 1.0).astype(BF16)
            halves = []
            for first, second in ((w00, w01), (w10, w11)):
                first, second = split(first * dep), split(second * dep)
                zero = jnp.zeros((), BF16)
                halves.append([jnp.where(here, x, jnp.where(after, y, zero)) for x, y in zip(first, second)])
            spread = jnp.concatenate([halves[0][0], halves[1][0], halves[0][1], halves[1][1]], 0)
            total += lax.dot_general(spread, one_hot(high), (((1,), (1,)), ((), ())), preferred_element_type=F32)
        acc_ref[...] = total
        return carry

    lax.fori_loop(0, lax.div(n + UNROLL - 1, UNROLL), body, 0)
    both = acc_ref[: 2 * LO, :] + acc_ref[2 * LO :, :]
    for r in range(ROWS):
        part = jnp.concatenate([both[r * LO : (r + 1) * LO], jnp.zeros((LANES - LO, HI), F32)], 0)
        table_ref[pl.ds(r, HI, stride=2), :] = part.T * scale
    lane = lanes8()
    for f in range(FLD):
        for t in range(COLS):
            total = jnp.zeros((8, LANES), F32)
            for q in range(-1, CHUNKS):
                first, last = max(q * CHUNK, t * LANES), min(q * CHUNK + CHUNK, t * LANES + LANES - 1, LON - 1)
                if first > last:
                    continue
                chunk = table_ref[(q % CHUNKS) * 32 + f * 8 : (q % CHUNKS) * 32 + f * 8 + 8, :]
                shift = (q * CHUNK - t * LANES) % LANES
                chunk = pltpu.roll(chunk, shift, 1) if shift else chunk
                mask = (lane >= first - t * LANES) & (lane <= last - t * LANES)
                total += jnp.where(mask, chunk, 0.0)
            adj_ref[t, f * 8 : f * 8 + 8, :] = total
    for t in range(COLS):
        adj = [adj_ref[t, f * 8 : f * 8 + 8, :] for f in range(FLD)]
        for m in range(GROUP):
            total = jnp.zeros((8, LANES), F32)
            for pair in range(FLD // 2):
                ens = ens_ref[m, pair, :, t * LANES : (t + 1) * LANES].astype(F32)
                total += ens[:8] * adj[2 * pair] + ens[8:] * adj[2 * pair + 1]
            proj_ref[t, m * 8 : m * 8 + 8, :] = total

    def store(row, tile):
        out_ref[pl.ds(row, 8, stride=LINE), :] = tile

    pack_rows(lambda m, t: proj_ref[t, m * 8 : m * 8 + 8, :], store, LINE)


def gradient_kernel(alpha_ref, got_ref, out_ref):
    for m in range(GROUP):
        cache = {}
        for t in range(COLS):
            width = min(LANES, LON - t * LANES)
            tile = unpack_tile(got_ref, m, t, cache)
            at = (slice(m * 8, m * 8 + 8), slice(t * LANES, t * LANES + width))
            out_ref[at] = alpha_ref[at] - tile[:, :width]


def shape(*dims, dtype=F32):
    return jax.ShapeDtypeStruct(dims, dtype)


def exchange(x):
    return lax.all_to_all(x, "tile", 0, 0, tiled=True)


def shards(alpha, ensemble, step_count, obs_index, obs_weight, obs_count, obs_value, inv_var):
    members = GROUP * lax.axis_size("member")
    scale = 1.0 / math.sqrt(members - 1)
    me = lax.axis_index("tile")
    steps = lax.dynamic_slice(step_count, (lax.rem(me, LEV),), (1,))
    counts = obs_count[0]
    wide = ((0, 0), (0, COLS * LANES - LON))
    rows = jnp.pad(alpha.reshape(GROUP * 8, LON), wide)
    ens = jnp.pad(ensemble.reshape(GROUP, 2, 16, LON), ((0, 0), (0, 0)) + wide)
    value = obs_value.reshape(TILES * OBS_ROWS, LANES)
    var = inv_var.reshape(TILES * OBS_ROWS, LANES)
    flat = shape(TILES * OBS_ROWS, LANES)

    sent = pl.pallas_call(
        pack_kernel,
        out_shape=shape(LAT * LINE_OBS, LANES),
        in_specs=[VMEM] * 3,
        out_specs=VMEM,
        compiler_params=params(16),
        name="pack",
    )(rows, value, var)
    got = exchange(sent)

    slots = pl.pallas_call(
        slots_kernel,
        out_shape=shape(TILES, 8, SLOT),
        in_specs=[VMEM] * 2,
        out_specs=VMEM,
        compiler_params=params(16),
        cost_estimate=pl.CostEstimate(flops=8000000, bytes_accessed=2097152, transcendentals=0),
        name="slots",
    )(obs_index[0], obs_weight[0])

    buf = pltpu.VMEM((2, 8, 8, LINE * LANES), F32)
    moved, value, var = pl.pallas_call(
        diffuse_first_kernel,
        out_shape=(shape(LAT * LINE, LANES), flat, flat),
        in_specs=[SMEM, VMEM],
        out_specs=[VMEM] * 3,
        scratch_shapes=[buf],
        compiler_params=params(16),
        name="diffuse_first",
    )(steps, got)
    got = exchange(moved)

    block_list = pltpu.SMEM((BLOCKS + 8,), I32)
    mine = pl.pallas_call(
        lambda *refs: observe_kernel(scale, *refs),
        out_shape=flat,
        in_specs=[SMEM] + [VMEM] * 3,
        out_specs=VMEM,
        scratch_shapes=[pltpu.VMEM((COLS, 32, LANES), F32), pltpu.VMEM((2 * HI, LANES), F32), block_list],
        compiler_params=params(16),
        name="observe",
    )(counts, got, ens, slots)
    others = [lax.ppermute(mine, "member", [(i, (i + k) % 4) for i in range(4)]) for k in (1, 3, 2)]

    sent, departure = pl.pallas_call(
        lambda *refs: adjoint_kernel(scale, *refs),
        out_shape=(shape(LAT * LINE, LANES), flat),
        in_specs=[SMEM] + [VMEM] * 8,
        out_specs=[VMEM] * 2,
        scratch_shapes=[
            pltpu.VMEM((4 * LO, HI), F32),
            pltpu.VMEM((2 * HI, LANES), F32),
            pltpu.VMEM((COLS, 32, LANES), F32),
            pltpu.VMEM((COLS, GROUP * 8, LANES), F32),
            block_list,
        ],
        compiler_params=params(20),
        name="adjoint",
    )(counts, mine, *others, value, var, slots, ens)
    got = exchange(sent)

    moved = pl.pallas_call(
        diffuse_kernel,
        out_shape=shape(LAT * LINE, LANES),
        in_specs=[SMEM, VMEM],
        out_specs=VMEM,
        scratch_shapes=[buf],
        compiler_params=params(16),
        name="diffuse",
    )(steps, got)
    got = exchange(moved)

    gradient = pl.pallas_call(
        gradient_kernel,
        out_shape=shape(GROUP * 8, LON),
        in_specs=[VMEM] * 2,
        out_specs=VMEM,
        compiler_params=params(16),
        name="gradient",
    )(rows, got)
    return gradient.reshape(alpha.shape), departure.reshape(1, TILES, SLOT)


def solution(mesh):
    return jax.shard_map(
        shards,
        mesh=mesh,
        in_specs=(
            P("member", None, "tile", None),
            P("member", None, None, "tile", None),
            P(),
            P("tile", None, None, None),
            P("tile", None, None, None),
            P("tile", None),
            P(None, "tile", None),
            P(None, "tile", None),
        ),
        out_specs=(P("member", None, "tile", None), P("tile", None, None)),
        check_vma=False,
    )
```

time: 1840 us -> 167 us (0.09)
  local copies, waits for them, and re-layouts: 783 us -> 22.5 us
  other arithmetic: 749 us -> 0 us
  waiting for transfers between devices: 185 us -> 50.8 us
  starting transfers between devices: 78.4 us -> 23.3 us
  Pallas kernels: 0 us -> 50 us
    gather x2 -> x0, local copies, waits for them, and re-layouts: 725 us -> none  [shards(): model_obs = jnp.sum(tile_weight * increment.reshape(-1)[tile_index], axis=1)]
    scatter-add x1 -> x0, other arithmetic: 683 us -> none  [shards(): jax.ops.segment_sum(spread.ravel(), tile_index.ravel(), fields * levels *...]
    ppermute x32 -> x3, waiting for transfers between devices: 131 us -> 5.51 us  [shards(): lax.ppermute(mine, 'member', [(i, (i + k) % 4) for i in range(4)])]
    ppermute x32 -> x3, starting transfers between devices: 74.4 us -> 4.43 us  [shards(): lax.ppermute(mine, 'member', [(i, (i + k) % 4) for i in range(4)])]
    add x15 -> x0, other arithmetic: 52.9 us -> none  [laplace_step(): return value + 0.2 * active[None, :, None, None] * laplace]
    pallas_call x0 -> x7, Pallas kernels: none -> 50 us  [the longest x1 16.6 us: shards(): pl.pallas_call(lambda *refs: adjoint_kernel(scale, *refs), out_shape=(sha...]
    psum x1 -> x0, waiting for transfers between devices: 46.8 us -> none  [shards(): increment = lax.psum(partial_value, 'member') * scale]
    slice x78 -> x0, local copies, waits for them, and re-layouts: 38.7 us -> none  [the longest x32 20 us: laplace_step(): jnp.roll(value, 1, 3)]
  transfers between devices with their start and end apart: 34 -> 6, of which waited for: 34 -> 6; matrix products, arithmetic and copies ran while one was open for 2% -> 3% of each run, Pallas kernels for 0% -> 2%
where the time goes in v1:
time: 167 us; the launch traced here: 168 us
  waiting for transfers between devices  50.8 us (30%)
  Pallas kernels  50 us (30%)
  starting transfers between devices  23.3 us (14%)
  local copies, waits for them, and re-layouts  22.5 us (13%)
  blocking collectives  20.2 us (12%)
    all_to_all x3, waiting for transfers between devices, exchange(): return lax.all_to_all(x, 'tile', 0, 0, tiled=True)  45.3 us
    all_to_all x1, blocking collectives, exchange(): return lax.all_to_all(x, 'tile', 0, 0, tiled=True)  20.2 us
    all_to_all x3, starting transfers between devices, exchange(): return lax.all_to_all(x, 'tile', 0, 0, tiled=True)  18.8 us
    pallas_call x1, Pallas kernels, shards(): pl.pallas_call(lambda *refs: adjoint_kernel(scale, *refs), out_shape=(sha...  16.6 us
    pallas_call x1, Pallas kernels, shards(): pl.pallas_call(lambda *refs: observe_kernel(scale, *refs), out_shape=flat...  15.5 us
    all_to_all x8, local copies, waits for them, and re-layouts, exchange(): return lax.all_to_all(x, 'tile', 0, 0, tiled=True)  9.5 us
    pallas_call x1, Pallas kernels, shards(): pl.pallas_call(diffuse_first_kernel, out_shape=(shape(LAT * LINE, LANES),...  7.14 us
    pallas_call x1, Pallas kernels, shards(): pl.pallas_call(diffuse_kernel, out_shape=shape(LAT * LINE, LANES), in_spe...  7.1 us
  transfers between devices with their start and end apart: 6, of which 6 were waited for; matrix products, arithmetic and copies ran while one was open for 3% of the time, Pallas kernels for 2%

profile of v1, /device:TPU:1, one launch (start us, length us, event | category | flops | bytes accessed | tf_op | source)
XLA Modules:
  0.0 167.6 jit_solution(11083664943259477308)
XLA Ops:
  0.6 1.9 %reshape.30 = f32[160,1440]{1,0:T(8,128)S(1)} reshape(f32[20,4,2,1440]{3,2,1,0:T(2,128)} %param.8) | data formatting | bytes 1843200 | tf_op jit(solution)/shard_map/reshape | solution.py:367
  2.5 0.0 copy-start.6
  2.5 0.0 copy-start.7
  2.5 0.1 pad.8.alpha_ref
  2.6 0.8 copy-done.6
  3.4 0.1 copy-done.7
  3.5 0.4 pack.1
  3.9 0.0 copy-start
  3.9 0.9 copy-done
  4.8 1.1 all_to_all.28
  6.0 0.0 copy-start.10
  6.0 9.6 %all-to-all-start = ((f32[32,74,128]{2,1,0:T(8,128)}), f32[32,74,128]{2,1,0:T(8,128)}, u32[]{:S(2)}, u32[]{:S(2)}) async-start(f32[32,74,128]{2,1,0:T(8,128)} %all_to_all.28), calls=%async_computation | async-start | bytes 2621440 | tf_op jit(solution)/shard_map/all_to_all | solution.py:357
  15.6 0.0 copy-done.10
  15.6 0.6 dynamic_slice.3.steps_ref
  16.2 19.2 %all-to-all-done = f32[32,74,128]{2,1,0:T(8,128)} async-done(((f32[32,74,128]{2,1,0:T(8,128)}), f32[32,74,128]{2,1,0:T(8,128)}, u32[]{:S(2)}, u32[]{:S(2)}) %all-to-all-start) | async-done | bytes 1212448 | tf_op jit(solution)/shard_map/all_to_all | solution.py:357
  35.4 1.4 all_to_all.30.in_ref
  36.8 7.1 %diffuse_first.1 = (f32[1856,128]{1,0:T(8,128)S(1)}, f32[256,128]{1,0:T(8,128)S(1)}, f32[256,128]{1,0:T(8,128)S(1)}) custom-call(s32[1]{0:T(128)} %dynamic_slice.3.steps_ref, f32[2368,128]{1,0:T(8,128)S(1)} %all_to_all.30.in_ref), custom_call_target="tpu_custom_call" | custom-call | tf_op jit(solution)/shard_map/diffuse_first/pallas_call | solution.py:394
  44.0 1.1 all_to_all.31
  45.0 0.0 copy-start.9
  45.0 4.8 %all-to-all-start.1 = ((f32[32,58,128]{2,1,0:T(8,128)}), f32[32,58,128]{2,1,0:T(8,128)}, u32[]{:S(2)}, u32[]{:S(2)}) async-start(f32[32,58,128]{2,1,0:T(8,128)} %all_to_all.31), calls=%async_computation.1 | async-start | bytes 2097152 | tf_op jit(solution)/shard_map/all_to_all | solution.py:357
  49.8 0.0 copy-done.9
  49.8 2.5 %reshape.33 = bf16[20,2,16,1440]{3,2,1,0:T(8,128)(2,1)} reshape(bf16[20,4,4,2,1440]{4,3,2,1,0:T(2,128)(2,1)S(1)} %copy-done.9) | data formatting | bytes 3686400 | tf_op jit(solution)/shard_map/reshape | solution.py:368
  52.3 0.0 copy-start.4
  52.3 0.0 copy-start.5
  52.3 1.8 %pad.9.refs_2_.refs_8_ = bf16[20,2,16,1536]{3,2,1,0:T(8,128)(2,1)S(1)} pad(bf16[20,2,16,1440]{3,2,1,0:T(8,128)(2,1)} %reshape.33, bf16[]{:T(256)} %constant.14.clone.1), padding=0_0x0_0x0_0x0_96 | pad | bytes 3809282 | tf_op jit(solution)/shard_map/jit(_pad)/pad | solution.py:368
  54.1 0.0 copy-done.4
  54.1 0.0 copy-done.5
  54.2 2.9 %slots.1.refs_3_.refs_7_ = f32[32,8,1024]{2,1,0:T(8,128)S(1)} custom-call(s32[32,4,1024]{2,1,0:T(4,128)S(1)} %bitcast.5, f32[32,4,1024]{2,1,0:T(4,128)S(1)} %bitcast.6), custom_call_target="tpu_custom_call" | custom-call | flops 8000000 | bytes 2097152 | tf_op jit(solution)/shard_map/slots/pallas_call | solution.py:383
  57.1 0.0 copy-start.8
  57.1 9.7 %all-to-all-done.1 = f32[32,58,128]{2,1,0:T(8,128)} async-done(((f32[32,58,128]{2,1,0:T(8,128)}), f32[32,58,128]{2,1,0:T(8,128)}, u32[]{:S(2)}, u32[]{:S(2)}) %all-to-all-start.1) | async-done | bytes 950304 | tf_op jit(solution)/shard_map/all_to_all | solution.py:357
  66.9 2.2 %all_to_all.33.refs_1_ = f32[1856,128]{1,0:T(8,128)} reshape(f32[32,58,128]{2,1,0:T(8,128)} %all-to-all-done.1) | data formatting | bytes 1900544 | tf_op jit(solution)/shard_map/all_to_all | solution.py:357
  69.1 0.0 copy-done.8
  69.1 0.0 copy-start.2
  69.1 1.2 copy-done.2
  70.3 15.5 %observe.1.refs_1_ = f32[256,128]{1,0:T(8,128)S(1)} custom-call(s32[32]{0:T(128)S(1)} %bitcast.9, f32[1856,128]{1,0:T(8,128)S(1)} %copy-done.2, bf16[20,2,16,1536]{3,2,1,0:T(8,128)(2,1)S(1)} %pad.9.refs_2_.refs_8_, f32[32,8,1024]{2,1,0:T(8,128)S(1)} %slots.1.refs_3_.refs_7_), custom_call_target="tpu_custom_call" | custom-call | tf_op jit(solution)/shard_map/observe/pallas_call | solution.py:406
  85.8 1.4 collective-permute-start
  87.2 1.5 collective-permute-start.1
  88.7 1.6 collective-permute-start.2
  90.3 1.5 collective-permute-done.refs_2_
  91.7 0.7 collective-permute-done.1.refs_3_
  92.4 3.4 %collective-permute-done.2.refs_4_ = f32[256,128]{1,0:T(8,128)S(1)} collective-permute-done((f32[256,128]{1,0:T(8,128)S(1)}, f32[256,128]{1,0:T(8,128)S(1)}, u32[]{:S(2)}, u32[]{:S(2)}) %collective-permute-start.2) | collective-permute-done | bytes 131104 | tf_op jit(solution)/shard_map/ppermute | solution.py:415
  95.8 16.6 %adjoint.1 = (f32[1856,128]{1,0:T(8,128)S(1)}, f32[256,128]{1,0:T(8,128)S(1)}) custom-call(s32[32]{0:T(128)S(1)} %bitcast.10, f32[256,128]{1,0:T(8,128)S(1)} %observe.1.refs_1_, f32[256,128]{1,0:T(8,128)S(1)} %collective-permute-done.refs_2_, f32[256,128]{1,0:T(8,128)S(1)} %collective-permute-done.1.refs_3_, f32[256,128]{1,0:T(8,128)S(1)} %collective-permute-done.2.refs_4_, ...), custom_call_target="tpu_custom_call" | custom-call | tf_op jit(solution)/shard_map/adjoint/pallas_call | solution.py:417
  112.3 0.0 copy-start.3
  112.4 0.9 copy-done.3
  113.3 1.3 all_to_all.34
  114.6 20.2 %all_to_all.44 = f32[32,58,128]{2,1,0:T(8,128)S(1)} all-to-all(f32[32,58,128]{2,1,0:T(8,128)S(1)} %all_to_all.34), channel_id=1, replica_groups=mesh['member'=4,'tile'=32] {'tile'}, dimensions={0} | all-to-all | bytes 1900544 | tf_op jit(solution)/shard_map/all_to_all | solution.py:357
  134.8 0.1 all_to_all.36.in_ref
  134.8 7.1 %diffuse.1 = f32[1856,128]{1,0:T(8,128)S(1)} custom-call(s32[1]{0:T(128)} %dynamic_slice.3.steps_ref, f32[1856,128]{1,0:T(8,128)S(1)} %all_to_all.36.in_ref), custom_call_target="tpu_custom_call" | custom-call | tf_op jit(solution)/shard_map/diffuse/pallas_call | solution.py:434
  142.0 1.0 all_to_all.37
  143.0 4.4 %all-to-all-start.3 = ((f32[32,58,128]{2,1,0:T(8,128)}), f32[32,58,128]{2,1,0:T(8,128)}, u32[]{:S(2)}, u32[]{:S(2)}) async-start(f32[32,58,128]{2,1,0:T(8,128)} %all_to_all.37), calls=%async_computation.3 | async-start | bytes 2097152 | tf_op jit(solution)/shard_map/all_to_all | solution.py:357
  147.5 0.0 copy-start.1
  147.5 0.7 reshape.35
  148.2 16.3 %all-to-all-done.3 = f32[32,58,128]{2,1,0:T(8,128)} async-done(((f32[32,58,128]{2,1,0:T(8,128)}), f32[32,58,128]{2,1,0:T(8,128)}, u32[]{:S(2)}, u32[]{:S(2)}) %all-to-all-start.3) | async-done | bytes 950304 | tf_op jit(solution)/shard_map/all_to_all | solution.py:357
  164.4 1.3 all_to_all.39.got_ref
  165.7 0.0 copy-done.1
  165.7 0.3 gradient.1
  166.1 1.5 reshape.34
Async XLA Ops:
  2.5 0.9 copy-start.6
  2.5 1.0 copy-start.7
  3.9 0.9 copy-start
  6.0 9.6 %copy-start.10 = (s32[4]{0:T(128)S(1)}, s32[4]{0:T(128)}, u32[]{:S(2)}) copy-start(s32[4]{0:T(128)} %param.10) | copy-start | bytes 52
  6.0 29.5 %all-to-all-start = ((f32[32,74,128]{2,1,0:T(8,128)}), f32[32,74,128]{2,1,0:T(8,128)}, u32[]{:S(2)}, u32[]{:S(2)}) async-start(f32[32,74,128]{2,1,0:T(8,128)} %all_to_all.28), calls=%async_computation | async-start | bytes 2621440 | tf_op jit(solution)/shard_map/all_to_all | solution.py:357
  45.0 4.8 %copy-start.9 = (bf16[20,4,4,2,1440]{4,3,2,1,0:T(2,128)(2,1)S(1)}, bf16[20,4,4,2,1440]{4,3,2,1,0:T(2,128)(2,1)}, u32[]{:S(2)}) copy-start(bf16[20,4,4,2,1440]{4,3,2,1,0:T(2,128)(2,1)} %param.9) | copy-start | bytes 5529604
  45.0 21.8 %all-to-all-start.1 = ((f32[32,58,128]{2,1,0:T(8,128)}), f32[32,58,128]{2,1,0:T(8,128)}, u32[]{:S(2)}, u32[]{:S(2)}) async-start(f32[32,58,128]{2,1,0:T(8,128)} %all_to_all.31), calls=%async_computation.1 | async-start | bytes 2097152 | tf_op jit(solution)/shard_map/all_to_all | solution.py:357
  52.3 1.8 %copy-start.4 = (s32[1,32,4,1024]{3,2,1,0:T(4,128)S(1)}, s32[1,32,4,1024]{3,2,1,0:T(4,128)}, u32[]{:S(2)}) copy-start(s32[1,32,4,1024]{3,2,1,0:T(4,128)} %param.11) | copy-start | bytes 1572868
  52.3 1.8 %copy-start.5 = (f32[1,32,4,1024]{3,2,1,0:T(4,128)S(1)}, f32[1,32,4,1024]{3,2,1,0:T(4,128)}, u32[]{:S(2)}) copy-start(f32[1,32,4,1024]{3,2,1,0:T(4,128)} %param.12) | copy-start | bytes 1572868
  57.1 12.0 %copy-start.8 = (s32[1,32]{1,0:T(1,128)S(1)}, s32[1,32]{1,0:T(1,128)}, u32[]{:S(2)}) copy-start(s32[1,32]{1,0:T(1,128)} %param.13) | copy-start | bytes 388
  69.1 1.2 copy-start.2
  85.8 5.9 %collective-permute-start = (f32[256,128]{1,0:T(8,128)S(1)}, f32[256,128]{1,0:T(8,128)S(1)}, u32[]{:S(2)}, u32[]{:S(2)}) collective-permute-start(f32[256,128]{1,0:T(8,128)S(1)} %observe.1.refs_1_), channel_id=1, source_target_pairs={{0,32},{32,64},{64,96},{96,0},{1,33},{33,65},{65,97},{97,1},{2,34}... | collective-permute-start | bytes 393224 | tf_op jit(solution)/shard_map/ppermute | solution.py:415
  87.2 5.2 %collective-permute-start.1 = (f32[256,128]{1,0:T(8,128)S(1)}, f32[256,128]{1,0:T(8,128)S(1)}, u32[]{:S(2)}, u32[]{:S(2)}) collective-permute-start(f32[256,128]{1,0:T(8,128)S(1)} %observe.1.refs_1_), channel_id=1, source_target_pairs={{0,96},{32,0},{64,32},{96,64},{1,97},{33,1},{65,33},{97,65},{2,98}... | collective-permute-start | bytes 393224 | tf_op jit(solution)/shard_map/ppermute | solution.py:415
  88.7 7.1 %collective-permute-start.2 = (f32[256,128]{1,0:T(8,128)S(1)}, f32[256,128]{1,0:T(8,128)S(1)}, u32[]{:S(2)}, u32[]{:S(2)}) collective-permute-start(f32[256,128]{1,0:T(8,128)S(1)} %observe.1.refs_1_), channel_id=1, source_target_pairs={{0,64},{32,96},{64,0},{96,32},{1,65},{33,97},{65,1},{97,33},{2,66}... | collective-permute-start | bytes 393224 | tf_op jit(solution)/shard_map/ppermute | solution.py:415
  112.3 1.0 copy-start.3
  143.0 21.4 %all-to-all-start.3 = ((f32[32,58,128]{2,1,0:T(8,128)}), f32[32,58,128]{2,1,0:T(8,128)}, u32[]{:S(2)}, u32[]{:S(2)}) async-start(f32[32,58,128]{2,1,0:T(8,128)} %all_to_all.37), calls=%async_computation.3 | async-start | bytes 2097152 | tf_op jit(solution)/shard_map/all_to_all | solution.py:357
  147.5 18.3 %copy-start.1 = (f32[160,1536]{1,0:T(8,128)S(1)}, f32[160,1536]{1,0:T(8,128)}, u32[]{:S(2)}) copy-start(f32[160,1536]{1,0:T(8,128)} %copy-done) | copy-start | bytes 2949124

commit v2 on v1

--- a/solution.py
+++ b/solution.py
@@ -21,15 +21,15 @@
 LINE = -(-PIECES * PIECE // LANES)
 COLS = -(-LON // LANES)
 OBS_ROWS = SLOT // LANES
-LINE_OBS = LINE + OBS_ROWS
+EARLY = OBS_ROWS - 1
+THERE, BACK = LINE + EARLY, 32
 
 CHUNK = 90
 CHUNKS = LON // CHUNK
 HI = CH * CHUNKS
 LO = 96
 BLOCK = 256
-PER_SRC = SLOT // BLOCK
-BLOCKS = TILES * PER_SRC
+BLOCKS = TILES * OBS_ROWS
 
 F32, BF16, I32 = jnp.float32, jnp.bfloat16, jnp.int32
 VMEM = pl.BlockSpec(memory_space=pltpu.VMEM)
@@ -94,7 +94,7 @@
         return (half, at // LANES, at % LANES)
 
     def fetch(half, j):
-        return got_ref[pl.ds((half * MGRP * 8 + mgrp * 8) * LINE + j, 8, stride=LINE), :]
+        return got_ref[pl.ds((half * MGRP * 8 + mgrp * 8) * BACK + j, 8, stride=BACK), :]
 
     return assemble(fetch, where_from, cache)
 
@@ -104,69 +104,69 @@
         return alpha_ref[member * 8 : member * 8 + 8, t * LANES : (t + 1) * LANES]
 
     def store(row, tile):
-        out_ref[pl.ds(row, 8, stride=LINE_OBS), :] = tile
-
-    pack_rows(fetch, store, LINE_OBS)
+        out_ref[pl.ds(row, 8, stride=THERE), :] = tile
+
+    pack_rows(fetch, store, THERE)
     for d in range(TILES):
         for r, ref in enumerate((value_ref, var_ref)):
-            at = (d * 2 + r) * LINE_OBS + LINE
-            out_ref[at : at + OBS_ROWS, :] = ref[d * OBS_ROWS : (d + 1) * OBS_ROWS, :]
+            at = (d * 2 + r) * THERE + LINE
+            out_ref[at : at + EARLY, :] = ref[d * OBS_ROWS : d * OBS_ROWS + EARLY, :]
 
 
 def diffuse_body(steps_ref, in_ref, out_ref, buf, line):
     lat8 = LAT // 8
-    for a in range(lat8):
-        for j in range(LINE):
-            buf[0, a, :, j * LANES : (j + 1) * LANES] = in_ref[pl.ds(a * line + j, 8, stride=8 * line), :]
+    for j in range(LINE):
+        for a in range(lat8):
+            buf[0, j, a] = in_ref[pl.ds(a * line + j, 8, stride=8 * line), :]
     sub = lax.broadcasted_iota(I32, (8, LANES), 0)
     lane = lanes8()
 
     def step(k, carry):
         now, later = lax.rem(k, 2), lax.rem(k + 1, 2)
-        old_right, cur = None, None
-        for a in range(lat8):
-            right = {}
-            left = {}
-
-            def tile(aa, j):
-                return buf[now, aa, :, j * LANES : (j + 1) * LANES]
-
-            x = [tile(a, j) for j in range(LINE)]
-            right = [pltpu.roll(v, 1, 1) for v in x]
-            left = [pltpu.roll(v, LANES - 1, 1) for v in x]
-            for j in range(LINE):
-                west = jnp.where(lane == 0, right[j - 1], right[j])
-                east = jnp.where(lane == LANES - 1, left[(j + 1) % LINE], left[j])
-                if a == 0:
-                    north = jnp.where(sub == 0, 0.0, pltpu.roll(tile(lat8 - 1, j), 1, 0))
-                else:
-                    north = tile(a - 1, j)
-                if a == lat8 - 1:
-                    south = jnp.where(sub == 7, 0.0, pltpu.roll(tile(0, j), 7, 0))
-                else:
-                    south = tile(a + 1, j)
-                laplace = ((north + south) + (west + east)) - 4.0 * x[j]
-                buf[later, a, :, j * LANES : (j + 1) * LANES] = x[j] + 0.2 * laplace
+
+        def column(j):
+            return [buf[now, j % LINE, a] for a in range(lat8)]
+
+        def turn(column, by):
+            return [pltpu.roll(v, by, 1) for v in column]
+
+        before = turn(column(LINE - 1), 1)
+        x = column(0)
+        left = turn(x, LANES - 1)
+        for j in range(LINE):
+            ahead = column(j + 1)
+            right = turn(x, 1)
+            after = turn(ahead, LANES - 1)
+            for a in range(lat8):
+                west = jnp.where(lane == 0, before[a], right[a])
+                east = jnp.where(lane == LANES - 1, after[a], left[a])
+                north = x[a - 1] if a else jnp.where(sub == 0, 0.0, pltpu.roll(x[lat8 - 1], 1, 0))
+                south = x[a + 1] if a < lat8 - 1 else jnp.where(sub == 7, 0.0, pltpu.roll(x[0], 7, 0))
+                buf[later, j, a] = 0.2 * ((north + south) + (west + east)) + (1.0 - 4.0 * 0.2) * x[a]
+            before, x, left = right, ahead, after
         return carry
 
     count = steps_ref[0]
     lax.fori_loop(0, count, step, 0)
     end = lax.rem(count, 2)
-    for a in range(lat8):
-        for j in range(LINE):
-            out_ref[pl.ds(a * LINE + j, 8, stride=8 * LINE), :] = buf[end, a, :, j * LANES : (j + 1) * LANES]
-
-
-def diffuse_first_kernel(steps_ref, in_ref, out_ref, value_ref, var_ref, buf):
-    diffuse_body(steps_ref, in_ref, out_ref, buf, LINE_OBS)
-    for t in range(TILES):
-        for r, ref in enumerate((value_ref, var_ref)):
-            at = (t * 2 + r) * LINE_OBS + LINE
-            ref[t * OBS_ROWS : (t + 1) * OBS_ROWS, :] = in_ref[at : at + OBS_ROWS, :]
+    for j in range(LINE):
+        for a in range(lat8):
+            out_ref[pl.ds(a * BACK + j, 8, stride=8 * BACK), :] = buf[end, j, a]
+
+
+def diffuse_first_kernel(steps_ref, in_ref, own_value_ref, own_var_ref, out_ref, value_ref, var_ref, buf):
+    diffuse_body(steps_ref, in_ref, out_ref, buf, THERE)
+    for r, (own_ref, ref) in enumerate(((own_value_ref, value_ref), (own_var_ref, var_ref))):
+        for t in range(TILES):
+            at = (t * 2 + r) * THERE + LINE
+            ref[t * OBS_ROWS : t * OBS_ROWS + EARLY, :] = in_ref[at : at + EARLY, :]
+        for t in range(0, TILES, 8):
+            late = own_ref[pl.ds(t * OBS_ROWS + EARLY, 8, stride=OBS_ROWS), :]
+            out_ref[pl.ds((t * 2 + r) * BACK + LINE, 8, stride=2 * BACK), :] = late
 
 
 def diffuse_kernel(steps_ref, in_ref, out_ref, buf):
-    diffuse_body(steps_ref, in_ref, out_ref, buf, LINE)
+    diffuse_body(steps_ref, in_ref, out_ref, buf, BACK)
 
 
 def slots_kernel(index_ref, weight_ref, out_ref):
@@ -187,28 +187,44 @@
             for column in (first, jnp.logical_not(first)):
                 rows.append(jnp.sum(jnp.where(row & column, weight, 0.0), 0, keepdims=True))
         for k, row in enumerate(rows):
-            out_ref[s, k : k + 1, :] = row
+            for j in range(OBS_ROWS):
+                out_ref[s * OBS_ROWS + j, k : k + 1, :] = row[:, j * LANES : (j + 1) * LANES]
         return carry
 
     lax.fori_loop(0, TILES, body, 0)
 
 
-def live_blocks(count_ref, list_ref, pad):
+def live_blocks(count_ref, list_ref):
     def body(s, n):
-        for j in range(PER_SRC):
-            list_ref[n + j] = s * PER_SRC + j
-        return n + lax.div(count_ref[s] + (BLOCK - 1), BLOCK)
+        for j in range(OBS_ROWS):
+            list_ref[n + j] = s * OBS_ROWS + j
+        return n + lax.div(count_ref[s] + (LANES - 1), LANES)
 
     n = lax.fori_loop(0, TILES, body, 0)
-    for j in range(pad):
+    for j in range(2 * FEW):
         list_ref[n + j] = 0
     return n
 
 
-def slot_rows(slot_ref, b):
-    s = lax.div(b, PER_SRC)
-    at = pl.multiple_of(lax.rem(b, PER_SRC) * BLOCK, BLOCK)
-    return [slot_ref[s, k : k + 1, pl.ds(at, BLOCK)] for k in range(6)]
+def over_live(n, body):
+    many = lax.div(n, 2 * MANY)
+    done = many * (2 * MANY)
+
+    def large(i, carry):
+        body(i * (2 * MANY), MANY)
+        return carry
+
+    def small(i, carry):
+        body(done + i * (2 * FEW), FEW)
+        return carry
+
+    lax.fori_loop(0, many, large, 0)
+    lax.fori_loop(0, lax.div(n - done + (2 * FEW - 1), 2 * FEW), small, 0)
+
+
+def slot_rows(slot_ref, pair):
+    blocks = [slot_ref[b] for b in pair]
+    return [jnp.concatenate([x[k : k + 1] for x in blocks], 1) for k in range(6)]
 
 
 def one_hot(high):
@@ -221,7 +237,7 @@
     return high, (x - high.astype(F32)).astype(BF16)
 
 
-UNROLL = 2
+MANY, FEW = 8, 2
 
 
 def observe_kernel(scale, count_ref, got_ref, ens_ref, slot_ref, out_ref, inc_ref, table_ref, list_ref):
@@ -253,59 +269,60 @@
     left = jnp.concatenate([parts[0][0], parts[1][0], parts[0][1], parts[1][1]], 0)
 
     out_ref[...] = jnp.zeros_like(out_ref)
-    n = live_blocks(count_ref, list_ref, UNROLL)
+    n = live_blocks(count_ref, list_ref)
     columns = lax.broadcasted_iota(I32, (LO, BLOCK), 0).astype(F32)
 
-    def body(i, carry):
-        for u in range(UNROLL):
-            b = list_ref[i * UNROLL + u]
-            high, low, w00, w01, w10, w11 = slot_rows(slot_ref, b)
+    def body(start, pairs):
+        for u in range(pairs):
+            pair = [list_ref[start + 2 * u + h] for h in range(2)]
+            high, low, w00, w01, w10, w11 = slot_rows(slot_ref, pair)
             picked = jnp.dot(left, one_hot(high), preferred_element_type=F32)
             both = picked[: 2 * LO] + picked[2 * LO :]
             here, after = columns == low, columns == low + 1.0
             value = jnp.where(here, w00, jnp.where(after, w01, 0.0)) * both[:LO]
             value += jnp.where(here, w10, jnp.where(after, w11, 0.0)) * both[LO:]
             value = jnp.sum(value, 0, keepdims=True)
-            for h in range(BLOCK // LANES):
-                out_ref[pl.ds(b * (BLOCK // LANES) + h, 1), :] = value[:, h * LANES : (h + 1) * LANES]
-        return carry
-
-    lax.fori_loop(0, lax.div(n + UNROLL - 1, UNROLL), body, 0)
-
-
-def adjoint_kernel(scale, count_ref, m0, m1, m2, m3, value_ref, var_ref, slot_ref, ens_ref, out_ref, dep_ref, acc_ref,
-                   table_ref, adj_ref, proj_ref, list_ref):
+            for h in range(2):
+                out_ref[pl.ds(pair[h], 1), :] = value[:, h * LANES : (h + 1) * LANES]
+
+    over_live(n, body)
+
+
+def adjoint_kernel(scale, count_ref, m0, m1, m2, m3, value_ref, var_ref, late_ref, slot_ref, ens_ref, out_ref, dep_ref,
+                   acc_ref, table_ref, adj_ref, proj_ref, list_ref):
     slot_at = lax.broadcasted_iota(I32, (OBS_ROWS, LANES), 0) * LANES + lax.broadcasted_iota(I32, (OBS_ROWS, LANES), 1)
+    last = slot_at >= EARLY * LANES
     for s in range(TILES):
         at = slice(s * OBS_ROWS, (s + 1) * OBS_ROWS)
         model = (m0[at, :] + m1[at, :]) + (m2[at, :] + m3[at, :])
-        weighted = var_ref[at, :] * (value_ref[at, :] - model)
+        late = [late_ref[(s * 2 + r) * BACK + LINE : (s * 2 + r) * BACK + LINE + 1, :] for r in range(2)]
+        value, var = (jnp.where(last, x, ref[at, :]) for x, ref in zip(late, (value_ref, var_ref)))
+        weighted = var * (value - model)
         dep_ref[at, :] = jnp.where(slot_at < count_ref[s], weighted, 0.0)
     acc_ref[...] = jnp.zeros_like(acc_ref)
-    n = live_blocks(count_ref, list_ref, UNROLL)
+    n = live_blocks(count_ref, list_ref)
     columns = lax.broadcasted_iota(I32, (LO, BLOCK), 0).astype(F32).astype(BF16)
 
-    def body(i, carry):
-        total = acc_ref[...]
-        for u in range(UNROLL):
-            at = i * UNROLL + u
-            b = list_ref[at]
-            live = (at < n).astype(F32)
-            high, low, w00, w01, w10, w11 = slot_rows(slot_ref, b)
-            per = BLOCK // LANES
-            dep = jnp.concatenate([dep_ref[pl.ds(b * per + h, 1), :] for h in range(per)], 1) * live
+    def body(start, pairs):
+        spreads, hots = [], []
+        for u in range(pairs):
+            at = [start + 2 * u + h for h in range(2)]
+            pair = [list_ref[k] for k in at]
+            high, low, w00, w01, w10, w11 = slot_rows(slot_ref, pair)
+            dep = [jnp.where(k < n, dep_ref[pl.ds(b, 1), :], 0.0) for k, b in zip(at, pair)]
+            dep = jnp.concatenate(dep, 1)
             here, after = columns == low.astype(BF16), columns == (low + 1.0).astype(BF16)
             halves = []
             for first, second in ((w00, w01), (w10, w11)):
                 first, second = split(first * dep), split(second * dep)
                 zero = jnp.zeros((), BF16)
                 halves.append([jnp.where(here, x, jnp.where(after, y, zero)) for x, y in zip(first, second)])
-            spread = jnp.concatenate([halves[0][0], halves[1][0], halves[0][1], halves[1][1]], 0)
-            total += lax.dot_general(spread, one_hot(high), (((1,), (1,)), ((), ())), preferred_element_type=F32)
-        acc_ref[...] = total
-        return carry
-
-    lax.fori_loop(0, lax.div(n + UNROLL - 1, UNROLL), body, 0)
+            spreads.append(jnp.concatenate([halves[0][0], halves[1][0], halves[0][1], halves[1][1]], 0))
+            hots.append(one_hot(high))
+        spread, hot = jnp.concatenate(spreads, 1), jnp.concatenate(hots, 1)
+        acc_ref[...] += lax.dot_general(spread, hot, (((1,), (1,)), ((), ())), preferred_element_type=F32)
+
+    over_live(n, body)
     both = acc_ref[: 2 * LO, :] + acc_ref[2 * LO :, :]
     for r in range(ROWS):
         part = jnp.concatenate([both[r * LO : (r + 1) * LO], jnp.zeros((LANES - LO, HI), F32)], 0)
@@ -334,9 +351,9 @@
             proj_ref[t, m * 8 : m * 8 + 8, :] = total
 
     def store(row, tile):
-        out_ref[pl.ds(row, 8, stride=LINE), :] = tile
-
-    pack_rows(lambda m, t: proj_ref[t, m * 8 : m * 8 + 8, :], store, LINE)
+        out_ref[pl.ds(row, 8, stride=BACK), :] = tile
+
+    pack_rows(lambda m, t: proj_ref[t, m * 8 : m * 8 + 8, :], store, BACK)
 
 
 def gradient_kernel(alpha_ref, got_ref, out_ref):
@@ -372,7 +389,7 @@
 
     sent = pl.pallas_call(
         pack_kernel,
-        out_shape=shape(LAT * LINE_OBS, LANES),
+        out_shape=shape(LAT * THERE, LANES),
         in_specs=[VMEM] * 3,
         out_specs=VMEM,
         compiler_params=params(16),
@@ -382,7 +399,7 @@
 
     slots = pl.pallas_call(
         slots_kernel,
-        out_shape=shape(TILES, 8, SLOT),
+        out_shape=shape(BLOCKS, 8, LANES),
         in_specs=[VMEM] * 2,
         out_specs=VMEM,
         compiler_params=params(16),
@@ -390,16 +407,16 @@
         name="slots",
     )(obs_index[0], obs_weight[0])
 
-    buf = pltpu.VMEM((2, 8, 8, LINE * LANES), F32)
+    buf = pltpu.VMEM((2, LINE, 8, 8, LANES), F32)
     moved, value, var = pl.pallas_call(
         diffuse_first_kernel,
-        out_shape=(shape(LAT * LINE, LANES), flat, flat),
-        in_specs=[SMEM, VMEM],
+        out_shape=(shape(LAT * BACK, LANES), flat, flat),
+        in_specs=[SMEM] + [VMEM] * 3,
         out_specs=[VMEM] * 3,
         scratch_shapes=[buf],
         compiler_params=params(16),
         name="diffuse_first",
-    )(steps, got)
+    )(steps, got, value, var)
     got = exchange(moved)
 
     block_list = pltpu.SMEM((BLOCKS + 8,), I32)
@@ -416,8 +433,8 @@
 
     sent, departure = pl.pallas_call(
         lambda *refs: adjoint_kernel(scale, *refs),
-        out_shape=(shape(LAT * LINE, LANES), flat),
-        in_specs=[SMEM] + [VMEM] * 8,
+        out_shape=(shape(LAT * BACK, LANES), flat),
+        in_specs=[SMEM] + [VMEM] * 9,
         out_specs=[VMEM] * 2,
         scratch_shapes=[
             pltpu.VMEM((4 * LO, HI), F32),
@@ -426,14 +443,14 @@
             pltpu.VMEM((COLS, GROUP * 8, LANES), F32),
             block_list,
         ],
-        compiler_params=params(20),
+        compiler_params=params(24),
         name="adjoint",
-    )(counts, mine, *others, value, var, slots, ens)
+    )(counts, mine, *others, value, var, got, slots, ens)
     got = exchange(sent)
 
     moved = pl.pallas_call(
         diffuse_kernel,
-        out_shape=shape(LAT * LINE, LANES),
+        out_shape=shape(LAT * BACK, LANES),
         in_specs=[SMEM, VMEM],
         out_specs=VMEM,
         scratch_shapes=[buf],

time: 167 us -> 144 us (0.86)
  Pallas kernels: 50 us -> 31.9 us
  local copies, waits for them, and re-layouts: 22.5 us -> 15 us
  starting transfers between devices: 23.3 us -> 29 us
  waiting for transfers between devices: 50.8 us -> 46.6 us
    all_to_all x8 -> x0, local copies, waits for them, and re-layouts: 9.5 us -> none  [exchange(): return lax.all_to_all(x, 'tile', 0, 0, tiled=True)]
    pallas_call x1, Pallas kernels: 16.6 us -> 9.07 us  [shards(): pl.pallas_call(lambda *refs: adjoint_kernel(scale, *refs), out_shape=(sha...]
    pallas_call x1, Pallas kernels: 15.5 us -> 9.49 us  [shards(): pl.pallas_call(lambda *refs: observe_kernel(scale, *refs), out_shape=flat...]
    all_to_all x3, starting transfers between devices: 18.8 us -> 24.5 us  [exchange(): return lax.all_to_all(x, 'tile', 0, 0, tiled=True)]
    all_to_all x3, waiting for transfers between devices: 45.3 us -> 40.3 us  [exchange(): return lax.all_to_all(x, 'tile', 0, 0, tiled=True)]
    pallas_call x4, Pallas kernels: 17.6 us -> 12.7 us  [the longest x1 4.42 us: shards(): pl.pallas_call(diffuse_kernel, out_shape=shape(LAT * BACK, LANES), in_spe...]
    reshape x1, local copies, waits for them, and re-layouts: 2.48 us -> 5.24 us  [shards(): ens = jnp.pad(ensemble.reshape(GROUP, 2, 16, LON), ((0, 0), (0, 0)) + wide)]
  transfers between devices with their start and end apart: 6 -> 6, of which waited for: 6 -> 5; matrix products, arithmetic and copies ran while one was open for 3% -> 6% of each run, Pallas kernels for 2% -> 2%
where the time goes in v2:
time: 144 us; the launch traced here: 143 us
  waiting for transfers between devices  46.6 us (32%)
  Pallas kernels  31.9 us (22%)
  starting transfers between devices  29 us (20%)
  blocking collectives  19.9 us (14%)
  local copies, waits for them, and re-layouts  15 us (10%)
    all_to_all x3, waiting for transfers between devices, exchange(): return lax.all_to_all(x, 'tile', 0, 0, tiled=True)  40.3 us
    all_to_all x3, starting transfers between devices, exchange(): return lax.all_to_all(x, 'tile', 0, 0, tiled=True)  24.5 us
    all_to_all x1, blocking collectives, exchange(): return lax.all_to_all(x, 'tile', 0, 0, tiled=True)  19.9 us
    pallas_call x1, Pallas kernels, shards(): pl.pallas_call(lambda *refs: observe_kernel(scale, *refs), out_shape=flat...  9.49 us
    pallas_call x1, Pallas kernels, shards(): pl.pallas_call(lambda *refs: adjoint_kernel(scale, *refs), out_shape=(sha...  9.07 us
    ppermute x3, waiting for transfers between devices, shards(): lax.ppermute(mine, 'member', [(i, (i + k) % 4) for i in range(4)])  6.29 us
    reshape x1, local copies, waits for them, and re-layouts, shards(): ens = jnp.pad(ensemble.reshape(GROUP, 2, 16, LON), ((0, 0), (0, 0)) + wide)  5.24 us
    ppermute x3, starting transfers between devices, shards(): lax.ppermute(mine, 'member', [(i, (i + k) % 4) for i in range(4)])  4.45 us
  transfers between devices with their start and end apart: 6, of which 5 were waited for; matrix products, arithmetic and copies ran while one was open for 6% of the time, Pallas kernels for 2%

profile of v2, /device:TPU:1, one launch (start us, length us, event | category | flops | bytes accessed | tf_op | source)
XLA Modules:
  0.0 143.3 jit_solution(16859381746381464259)
XLA Ops:
  0.6 0.0 copy-start.7
  0.6 0.0 copy-start.8
  0.6 1.9 %reshape.30 = f32[160,1440]{1,0:T(8,128)S(1)} reshape(f32[20,4,2,1440]{3,2,1,0:T(2,128)} %param.8) | data formatting | bytes 1843200 | tf_op jit(solution)/shard_map/reshape | solution.py:384
  2.6 0.1 pad.8.alpha_ref
  2.6 0.0 copy-done.7
  2.7 0.0 copy-done.8
  2.7 0.0 copy-start.10
  2.7 1.4 pack.1
  4.1 0.0 copy-start.3
  4.1 0.9 copy-done.3
  5.1 9.4 %all-to-all-start = ((f32[32,72,128]{2,1,0:T(8,128)}), f32[32,72,128]{2,1,0:T(8,128)S(1)}, u32[]{:S(2)}, u32[]{:S(2)}) async-start(f32[32,72,128]{2,1,0:T(8,128)} %bitcast.3), calls=%async_computation | async-start | bytes 2359296 | tf_op jit(solution)/shard_map/all_to_all | solution.py:374
  14.5 0.0 copy-done.10
  14.5 0.6 dynamic_slice.3.steps_ref
  15.1 17.8 %all-to-all-done = f32[32,72,128]{2,1,0:T(8,128)S(1)} async-done(((f32[32,72,128]{2,1,0:T(8,128)}), f32[32,72,128]{2,1,0:T(8,128)S(1)}, u32[]{:S(2)}, u32[]{:S(2)}) %all-to-all-start) | async-done | bytes 1179680 | tf_op jit(solution)/shard_map/all_to_all | solution.py:374
  32.8 4.4 %diffuse_first.1 = (f32[2048,128]{1,0:T(8,128)}, f32[256,128]{1,0:T(8,128)S(1)}, f32[256,128]{1,0:T(8,128)S(1)}) custom-call(s32[1]{0:T(128)} %dynamic_slice.3.steps_ref, f32[2304,128]{1,0:T(8,128)S(1)} %bitcast.15, f32[256,128]{1,0:T(8,128)S(1)} %bitcast.22, f32[256,128]{1,0:T(8,128)S(1)} %bitcast.24), custom_call_target="tpu_custom_call" | custom-call | tf_op jit(solution)/shard_map/diffuse_first/pallas_call | solution.py:411
  37.2 7.5 %all-to-all-start.1 = ((f32[32,64,128]{2,1,0:T(8,128)}), f32[32,64,128]{2,1,0:T(8,128)S(1)}, u32[]{:S(2)}, u32[]{:S(2)}) async-start(f32[32,64,128]{2,1,0:T(8,128)} %bitcast.5), calls=%async_computation.1 | async-start | bytes 2097152 | tf_op jit(solution)/shard_map/all_to_all | solution.py:374
  44.8 5.2 %reshape.33 = bf16[20,2,16,1440]{3,2,1,0:T(8,128)(2,1)} reshape(bf16[20,4,4,2,1440]{4,3,2,1,0:T(2,128)(2,1)} %param.9) | data formatting | bytes 3686400 | tf_op jit(solution)/shard_map/reshape | solution.py:385
  50.0 0.0 copy-start.5
  50.0 0.0 copy-start.6
  50.0 1.8 %pad.9.refs_2_.refs_9_ = bf16[20,2,16,1536]{3,2,1,0:T(8,128)(2,1)S(1)} pad(bf16[20,2,16,1440]{3,2,1,0:T(8,128)(2,1)} %reshape.33, bf16[]{:T(256)} %constant.14.clone.1), padding=0_0x0_0x0_0x0_96 | pad | bytes 3809282 | tf_op jit(solution)/shard_map/jit(_pad)/pad | solution.py:385
  51.8 0.0 copy-start.9
  51.9 0.0 copy-done.5
  51.9 0.0 copy-done.6
  51.9 2.5 %slots.1.refs_3_.refs_8_ = f32[256,8,128]{2,1,0:T(8,128)S(1)} custom-call(s32[32,4,1024]{2,1,0:T(4,128)S(1)} %bitcast.19, f32[32,4,1024]{2,1,0:T(4,128)S(1)} %bitcast.20), custom_call_target="tpu_custom_call" | custom-call | flops 8000000 | bytes 2097152 | tf_op jit(solution)/shard_map/slots/pallas_call | solution.py:400
  54.3 0.0 copy-start
  54.4 1.0 copy-done
  55.3 6.4 %all-to-all-done.1 = f32[32,64,128]{2,1,0:T(8,128)S(1)} async-done(((f32[32,64,128]{2,1,0:T(8,128)}), f32[32,64,128]{2,1,0:T(8,128)S(1)}, u32[]{:S(2)}, u32[]{:S(2)}) %all-to-all-start.1) | async-done | bytes 1048608 | tf_op jit(solution)/shard_map/all_to_all | solution.py:374
  61.7 0.0 copy-done.9
  61.7 0.0 copy-start.1
  61.7 1.2 copy-done.1
  62.9 0.0 copy-start.2
  62.9 9.5 %observe.1.refs_1_ = f32[256,128]{1,0:T(8,128)S(1)} custom-call(s32[32]{0:T(128)S(1)} %bitcast.25, f32[2048,128]{1,0:T(8,128)S(1)} %bitcast.13, bf16[20,2,16,1536]{3,2,1,0:T(8,128)(2,1)S(1)} %pad.9.refs_2_.refs_9_, f32[256,8,128]{2,1,0:T(8,128)S(1)} %copy-done.1), custom_call_target="tpu_custom_call" | custom-call | tf_op jit(solution)/shard_map/observe/pallas_call | solution.py:423
  72.4 1.4 collective-permute-start
  73.8 1.5 %collective-permute-start.1 = (f32[256,128]{1,0:T(8,128)S(1)}, f32[256,128]{1,0:T(8,128)S(1)}, u32[]{:S(2)}, u32[]{:S(2)}) collective-permute-start(f32[256,128]{1,0:T(8,128)S(1)} %observe.1.refs_1_), channel_id=1, source_target_pairs={{0,96},{32,0},{64,32},{96,64},{1,97},{33,1},{65,33},{97,65},{2,98}... | collective-permute-start | bytes 393224 | tf_op jit(solution)/shard_map/ppermute | solution.py:432
  75.3 1.6 %collective-permute-start.2 = (f32[256,128]{1,0:T(8,128)S(1)}, f32[256,128]{1,0:T(8,128)S(1)}, u32[]{:S(2)}, u32[]{:S(2)}) collective-permute-start(f32[256,128]{1,0:T(8,128)S(1)} %observe.1.refs_1_), channel_id=1, source_target_pairs={{0,64},{32,96},{64,0},{96,32},{1,65},{33,97},{65,1},{97,33},{2,66}... | collective-permute-start | bytes 393224 | tf_op jit(solution)/shard_map/ppermute | solution.py:432
  76.9 2.2 %collective-permute-done.refs_2_ = f32[256,128]{1,0:T(8,128)S(1)} collective-permute-done((f32[256,128]{1,0:T(8,128)S(1)}, f32[256,128]{1,0:T(8,128)S(1)}, u32[]{:S(2)}, u32[]{:S(2)}) %collective-permute-start) | collective-permute-done | bytes 131104 | tf_op jit(solution)/shard_map/ppermute | solution.py:432
  79.0 0.0 collective-permute-done.1.refs_3_
  79.1 4.1 %collective-permute-done.2.refs_4_ = f32[256,128]{1,0:T(8,128)S(1)} collective-permute-done((f32[256,128]{1,0:T(8,128)S(1)}, f32[256,128]{1,0:T(8,128)S(1)}, u32[]{:S(2)}, u32[]{:S(2)}) %collective-permute-start.2) | collective-permute-done | bytes 131104 | tf_op jit(solution)/shard_map/ppermute | solution.py:432
  83.2 0.0 copy-done.2
  83.2 9.1 %adjoint.1 = (f32[2048,128]{1,0:T(8,128)S(1)}, f32[256,128]{1,0:T(8,128)S(1)}) custom-call(s32[32]{0:T(128)S(1)} %bitcast.26, f32[256,128]{1,0:T(8,128)S(1)} %observe.1.refs_1_, f32[256,128]{1,0:T(8,128)S(1)} %collective-permute-done.refs_2_, f32[256,128]{1,0:T(8,128)S(1)} %collective-permute-done.1.refs_3_, f32[256,128]{1,0:T(8,128)S(1)} %collective-permute-done.2.refs_4_, ...), custom_call_target="tpu_custom_call" | custom-call | tf_op jit(solution)/shard_map/adjoint/pallas_call | solution.py:434
  92.2 19.9 %all_to_all.44 = f32[32,64,128]{2,1,0:T(8,128)S(1)} all-to-all(f32[32,64,128]{2,1,0:T(8,128)S(1)} %bitcast.18), channel_id=1, replica_groups=mesh['member'=4,'tile'=32] {'tile'}, dimensions={0} | all-to-all | bytes 2097152 | tf_op jit(solution)/shard_map/all_to_all | solution.py:374
  112.1 0.0 copy-start.4
  112.1 4.4 %diffuse.1 = f32[2048,128]{1,0:T(8,128)} custom-call(s32[1]{0:T(128)} %dynamic_slice.3.steps_ref, f32[2048,128]{1,0:T(8,128)S(1)} %bitcast.17), custom_call_target="tpu_custom_call" | custom-call | tf_op jit(solution)/shard_map/diffuse/pallas_call | solution.py:451
  116.6 7.6 %all-to-all-start.3 = ((f32[32,64,128]{2,1,0:T(8,128)}), f32[32,64,128]{2,1,0:T(8,128)S(1)}, u32[]{:S(2)}, u32[]{:S(2)}) async-start(f32[32,64,128]{2,1,0:T(8,128)} %bitcast.11), calls=%async_computation.3 | async-start | bytes 2097152 | tf_op jit(solution)/shard_map/all_to_all | solution.py:374
  124.1 0.7 reshape.35
  124.8 16.2 %all-to-all-done.3 = f32[32,64,128]{2,1,0:T(8,128)S(1)} async-done(((f32[32,64,128]{2,1,0:T(8,128)}), f32[32,64,128]{2,1,0:T(8,128)S(1)}, u32[]{:S(2)}, u32[]{:S(2)}) %all-to-all-start.3) | async-done | bytes 1048608 | tf_op jit(solution)/shard_map/all_to_all | solution.py:374
  141.0 0.0 copy-done.4
  141.0 0.7 gradient.1
  141.7 1.5 %reshape.34 = f32[20,4,2,1440]{3,2,1,0:T(2,128)} reshape(f32[160,1440]{1,0:T(8,128)S(1)} %gradient.1) | data formatting | bytes 1843200 | tf_op jit(solution)/shard_map/reshape | solution.py:470
Async XLA Ops:
  0.6 2.0 %copy-start.7 = (f32[32,1,1024]{2,1,0:T(1,128)S(1)}, f32[32,1,1024]{2,1,0:T(1,128)}, u32[]{:S(2)}) copy-start(f32[32,1,1024]{2,1,0:T(1,128)} %param.14) | copy-start | bytes 393220
  0.6 2.0 %copy-start.8 = (f32[32,1,1024]{2,1,0:T(1,128)S(1)}, f32[32,1,1024]{2,1,0:T(1,128)}, u32[]{:S(2)}) copy-start(f32[32,1,1024]{2,1,0:T(1,128)} %param.15) | copy-start | bytes 393220
  2.7 11.8 %copy-start.10 = (s32[4]{0:T(128)S(1)}, s32[4]{0:T(128)}, u32[]{:S(2)}) copy-start(s32[4]{0:T(128)} %param.10) | copy-start | bytes 52
  4.1 0.9 copy-start.3
  5.1 27.8 %all-to-all-start = ((f32[32,72,128]{2,1,0:T(8,128)}), f32[32,72,128]{2,1,0:T(8,128)S(1)}, u32[]{:S(2)}, u32[]{:S(2)}) async-start(f32[32,72,128]{2,1,0:T(8,128)} %bitcast.3), calls=%async_computation | async-start | bytes 2359296 | tf_op jit(solution)/shard_map/all_to_all | solution.py:374
  37.2 24.4 %all-to-all-start.1 = ((f32[32,64,128]{2,1,0:T(8,128)}), f32[32,64,128]{2,1,0:T(8,128)S(1)}, u32[]{:S(2)}, u32[]{:S(2)}) async-start(f32[32,64,128]{2,1,0:T(8,128)} %bitcast.5), calls=%async_computation.1 | async-start | bytes 2097152 | tf_op jit(solution)/shard_map/all_to_all | solution.py:374
  50.0 1.8 %copy-start.5 = (s32[1,32,4,1024]{3,2,1,0:T(4,128)S(1)}, s32[1,32,4,1024]{3,2,1,0:T(4,128)}, u32[]{:S(2)}) copy-start(s32[1,32,4,1024]{3,2,1,0:T(4,128)} %param.11) | copy-start | bytes 1572868
  50.0 1.9 %copy-start.6 = (f32[1,32,4,1024]{3,2,1,0:T(4,128)S(1)}, f32[1,32,4,1024]{3,2,1,0:T(4,128)}, u32[]{:S(2)}) copy-start(f32[1,32,4,1024]{3,2,1,0:T(4,128)} %param.12) | copy-start | bytes 1572868
  51.8 9.8 %copy-start.9 = (s32[1,32]{1,0:T(1,128)S(1)}, s32[1,32]{1,0:T(1,128)}, u32[]{:S(2)}) copy-start(s32[1,32]{1,0:T(1,128)} %param.13) | copy-start | bytes 388
  54.3 1.0 copy-start
  61.7 1.2 copy-start.1
  62.9 20.2 %copy-start.2 = (f32[256,8,128]{2,1,0:T(8,128)S(1)}, f32[256,8,128]{2,1,0:T(8,128)}, u32[]{:S(2)}) copy-start(f32[256,8,128]{2,1,0:T(8,128)} %copy-done) | copy-start | bytes 3145732
  72.4 6.6 %collective-permute-start = (f32[256,128]{1,0:T(8,128)S(1)}, f32[256,128]{1,0:T(8,128)S(1)}, u32[]{:S(2)}, u32[]{:S(2)}) collective-permute-start(f32[256,128]{1,0:T(8,128)S(1)} %observe.1.refs_1_), channel_id=1, source_target_pairs={{0,32},{32,64},{64,96},{96,0},{1,33},{33,65},{65,97},{97,1},{2,34}... | collective-permute-start | bytes 393224 | tf_op jit(solution)/shard_map/ppermute | solution.py:432
  73.8 5.3 %collective-permute-start.1 = (f32[256,128]{1,0:T(8,128)S(1)}, f32[256,128]{1,0:T(8,128)S(1)}, u32[]{:S(2)}, u32[]{:S(2)}) collective-permute-start(f32[256,128]{1,0:T(8,128)S(1)} %observe.1.refs_1_), channel_id=1, source_target_pairs={{0,96},{32,0},{64,32},{96,64},{1,97},{33,1},{65,33},{97,65},{2,98}... | collective-permute-start | bytes 393224 | tf_op jit(solution)/shard_map/ppermute | solution.py:432
  75.3 7.9 %collective-permute-start.2 = (f32[256,128]{1,0:T(8,128)S(1)}, f32[256,128]{1,0:T(8,128)S(1)}, u32[]{:S(2)}, u32[]{:S(2)}) collective-permute-start(f32[256,128]{1,0:T(8,128)S(1)} %observe.1.refs_1_), channel_id=1, source_target_pairs={{0,64},{32,96},{64,0},{96,32},{1,65},{33,97},{65,1},{97,33},{2,66}... | collective-permute-start | bytes 393224 | tf_op jit(solution)/shard_map/ppermute | solution.py:432
  112.1 28.9 %copy-start.4 = (f32[160,1536]{1,0:T(8,128)S(1)}, f32[160,1536]{1,0:T(8,128)}, u32[]{:S(2)}) copy-start(f32[160,1536]{1,0:T(8,128)} %copy-done.3) | copy-start | bytes 2949124
  116.6 24.5 %all-to-all-start.3 = ((f32[32,64,128]{2,1,0:T(8,128)}), f32[32,64,128]{2,1,0:T(8,128)S(1)}, u32[]{:S(2)}, u32[]{:S(2)}) async-start(f32[32,64,128]{2,1,0:T(8,128)} %bitcast.11), calls=%async_computation.3 | async-start | bytes 2097152 | tf_op jit(solution)/shard_map/all_to_all | solution.py:374

commit v3 on v2

--- a/solution.py
+++ b/solution.py
@@ -21,8 +21,8 @@
 LINE = -(-PIECES * PIECE // LANES)
 COLS = -(-LON // LANES)
 OBS_ROWS = SLOT // LANES
-EARLY = OBS_ROWS - 1
-THERE, BACK = LINE + EARLY, 32
+THERE, BACK = LINE + OBS_ROWS, LINE
+DEEP, WIDE = 16, 32
 
 CHUNK = 90
 CHUNKS = LON // CHUNK
@@ -110,63 +110,87 @@
     for d in range(TILES):
         for r, ref in enumerate((value_ref, var_ref)):
             at = (d * 2 + r) * THERE + LINE
-            out_ref[at : at + EARLY, :] = ref[d * OBS_ROWS : d * OBS_ROWS + EARLY, :]
-
-
-def diffuse_body(steps_ref, in_ref, out_ref, buf, line):
-    lat8 = LAT // 8
-    for j in range(LINE):
-        for a in range(lat8):
-            buf[0, j, a] = in_ref[pl.ds(a * line + j, 8, stride=8 * line), :]
+            out_ref[at : at + OBS_ROWS, :] = ref[d * OBS_ROWS : (d + 1) * OBS_ROWS, :]
+
+
+def diffuse_step(src, dst):
     sub = lax.broadcasted_iota(I32, (8, LANES), 0)
     lane = lanes8()
 
-    def step(k, carry):
-        now, later = lax.rem(k, 2), lax.rem(k + 1, 2)
-
-        def column(j):
-            return [buf[now, j % LINE, a] for a in range(lat8)]
-
-        def turn(column, by):
-            return [pltpu.roll(v, by, 1) for v in column]
-
-        before = turn(column(LINE - 1), 1)
-        x = column(0)
-        left = turn(x, LANES - 1)
-        for j in range(LINE):
-            ahead = column(j + 1)
-            right = turn(x, 1)
-            after = turn(ahead, LANES - 1)
-            for a in range(lat8):
-                west = jnp.where(lane == 0, before[a], right[a])
-                east = jnp.where(lane == LANES - 1, after[a], left[a])
-                north = x[a - 1] if a else jnp.where(sub == 0, 0.0, pltpu.roll(x[lat8 - 1], 1, 0))
-                south = x[a + 1] if a < lat8 - 1 else jnp.where(sub == 7, 0.0, pltpu.roll(x[0], 7, 0))
-                buf[later, j, a] = 0.2 * ((north + south) + (west + east)) + (1.0 - 4.0 * 0.2) * x[a]
-            before, x, left = right, ahead, after
+    def plane(g):
+        return [src[g, a] for a in range(DEEP)]
+
+    above = [jnp.where(lane < WIDE, 0.0, pltpu.roll(v, WIDE, 1)) for v in plane(DEEP - 1)]
+    here = plane(0)
+    for g in range(DEEP):
+        if g < DEEP - 1:
+            below = plane(g + 1)
+        else:
+            below = [jnp.where(lane >= LANES - WIDE, 0.0, pltpu.roll(v, LANES - WIDE, 1)) for v in plane(0)]
+        west = pltpu.roll(here[-1], 1, 0)
+        west = jnp.where(sub == 0, pltpu.roll(west, 1, 1), west)
+        east = pltpu.roll(here[0], 7, 0)
+        east = jnp.where(sub == 7, pltpu.roll(east, LANES - 1, 1), east)
+        line = [west] + here + [east]
+        for a in range(DEEP):
+            near = (above[a] + below[a]) + (line[a] + line[a + 2])
+            dst[g, a] = 0.2 * near + (1.0 - 4.0 * 0.2) * here[a]
+        above, here = here, below
+
+
+def diffuse_body(steps_ref, in_ref, out_ref, one, two, turned, line):
+    blocks = LANES // WIDE
+    for g in range(DEEP):
+        lines = []
+        for q in range(blocks):
+            at = (DEEP * q + g) * line
+            piece = in_ref[at : at + LINE, :]
+            lines += [piece, jnp.zeros((WIDE - LINE, LANES), F32)]
+        turned[g] = jnp.concatenate(lines, 0).T
+    for g in range(DEEP):
+        for a in range(DEEP):
+            one[g, a] = turned[g, pl.ds(a, 8, stride=DEEP), :]
+    count = steps_ref[0]
+
+    def pair(k, carry):
+        diffuse_step(one, two)
+        diffuse_step(two, one)
         return carry
 
-    count = steps_ref[0]
-    lax.fori_loop(0, count, step, 0)
-    end = lax.rem(count, 2)
-    for j in range(LINE):
-        for a in range(lat8):
-            out_ref[pl.ds(a * BACK + j, 8, stride=8 * BACK), :] = buf[end, j, a]
-
-
-def diffuse_first_kernel(steps_ref, in_ref, own_value_ref, own_var_ref, out_ref, value_ref, var_ref, buf):
-    diffuse_body(steps_ref, in_ref, out_ref, buf, THERE)
-    for r, (own_ref, ref) in enumerate(((own_value_ref, value_ref), (own_var_ref, var_ref))):
-        for t in range(TILES):
+    lax.fori_loop(0, lax.div(count, 2), pair, 0)
+
+    def put(src):
+        for g in range(DEEP):
+            for a in range(DEEP):
+                turned[g, pl.ds(a, 8, stride=DEEP), :] = src[g, a]
+        for g in range(DEEP):
+            lines = turned[g].T
+            for q in range(blocks):
+                at = (DEEP * q + g) * BACK
+                out_ref[at : at + LINE, :] = lines[q * WIDE : q * WIDE + LINE]
+
+    odd = lax.rem(count, 2)
+
+    @pl.when(odd == 1)
+    def _():
+        diffuse_step(one, two)
+        put(two)
+
+    @pl.when(odd == 0)
+    def _():
+        put(one)
+
+
+def diffuse_first_kernel(steps_ref, in_ref, out_ref, value_ref, var_ref, one, two, turned):
+    diffuse_body(steps_ref, in_ref, out_ref, one, two, turned, THERE)
+    for t in range(TILES):
+        for r, ref in enumerate((value_ref, var_ref)):
             at = (t * 2 + r) * THERE + LINE
-            ref[t * OBS_ROWS : t * OBS_ROWS + EARLY, :] = in_ref[at : at + EARLY, :]
-        for t in range(0, TILES, 8):
-            late = own_ref[pl.ds(t * OBS_ROWS + EARLY, 8, stride=OBS_ROWS), :]
-            out_ref[pl.ds((t * 2 + r) * BACK + LINE, 8, stride=2 * BACK), :] = late
-
-
-def diffuse_kernel(steps_ref, in_ref, out_ref, buf):
-    diffuse_body(steps_ref, in_ref, out_ref, buf, BACK)
+            ref[t * OBS_ROWS : (t + 1) * OBS_ROWS, :] = in_ref[at : at + OBS_ROWS, :]
+
+
+def diffuse_kernel(steps_ref, in_ref, out_ref, one, two, turned):
+    diffuse_body(steps_ref, in_ref, out_ref, one, two, turned, BACK)
 
 
 def slots_kernel(index_ref, weight_ref, out_ref):
@@ -288,16 +312,13 @@
     over_live(n, body)
 
 
-def adjoint_kernel(scale, count_ref, m0, m1, m2, m3, value_ref, var_ref, late_ref, slot_ref, ens_ref, out_ref, dep_ref,
-                   acc_ref, table_ref, adj_ref, proj_ref, list_ref):
+def adjoint_kernel(scale, count_ref, m0, m1, m2, m3, value_ref, var_ref, slot_ref, ens_ref, out_ref, dep_ref, acc_ref,
+                   table_ref, adj_ref, proj_ref, list_ref):
     slot_at = lax.broadcasted_iota(I32, (OBS_ROWS, LANES), 0) * LANES + lax.broadcasted_iota(I32, (OBS_ROWS, LANES), 1)
-    last = slot_at >= EARLY * LANES
     for s in range(TILES):
         at = slice(s * OBS_ROWS, (s + 1) * OBS_ROWS)
         model = (m0[at, :] + m1[at, :]) + (m2[at, :] + m3[at, :])
-        late = [late_ref[(s * 2 + r) * BACK + LINE : (s * 2 + r) * BACK + LINE + 1, :] for r in range(2)]
-        value, var = (jnp.where(last, x, ref[at, :]) for x, ref in zip(late, (value_ref, var_ref)))
-        weighted = var * (value - model)
+        weighted = var_ref[at, :] * (value_ref[at, :] - model)
         dep_ref[at, :] = jnp.where(slot_at < count_ref[s], weighted, 0.0)
     acc_ref[...] = jnp.zeros_like(acc_ref)
     n = live_blocks(count_ref, list_ref)
@@ -371,7 +392,9 @@
 
 
 def exchange(x):
-    return lax.all_to_all(x, "tile", 0, 0, tiled=True)
+    rows = x.shape[0] // TILES
+    x = x.reshape(TILES, rows // 2, 2, LANES)
+    return lax.all_to_all(x, "tile", 0, 0, tiled=True).reshape(TILES * rows, LANES)
 
 
 def shards(alpha, ensemble, step_count, obs_index, obs_weight, obs_count, obs_value, inv_var):
@@ -407,16 +430,16 @@
         name="slots",
     )(obs_index[0], obs_weight[0])
 
-    buf = pltpu.VMEM((2, LINE, 8, 8, LANES), F32)
+    buf = [pltpu.VMEM((DEEP, DEEP, 8, LANES), F32)] * 2 + [pltpu.VMEM((DEEP, LANES, LANES), F32)]
     moved, value, var = pl.pallas_call(
         diffuse_first_kernel,
         out_shape=(shape(LAT * BACK, LANES), flat, flat),
-        in_specs=[SMEM] + [VMEM] * 3,
+        in_specs=[SMEM, VMEM],
         out_specs=[VMEM] * 3,
-        scratch_shapes=[buf],
+        scratch_shapes=buf,
         compiler_params=params(16),
         name="diffuse_first",
-    )(steps, got, value, var)
+    )(steps, got)
     got = exchange(moved)
 
     block_list = pltpu.SMEM((BLOCKS + 8,), I32)
@@ -434,7 +457,7 @@
     sent, departure = pl.pallas_call(
         lambda *refs: adjoint_kernel(scale, *refs),
         out_shape=(shape(LAT * BACK, LANES), flat),
-        in_specs=[SMEM] + [VMEM] * 9,
+        in_specs=[SMEM] + [VMEM] * 8,
         out_specs=[VMEM] * 2,
         scratch_shapes=[
             pltpu.VMEM((4 * LO, HI), F32),
@@ -445,7 +468,7 @@
         ],
         compiler_params=params(24),
         name="adjoint",
-    )(counts, mine, *others, value, var, got, slots, ens)
+    )(counts, mine, *others, value, var, slots, ens)
     got = exchange(sent)
 
     moved = pl.pallas_call(
@@ -453,7 +476,7 @@
         out_shape=shape(LAT * BACK, LANES),
         in_specs=[SMEM, VMEM],
         out_specs=VMEM,
-        scratch_shapes=[buf],
+        scratch_shapes=buf,
         compiler_params=params(16),
         name="diffuse",
     )(steps, got)

time: 144 us -> 133 us (0.924)
  starting transfers between devices: 29 us -> 22.1 us
  local copies, waits for them, and re-layouts: 15 us -> 10.1 us
  Pallas kernels: 31.9 us -> 29.6 us
  blocking collectives: 19.9 us -> 21.9 us
    all_to_all x3, starting transfers between devices: 24.5 us -> 17.7 us  [exchange(): lax.all_to_all(x, 'tile', 0, 0, tiled=True).reshape(TILES * rows, LANES)]
    reshape x1, local copies, waits for them, and re-layouts: 5.24 us -> 2.49 us  [shards(): ens = jnp.pad(ensemble.reshape(GROUP, 2, 16, LON), ((0, 0), (0, 0)) + wide)]
    unnamed x22 -> x18, local copies, waits for them, and re-layouts: 3.18 us -> 0.98 us
    all_to_all x1, blocking collectives: 19.9 us -> 21.9 us  [exchange(): lax.all_to_all(x, 'tile', 0, 0, tiled=True).reshape(TILES * rows, LANES)]
    all_to_all x3, waiting for transfers between devices: 40.3 us -> 42.3 us  [exchange(): lax.all_to_all(x, 'tile', 0, 0, tiled=True).reshape(TILES * rows, LANES)]
  transfers between devices with their start and end apart: 6 -> 6, of which waited for: 5 -> 6; matrix products, arithmetic and copies ran while one was open for 6% -> 4% of each run, Pallas kernels for 2% -> 2%
where the time goes in v3:
time: 133 us; the launch traced here: 132 us
  waiting for transfers between devices  47.6 us (36%)
  Pallas kernels  29.6 us (22%)
  starting transfers between devices  22.1 us (17%)
  blocking collectives  21.9 us (16%)
  local copies, waits for them, and re-layouts  10.1 us (8%)
    all_to_all x3, waiting for transfers between devices, exchange(): lax.all_to_all(x, 'tile', 0, 0, tiled=True).reshape(TILES * rows, LANES)  42.3 us
    all_to_all x1, blocking collectives, exchange(): lax.all_to_all(x, 'tile', 0, 0, tiled=True).reshape(TILES * rows, LANES)  21.9 us
    all_to_all x3, starting transfers between devices, exchange(): lax.all_to_all(x, 'tile', 0, 0, tiled=True).reshape(TILES * rows, LANES)  17.7 us
    pallas_call x1, Pallas kernels, shards(): pl.pallas_call(lambda *refs: observe_kernel(scale, *refs), out_shape=flat...  8.63 us
    pallas_call x1, Pallas kernels, shards(): pl.pallas_call(lambda *refs: adjoint_kernel(scale, *refs), out_shape=(sha...  7.75 us
    ppermute x3, waiting for transfers between devices, shards(): lax.ppermute(mine, 'member', [(i, (i + k) % 4) for i in range(4)])  5.37 us
    pallas_call x1, Pallas kernels, shards(): pl.pallas_call(diffuse_kernel, out_shape=shape(LAT * BACK, LANES), in_spe...  4.55 us
    pallas_call x1, Pallas kernels, shards(): pl.pallas_call(diffuse_first_kernel, out_shape=(shape(LAT * BACK, LANES),...  4.49 us
  transfers between devices with their start and end apart: 6, of which 6 were waited for; matrix products, arithmetic and copies ran while one was open for 4% of the time, Pallas kernels for 2%

profile of v3, /device:TPU:1, one launch (start us, length us, event | category | flops | bytes accessed | tf_op | source)
XLA Modules:
  0.0 132.2 jit_solution(10472965585956983214)
XLA Ops:
  0.6 0.0 copy-start.4
  0.6 0.0 copy-start.5
  0.6 1.9 %reshape.46 = f32[160,1440]{1,0:T(8,128)S(1)} reshape(f32[20,4,2,1440]{3,2,1,0:T(2,128)} %param.8) | data formatting | bytes 1843200 | tf_op jit(solution)/shard_map/reshape | solution.py:407
  2.6 0.1 pad.8.alpha_ref
  2.6 0.0 copy-done.4
  2.7 0.0 copy-done.5
  2.7 0.0 copy-start.8
  2.7 1.4 %pack.1 = f32[2368,128]{1,0:T(8,128)} custom-call(f32[160,1536]{1,0:T(8,128)S(1)} %pad.8.alpha_ref, f32[256,128]{1,0:T(8,128)S(1)} %bitcast.19, f32[256,128]{1,0:T(8,128)S(1)} %bitcast.20), custom_call_target="tpu_custom_call" | custom-call | tf_op jit(solution)/shard_map/pack/pallas_call | solution.py:413
  4.1 0.0 copy-start
  4.1 0.9 copy-done
  5.1 9.4 %all-to-all-start = ((f32[32,37,2,128]{3,2,1,0:T(2,128)}), f32[32,37,2,128]{3,2,1,0:T(2,128)S(1)}, u32[]{:S(2)}, u32[]{:S(2)}) async-start(f32[32,37,2,128]{3,2,1,0:T(2,128)} %bitcast.3), calls=%async_computation | async-start | bytes 2424832 | tf_op jit(solution)/shard_map/all_to_all | solution.py:397
  14.5 0.0 copy-start.7
  14.5 0.0 copy-done.8
  14.5 0.6 dynamic_slice.3.steps_ref
  15.1 18.1 %all-to-all-done = f32[32,37,2,128]{3,2,1,0:T(2,128)S(1)} async-done(((f32[32,37,2,128]{3,2,1,0:T(2,128)}), f32[32,37,2,128]{3,2,1,0:T(2,128)S(1)}, u32[]{:S(2)}, u32[]{:S(2)}) %all-to-all-start) | async-done | bytes 1212448 | tf_op jit(solution)/shard_map/all_to_all | solution.py:397
  33.2 4.5 %diffuse_first.1 = (f32[1856,128]{1,0:T(8,128)}, f32[256,128]{1,0:T(8,128)S(1)}, f32[256,128]{1,0:T(8,128)S(1)}) custom-call(s32[1]{0:T(128)} %dynamic_slice.3.steps_ref, f32[2368,128]{1,0:T(8,128)S(1)} %bitcast.13), custom_call_target="tpu_custom_call" | custom-call | tf_op jit(solution)/shard_map/diffuse_first/pallas_call | solution.py:434
  37.7 4.4 %all-to-all-start.1 = ((f32[32,29,2,128]{3,2,1,0:T(2,128)}), f32[32,29,2,128]{3,2,1,0:T(2,128)}, u32[]{:S(2)}, u32[]{:S(2)}) async-start(f32[32,29,2,128]{3,2,1,0:T(2,128)} %bitcast.5), calls=%async_computation.1 | async-start | bytes 1900544 | tf_op jit(solution)/shard_map/all_to_all | solution.py:397
  42.1 0.0 copy-done.7
  42.2 2.5 %reshape.53 = bf16[20,2,16,1440]{3,2,1,0:T(8,128)(2,1)} reshape(bf16[20,4,4,2,1440]{4,3,2,1,0:T(2,128)(2,1)S(1)} %copy-done.7) | data formatting | bytes 3686400 | tf_op jit(solution)/shard_map/reshape | solution.py:408
  44.6 0.0 copy-start.2
  44.6 0.0 copy-start.3
  44.6 1.8 %pad.9.refs_2_.refs_8_ = bf16[20,2,16,1536]{3,2,1,0:T(8,128)(2,1)S(1)} pad(bf16[20,2,16,1440]{3,2,1,0:T(8,128)(2,1)} %reshape.53, bf16[]{:T(256)} %constant.14.clone.1), padding=0_0x0_0x0_0x0_96 | pad | bytes 3809282 | tf_op jit(solution)/shard_map/jit(_pad)/pad | solution.py:408
  46.5 0.0 copy-start.6
  46.5 0.0 copy-done.2
  46.5 0.0 copy-done.3
  46.5 2.5 %slots.1.refs_3_.refs_7_ = f32[256,8,128]{2,1,0:T(8,128)S(1)} custom-call(s32[32,4,1024]{2,1,0:T(4,128)S(1)} %bitcast.17, f32[32,4,1024]{2,1,0:T(4,128)S(1)} %bitcast.18), custom_call_target="tpu_custom_call" | custom-call | flops 8000000 | bytes 2097152 | tf_op jit(solution)/shard_map/slots/pallas_call | solution.py:423
  49.0 9.0 %all-to-all-done.1 = f32[32,29,2,128]{3,2,1,0:T(2,128)} async-done(((f32[32,29,2,128]{3,2,1,0:T(2,128)}), f32[32,29,2,128]{3,2,1,0:T(2,128)}, u32[]{:S(2)}, u32[]{:S(2)}) %all-to-all-start.1) | async-done | bytes 950304 | tf_op jit(solution)/shard_map/all_to_all | solution.py:397
  58.0 0.0 copy-done.6
  58.0 8.6 %observe.1.refs_1_ = f32[256,128]{1,0:T(8,128)S(1)} custom-call(s32[32]{0:T(128)S(1)} %bitcast.21, f32[1856,128]{1,0:T(8,128)} %bitcast.6.refs_1_, bf16[20,2,16,1536]{3,2,1,0:T(8,128)(2,1)S(1)} %pad.9.refs_2_.refs_8_, f32[256,8,128]{2,1,0:T(8,128)S(1)} %slots.1.refs_3_.refs_7_), custom_call_target="tpu_custom_call" | custom-call | tf_op jit(solution)/shard_map/observe/pallas_call | solution.py:446
  66.6 1.4 %collective-permute-start = (f32[256,128]{1,0:T(8,128)S(1)}, f32[256,128]{1,0:T(8,128)S(1)}, u32[]{:S(2)}, u32[]{:S(2)}) collective-permute-start(f32[256,128]{1,0:T(8,128)S(1)} %observe.1.refs_1_), channel_id=1, source_target_pairs={{0,32},{32,64},{64,96},{96,0},{1,33},{33,65},{65,97},{97,1},{2,34}... | collective-permute-start | bytes 393224 | tf_op jit(solution)/shard_map/ppermute | solution.py:455
  68.0 1.5 %collective-permute-start.1 = (f32[256,128]{1,0:T(8,128)S(1)}, f32[256,128]{1,0:T(8,128)S(1)}, u32[]{:S(2)}, u32[]{:S(2)}) collective-permute-start(f32[256,128]{1,0:T(8,128)S(1)} %observe.1.refs_1_), channel_id=1, source_target_pairs={{0,96},{32,0},{64,32},{96,64},{1,97},{33,1},{65,33},{97,65},{2,98}... | collective-permute-start | bytes 393224 | tf_op jit(solution)/shard_map/ppermute | solution.py:455
  69.5 1.6 %collective-permute-start.2 = (f32[256,128]{1,0:T(8,128)S(1)}, f32[256,128]{1,0:T(8,128)S(1)}, u32[]{:S(2)}, u32[]{:S(2)}) collective-permute-start(f32[256,128]{1,0:T(8,128)S(1)} %observe.1.refs_1_), channel_id=1, source_target_pairs={{0,64},{32,96},{64,0},{96,32},{1,65},{33,97},{65,1},{97,33},{2,66}... | collective-permute-start | bytes 393224 | tf_op jit(solution)/shard_map/ppermute | solution.py:455
  71.1 0.7 collective-permute-done.refs_2_
  71.8 0.3 collective-permute-done.1.refs_3_
  72.1 4.3 %collective-permute-done.2.refs_4_ = f32[256,128]{1,0:T(8,128)S(1)} collective-permute-done((f32[256,128]{1,0:T(8,128)S(1)}, f32[256,128]{1,0:T(8,128)S(1)}, u32[]{:S(2)}, u32[]{:S(2)}) %collective-permute-start.2) | collective-permute-done | bytes 131104 | tf_op jit(solution)/shard_map/ppermute | solution.py:455
  76.5 7.7 %adjoint.1 = (f32[1856,128]{1,0:T(8,128)S(1)}, f32[256,128]{1,0:T(8,128)S(1)}) custom-call(s32[32]{0:T(128)S(1)} %bitcast.22, f32[256,128]{1,0:T(8,128)S(1)} %observe.1.refs_1_, f32[256,128]{1,0:T(8,128)S(1)} %collective-permute-done.refs_2_, f32[256,128]{1,0:T(8,128)S(1)} %collective-permute-done.1.refs_3_, f32[256,128]{1,0:T(8,128)S(1)} %collective-permute-done.2.refs_4_, ...), custom_call_target="tpu_custom_call" | custom-call | tf_op jit(solution)/shard_map/adjoint/pallas_call | solution.py:457
  84.2 21.9 %all_to_all.20 = f32[32,29,2,128]{3,2,1,0:T(2,128)S(1)} all-to-all(f32[32,29,2,128]{3,2,1,0:T(2,128)S(1)} %bitcast.16), channel_id=1, replica_groups=mesh['member'=4,'tile'=32] {'tile'}, dimensions={0} | all-to-all | bytes 1900544 | tf_op jit(solution)/shard_map/all_to_all | solution.py:397
  106.1 0.0 copy-start.1
  106.1 4.5 %diffuse.1 = f32[1856,128]{1,0:T(8,128)} custom-call(s32[1]{0:T(128)} %dynamic_slice.3.steps_ref, f32[1856,128]{1,0:T(8,128)S(1)} %bitcast.15), custom_call_target="tpu_custom_call" | custom-call | tf_op jit(solution)/shard_map/diffuse/pallas_call | solution.py:474
  110.7 3.8 %all-to-all-start.3 = ((f32[32,29,2,128]{3,2,1,0:T(2,128)}), f32[32,29,2,128]{3,2,1,0:T(2,128)S(1)}, u32[]{:S(2)}, u32[]{:S(2)}) async-start(f32[32,29,2,128]{3,2,1,0:T(2,128)} %bitcast.11), calls=%async_computation.3 | async-start | bytes 1900544 | tf_op jit(solution)/shard_map/all_to_all | solution.py:397
  114.5 0.7 reshape.59
  115.1 15.1 %all-to-all-done.3 = f32[32,29,2,128]{3,2,1,0:T(2,128)S(1)} async-done(((f32[32,29,2,128]{3,2,1,0:T(2,128)}), f32[32,29,2,128]{3,2,1,0:T(2,128)S(1)}, u32[]{:S(2)}, u32[]{:S(2)}) %all-to-all-start.3) | async-done | bytes 950304 | tf_op jit(solution)/shard_map/all_to_all | solution.py:397
  130.3 0.0 copy-done.1
  130.3 0.3 gradient.1
  130.6 1.5 %reshape.58 = f32[20,4,2,1440]{3,2,1,0:T(2,128)} reshape(f32[160,1440]{1,0:T(8,128)S(1)} %gradient.1) | data formatting | bytes 1843200 | tf_op jit(solution)/shard_map/reshape | solution.py:493
Async XLA Ops:
  0.6 2.0 %copy-start.4 = (f32[32,1,1024]{2,1,0:T(1,128)S(1)}, f32[32,1,1024]{2,1,0:T(1,128)}, u32[]{:S(2)}) copy-start(f32[32,1,1024]{2,1,0:T(1,128)} %param.14) | copy-start | bytes 393220
  0.6 2.0 %copy-start.5 = (f32[32,1,1024]{2,1,0:T(1,128)S(1)}, f32[32,1,1024]{2,1,0:T(1,128)}, u32[]{:S(2)}) copy-start(f32[32,1,1024]{2,1,0:T(1,128)} %param.15) | copy-start | bytes 393220
  2.7 11.9 %copy-start.8 = (s32[4]{0:T(128)S(1)}, s32[4]{0:T(128)}, u32[]{:S(2)}) copy-start(s32[4]{0:T(128)} %param.10) | copy-start | bytes 52
  4.1 0.9 copy-start
  5.1 28.2 %all-to-all-start = ((f32[32,37,2,128]{3,2,1,0:T(2,128)}), f32[32,37,2,128]{3,2,1,0:T(2,128)S(1)}, u32[]{:S(2)}, u32[]{:S(2)}) async-start(f32[32,37,2,128]{3,2,1,0:T(2,128)} %bitcast.3), calls=%async_computation | async-start | bytes 2424832 | tf_op jit(solution)/shard_map/all_to_all | solution.py:397
  14.5 27.6 %copy-start.7 = (bf16[20,4,4,2,1440]{4,3,2,1,0:T(2,128)(2,1)S(1)}, bf16[20,4,4,2,1440]{4,3,2,1,0:T(2,128)(2,1)}, u32[]{:S(2)}) copy-start(bf16[20,4,4,2,1440]{4,3,2,1,0:T(2,128)(2,1)} %param.9) | copy-start | bytes 5529604
  37.7 20.3 %all-to-all-start.1 = ((f32[32,29,2,128]{3,2,1,0:T(2,128)}), f32[32,29,2,128]{3,2,1,0:T(2,128)}, u32[]{:S(2)}, u32[]{:S(2)}) async-start(f32[32,29,2,128]{3,2,1,0:T(2,128)} %bitcast.5), calls=%async_computation.1 | async-start | bytes 1900544 | tf_op jit(solution)/shard_map/all_to_all | solution.py:397
  44.6 1.8 %copy-start.2 = (s32[1,32,4,1024]{3,2,1,0:T(4,128)S(1)}, s32[1,32,4,1024]{3,2,1,0:T(4,128)}, u32[]{:S(2)}) copy-start(s32[1,32,4,1024]{3,2,1,0:T(4,128)} %param.11) | copy-start | bytes 1572868
  44.6 1.9 %copy-start.3 = (f32[1,32,4,1024]{3,2,1,0:T(4,128)S(1)}, f32[1,32,4,1024]{3,2,1,0:T(4,128)}, u32[]{:S(2)}) copy-start(f32[1,32,4,1024]{3,2,1,0:T(4,128)} %param.12) | copy-start | bytes 1572868
  46.5 11.5 %copy-start.6 = (s32[1,32]{1,0:T(1,128)S(1)}, s32[1,32]{1,0:T(1,128)}, u32[]{:S(2)}) copy-start(s32[1,32]{1,0:T(1,128)} %param.13) | copy-start | bytes 388
  66.6 5.2 %collective-permute-start = (f32[256,128]{1,0:T(8,128)S(1)}, f32[256,128]{1,0:T(8,128)S(1)}, u32[]{:S(2)}, u32[]{:S(2)}) collective-permute-start(f32[256,128]{1,0:T(8,128)S(1)} %observe.1.refs_1_), channel_id=1, source_target_pairs={{0,32},{32,64},{64,96},{96,0},{1,33},{33,65},{65,97},{97,1},{2,34}... | collective-permute-start | bytes 393224 | tf_op jit(solution)/shard_map/ppermute | solution.py:455
  68.0 4.1 %collective-permute-start.1 = (f32[256,128]{1,0:T(8,128)S(1)}, f32[256,128]{1,0:T(8,128)S(1)}, u32[]{:S(2)}, u32[]{:S(2)}) collective-permute-start(f32[256,128]{1,0:T(8,128)S(1)} %observe.1.refs_1_), channel_id=1, source_target_pairs={{0,96},{32,0},{64,32},{96,64},{1,97},{33,1},{65,33},{97,65},{2,98}... | collective-permute-start | bytes 393224 | tf_op jit(solution)/shard_map/ppermute | solution.py:455
  69.5 6.9 %collective-permute-start.2 = (f32[256,128]{1,0:T(8,128)S(1)}, f32[256,128]{1,0:T(8,128)S(1)}, u32[]{:S(2)}, u32[]{:S(2)}) collective-permute-start(f32[256,128]{1,0:T(8,128)S(1)} %observe.1.refs_1_), channel_id=1, source_target_pairs={{0,64},{32,96},{64,0},{96,32},{1,65},{33,97},{65,1},{97,33},{2,66}... | collective-permute-start | bytes 393224 | tf_op jit(solution)/shard_map/ppermute | solution.py:455
  106.1 24.2 %copy-start.1 = (f32[160,1536]{1,0:T(8,128)S(1)}, f32[160,1536]{1,0:T(8,128)}, u32[]{:S(2)}) copy-start(f32[160,1536]{1,0:T(8,128)} %copy-done) | copy-start | bytes 2949124
  110.7 19.6 %all-to-all-start.3 = ((f32[32,29,2,128]{3,2,1,0:T(2,128)}), f32[32,29,2,128]{3,2,1,0:T(2,128)S(1)}, u32[]{:S(2)}, u32[]{:S(2)}) async-start(f32[32,29,2,128]{3,2,1,0:T(2,128)} %bitcast.11), calls=%async_computation.3 | async-start | bytes 1900544 | tf_op jit(solution)/shard_map/all_to_all | solution.py:397

commit v4 on v3

--- a/solution.py
+++ b/solution.py
@@ -101,7 +101,11 @@
 
 def pack_kernel(alpha_ref, value_ref, var_ref, out_ref):
     def fetch(member, t):
-        return alpha_ref[member * 8 : member * 8 + 8, t * LANES : (t + 1) * LANES]
+        width = min(LANES, LON - t * LANES)
+        tile = alpha_ref[member, :, :, t * LANES : t * LANES + width].reshape(8, width)
+        if width == LANES:
+            return tile
+        return jnp.concatenate([tile, jnp.zeros((8, LANES - width), F32)], 1)
 
     def store(row, tile):
         out_ref[pl.ds(row, 8, stride=THERE), :] = tile
@@ -193,7 +197,7 @@
     diffuse_body(steps_ref, in_ref, out_ref, one, two, turned, BACK)
 
 
-def slots_kernel(index_ref, weight_ref, out_ref):
+def slots_kernel(count_ref, index_ref, weight_ref, out_ref, list_ref):
     def body(s, carry):
         index = index_ref[s]
         weight = weight_ref[s]
@@ -216,6 +220,7 @@
         return carry
 
     lax.fori_loop(0, TILES, body, 0)
+    live_blocks(count_ref, list_ref)
 
 
 def live_blocks(count_ref, list_ref):
@@ -225,25 +230,29 @@
         return n + lax.div(count_ref[s] + (LANES - 1), LANES)
 
     n = lax.fori_loop(0, TILES, body, 0)
-    for j in range(2 * FEW):
+    for j in range(2 * SIZES[-1]):
         list_ref[n + j] = 0
-    return n
+    list_ref[LISTED - 1] = n
 
 
 def over_live(n, body):
-    many = lax.div(n, 2 * MANY)
-    done = many * (2 * MANY)
-
     def large(i, carry):
-        body(i * (2 * MANY), MANY)
+        body(i * (2 * SIZES[0]), SIZES[0])
         return carry
 
-    def small(i, carry):
-        body(done + i * (2 * FEW), FEW)
-        return carry
-
+    many = lax.div(n, 2 * SIZES[0])
     lax.fori_loop(0, many, large, 0)
-    lax.fori_loop(0, lax.div(n - done + (2 * FEW - 1), 2 * FEW), small, 0)
+    done = many * (2 * SIZES[0])
+    left = lax.div(n - done + (2 * SIZES[-1] - 1), 2 * SIZES[-1]) * SIZES[-1]
+    for size in SIZES:
+        fits = left >= size
+
+        @pl.when(fits)
+        def _(done=done, size=size):
+            body(done, size)
+
+        done += jnp.where(fits, 2 * size, 0)
+        left -= jnp.where(fits, size, 0)
 
 
 def slot_rows(slot_ref, pair):
@@ -261,10 +270,11 @@
     return high, (x - high.astype(F32)).astype(BF16)
 
 
-MANY, FEW = 8, 2
-
-
-def observe_kernel(scale, count_ref, got_ref, ens_ref, slot_ref, out_ref, inc_ref, table_ref, list_ref):
+SIZES = (16, 8, 4, 2)
+LISTED = BLOCKS + 16
+
+
+def observe_kernel(scale, list_ref, got_ref, ens_ref, slot_ref, out_ref, inc_ref, table_ref):
     for t in range(COLS):
         total = [jnp.zeros((8, LANES), F32) for f in range(FLD)]
         for m in range(GROUP):
@@ -293,7 +303,7 @@
     left = jnp.concatenate([parts[0][0], parts[1][0], parts[0][1], parts[1][1]], 0)
 
     out_ref[...] = jnp.zeros_like(out_ref)
-    n = live_blocks(count_ref, list_ref)
+    n = list_ref[LISTED - 1]
     columns = lax.broadcasted_iota(I32, (LO, BLOCK), 0).astype(F32)
 
     def body(start, pairs):
@@ -312,8 +322,8 @@
     over_live(n, body)
 
 
-def adjoint_kernel(scale, count_ref, m0, m1, m2, m3, value_ref, var_ref, slot_ref, ens_ref, out_ref, dep_ref, acc_ref,
-                   table_ref, adj_ref, proj_ref, list_ref):
+def adjoint_kernel(scale, count_ref, list_ref, m0, m1, m2, m3, value_ref, var_ref, slot_ref, ens_ref, out_ref, dep_ref,
+                   acc_ref, table_ref, adj_ref, proj_ref):
     slot_at = lax.broadcasted_iota(I32, (OBS_ROWS, LANES), 0) * LANES + lax.broadcasted_iota(I32, (OBS_ROWS, LANES), 1)
     for s in range(TILES):
         at = slice(s * OBS_ROWS, (s + 1) * OBS_ROWS)
@@ -321,7 +331,7 @@
         weighted = var_ref[at, :] * (value_ref[at, :] - model)
         dep_ref[at, :] = jnp.where(slot_at < count_ref[s], weighted, 0.0)
     acc_ref[...] = jnp.zeros_like(acc_ref)
-    n = live_blocks(count_ref, list_ref)
+    n = list_ref[LISTED - 1]
     columns = lax.broadcasted_iota(I32, (LO, BLOCK), 0).astype(F32).astype(BF16)
 
     def body(start, pairs):
@@ -383,8 +393,8 @@
         for t in range(COLS):
             width = min(LANES, LON - t * LANES)
             tile = unpack_tile(got_ref, m, t, cache)
-            at = (slice(m * 8, m * 8 + 8), slice(t * LANES, t * LANES + width))
-            out_ref[at] = alpha_ref[at] - tile[:, :width]
+            at = (m, slice(None), slice(None), slice(t * LANES, t * LANES + width))
+            out_ref[at] = alpha_ref[at] - tile[:, :width].reshape(LEV, ROWS, width)
 
 
 def shape(*dims, dtype=F32):
@@ -404,7 +414,6 @@
     steps = lax.dynamic_slice(step_count, (lax.rem(me, LEV),), (1,))
     counts = obs_count[0]
     wide = ((0, 0), (0, COLS * LANES - LON))
-    rows = jnp.pad(alpha.reshape(GROUP * 8, LON), wide)
     ens = jnp.pad(ensemble.reshape(GROUP, 2, 16, LON), ((0, 0), (0, 0)) + wide)
     value = obs_value.reshape(TILES * OBS_ROWS, LANES)
     var = inv_var.reshape(TILES * OBS_ROWS, LANES)
@@ -417,18 +426,18 @@
         out_specs=VMEM,
         compiler_params=params(16),
         name="pack",
-    )(rows, value, var)
+    )(alpha, value, var)
     got = exchange(sent)
 
-    slots = pl.pallas_call(
+    slots, listed = pl.pallas_call(
         slots_kernel,
-        out_shape=shape(BLOCKS, 8, LANES),
-        in_specs=[VMEM] * 2,
-        out_specs=VMEM,
+        out_shape=(shape(BLOCKS, 8, LANES), shape(LISTED, dtype=I32)),
+        in_specs=[SMEM] + [VMEM] * 2,
+        out_specs=(VMEM, SMEM),
         compiler_params=params(16),
         cost_estimate=pl.CostEstimate(flops=8000000, bytes_accessed=2097152, transcendentals=0),
         name="slots",
-    )(obs_index[0], obs_weight[0])
+    )(counts, obs_index[0], obs_weight[0])
 
     buf = [pltpu.VMEM((DEEP, DEEP, 8, LANES), F32)] * 2 + [pltpu.VMEM((DEEP, LANES, LANES), F32)]
     moved, value, var = pl.pallas_call(
@@ -442,33 +451,31 @@
     )(steps, got)
     got = exchange(moved)
 
-    block_list = pltpu.SMEM((BLOCKS + 8,), I32)
     mine = pl.pallas_call(
         lambda *refs: observe_kernel(scale, *refs),
         out_shape=flat,
         in_specs=[SMEM] + [VMEM] * 3,
         out_specs=VMEM,
-        scratch_shapes=[pltpu.VMEM((COLS, 32, LANES), F32), pltpu.VMEM((2 * HI, LANES), F32), block_list],
+        scratch_shapes=[pltpu.VMEM((COLS, 32, LANES), F32), pltpu.VMEM((2 * HI, LANES), F32)],
         compiler_params=params(16),
         name="observe",
-    )(counts, got, ens, slots)
+    )(listed, got, ens, slots)
     others = [lax.ppermute(mine, "member", [(i, (i + k) % 4) for i in range(4)]) for k in (1, 3, 2)]
 
     sent, departure = pl.pallas_call(
         lambda *refs: adjoint_kernel(scale, *refs),
         out_shape=(shape(LAT * BACK, LANES), flat),
-        in_specs=[SMEM] + [VMEM] * 8,
+        in_specs=[SMEM] * 2 + [VMEM] * 8,
         out_specs=[VMEM] * 2,
         scratch_shapes=[
             pltpu.VMEM((4 * LO, HI), F32),
             pltpu.VMEM((2 * HI, LANES), F32),
             pltpu.VMEM((COLS, 32, LANES), F32),
             pltpu.VMEM((COLS, GROUP * 8, LANES), F32),
-            block_list,
         ],
         compiler_params=params(24),
         name="adjoint",
-    )(counts, mine, *others, value, var, slots, ens)
+    )(counts, listed, mine, *others, value, var, slots, ens)
     got = exchange(sent)
 
     moved = pl.pallas_call(
@@ -484,13 +491,13 @@
 
     gradient = pl.pallas_call(
         gradient_kernel,
-        out_shape=shape(GROUP * 8, LON),
+        out_shape=shape(*alpha.shape),
         in_specs=[VMEM] * 2,
         out_specs=VMEM,
         compiler_params=params(16),
         name="gradient",
-    )(rows, got)
-    return gradient.reshape(alpha.shape), departure.reshape(1, TILES, SLOT)
+    )(alpha, got)
+    return gradient, departure.reshape(1, TILES, SLOT)
 
 
 def solution(mesh):

time: 133 us -> 130 us (0.977)
  waiting for transfers between devices: 47.6 us -> 45.5 us
  local copies, waits for them, and re-layouts: 10.1 us -> 8.6 us
    reshape x3 -> x1, local copies, waits for them, and re-layouts: 4.15 us -> 0.68 us  [shards(): return (gradient, departure.reshape(1, TILES, SLOT))]
    pallas_call x2, Pallas kernels: 2.8 us -> 5.46 us  [the longest x1 4.07 us: shards(): pl.pallas_call(slots_kernel, out_shape=(shape(BLOCKS, 8, LANES), shape(LI...]
    unnamed x18, local copies, waits for them, and re-layouts: 0.98 us -> 3.03 us
    all_to_all x3, waiting for transfers between devices: 42.3 us -> 40.7 us  [exchange(): lax.all_to_all(x, 'tile', 0, 0, tiled=True).reshape(TILES * rows, LANES)]
    pallas_call x1, Pallas kernels: 7.75 us -> 6.31 us  [shards(): pl.pallas_call(lambda *refs: adjoint_kernel(scale, *refs), out_shape=(sha...]
    pallas_call x1, Pallas kernels: 8.63 us -> 7.2 us  [shards(): pl.pallas_call(lambda *refs: observe_kernel(scale, *refs), out_shape=flat...]
  transfers between devices with their start and end apart: 6 -> 6, of which waited for: 6 -> 5; matrix products, arithmetic and copies ran while one was open for 4% -> 4% of each run, Pallas kernels for 2% -> 3%
where the time goes in v4:
time: 130 us; the launch traced here: 129 us
  waiting for transfers between devices  45.5 us (35%)
  Pallas kernels  29.4 us (23%)
  blocking collectives  22.9 us (18%)
  starting transfers between devices  22.1 us (17%)
  local copies, waits for them, and re-layouts  8.6 us (7%)
    all_to_all x3, waiting for transfers between devices, exchange(): lax.all_to_all(x, 'tile', 0, 0, tiled=True).reshape(TILES * rows, LANES)  40.7 us
    all_to_all x1, blocking collectives, exchange(): lax.all_to_all(x, 'tile', 0, 0, tiled=True).reshape(TILES * rows, LANES)  22.9 us
    all_to_all x3, starting transfers between devices, exchange(): lax.all_to_all(x, 'tile', 0, 0, tiled=True).reshape(TILES * rows, LANES)  17.7 us
    pallas_call x1, Pallas kernels, shards(): pl.pallas_call(lambda *refs: observe_kernel(scale, *refs), out_shape=flat...  7.2 us
    pallas_call x1, Pallas kernels, shards(): pl.pallas_call(lambda *refs: adjoint_kernel(scale, *refs), out_shape=(sha...  6.31 us
    ppermute x3, waiting for transfers between devices, shards(): lax.ppermute(mine, 'member', [(i, (i + k) % 4) for i in range(4)])  4.82 us
    pallas_call x1, Pallas kernels, shards(): pl.pallas_call(diffuse_kernel, out_shape=shape(LAT * BACK, LANES), in_spe...  4.54 us
    pallas_call x1, Pallas kernels, shards(): pl.pallas_call(diffuse_first_kernel, out_shape=(shape(LAT * BACK, LANES),...  4.47 us
  transfers between devices with their start and end apart: 6, of which 5 were waited for; matrix products, arithmetic and copies ran while one was open for 4% of the time, Pallas kernels for 3%

profile of v4, /device:TPU:1, one launch (start us, length us, event | category | flops | bytes accessed | tf_op | source)
XLA Modules:
  0.0 129.3 jit_solution(8694795872354950021)
XLA Ops:
  0.6 0.0 copy-start
  0.6 1.2 copy-done
  1.8 0.0 copy-start.4
  1.8 0.9 copy-done.4
  2.7 0.0 copy-start.5
  2.7 0.9 copy-done.5
  3.6 0.0 copy-start.8
  3.6 1.4 %pack.1 = f32[2368,128]{1,0:T(8,128)} custom-call(f32[20,4,2,1440]{3,2,1,0:T(2,128)S(1)} %copy-done, f32[256,128]{1,0:T(8,128)S(1)} %bitcast.19, f32[256,128]{1,0:T(8,128)S(1)} %bitcast.20), custom_call_target="tpu_custom_call" | custom-call | tf_op jit(solution)/shard_map/pack/pallas_call | solution.py:422
  5.1 9.4 %all-to-all-start = ((f32[32,37,2,128]{3,2,1,0:T(2,128)}), f32[32,37,2,128]{3,2,1,0:T(2,128)S(1)}, u32[]{:S(2)}, u32[]{:S(2)}) async-start(f32[32,37,2,128]{3,2,1,0:T(2,128)} %bitcast.5), calls=%async_computation | async-start | bytes 2424832 | tf_op jit(solution)/shard_map/all_to_all | solution.py:407
  14.5 0.0 copy-start.7
  14.6 0.0 copy-done.8
  14.6 0.6 dynamic_slice.3.steps_ref
  15.2 18.1 %all-to-all-done = f32[32,37,2,128]{3,2,1,0:T(2,128)S(1)} async-done(((f32[32,37,2,128]{3,2,1,0:T(2,128)}), f32[32,37,2,128]{3,2,1,0:T(2,128)S(1)}, u32[]{:S(2)}, u32[]{:S(2)}) %all-to-all-start) | async-done | bytes 1212448 | tf_op jit(solution)/shard_map/all_to_all | solution.py:407
  33.3 4.5 %diffuse_first.1 = (f32[1856,128]{1,0:T(8,128)}, f32[256,128]{1,0:T(8,128)S(1)}, f32[256,128]{1,0:T(8,128)S(1)}) custom-call(s32[1]{0:T(128)} %dynamic_slice.3.steps_ref, f32[2368,128]{1,0:T(8,128)S(1)} %bitcast.13), custom_call_target="tpu_custom_call" | custom-call | tf_op jit(solution)/shard_map/diffuse_first/pallas_call | solution.py:443
  37.7 4.4 %all-to-all-start.1 = ((f32[32,29,2,128]{3,2,1,0:T(2,128)}), f32[32,29,2,128]{3,2,1,0:T(2,128)}, u32[]{:S(2)}, u32[]{:S(2)}) async-start(f32[32,29,2,128]{3,2,1,0:T(2,128)} %bitcast.7), calls=%async_computation.1 | async-start | bytes 1900544 | tf_op jit(solution)/shard_map/all_to_all | solution.py:407
  42.2 0.0 copy-done.7
  42.2 2.5 %reshape.46 = bf16[20,2,16,1440]{3,2,1,0:T(8,128)(2,1)} reshape(bf16[20,4,4,2,1440]{4,3,2,1,0:T(2,128)(2,1)S(1)} %copy-done.7) | data formatting | bytes 3686400 | tf_op jit(solution)/shard_map/reshape | solution.py:417
  44.7 0.0 copy-start.2
  44.7 0.0 copy-start.3
  44.7 0.0 copy-start.6
  44.7 1.8 %pad.4.refs_2_.refs_9_ = bf16[20,2,16,1536]{3,2,1,0:T(8,128)(2,1)S(1)} pad(bf16[20,2,16,1440]{3,2,1,0:T(8,128)(2,1)} %reshape.46, bf16[]{:T(256)} %constant.12.clone.1), padding=0_0x0_0x0_0x0_96 | pad | bytes 3809282 | tf_op jit(solution)/shard_map/jit(_pad)/pad | solution.py:417
  46.5 0.0 copy-done.2
  46.5 0.0 copy-done.3
  46.5 0.0 copy-done.6
  46.5 4.1 %slots.1 = (f32[256,8,128]{2,1,0:T(8,128)S(1)}, s32[272]{0:T(512)S(1)}) custom-call(s32[32]{0:T(128)S(1)} %bitcast.21, s32[32,4,1024]{2,1,0:T(4,128)S(1)} %bitcast.17, f32[32,4,1024]{2,1,0:T(4,128)S(1)} %bitcast.18), custom_call_target="tpu_custom_call" | custom-call | flops 8000000 | bytes 2097152 | tf_op jit(solution)/shard_map/slots/pallas_call | solution.py:432
  50.6 7.4 %all-to-all-done.1 = f32[32,29,2,128]{3,2,1,0:T(2,128)} async-done(((f32[32,29,2,128]{3,2,1,0:T(2,128)}), f32[32,29,2,128]{3,2,1,0:T(2,128)}, u32[]{:S(2)}, u32[]{:S(2)}) %all-to-all-start.1) | async-done | bytes 950304 | tf_op jit(solution)/shard_map/all_to_all | solution.py:407
  58.0 7.2 %observe.1.refs_2_ = f32[256,128]{1,0:T(8,128)S(1)} custom-call(s32[272]{0:T(512)S(1)} %get-tuple-element.9.refs_0_.refs_1_, f32[1856,128]{1,0:T(8,128)} %bitcast.8.refs_1_, bf16[20,2,16,1536]{3,2,1,0:T(8,128)(2,1)S(1)} %pad.4.refs_2_.refs_9_, f32[256,8,128]{2,1,0:T(8,128)S(1)} %get-tuple-element.11.refs_3_.refs_8_), custom_call_target="tpu_custom_call" | custom-call | tf_op jit(solution)/shard_map/observe/pallas_call | solution.py:454
  65.2 3.0 %collective-permute-start.2 = (f32[256,128]{1,0:T(8,128)S(1)}, f32[256,128]{1,0:T(8,128)S(1)}, u32[]{:S(2)}, u32[]{:S(2)}) collective-permute-start(f32[256,128]{1,0:T(8,128)S(1)} %observe.1.refs_2_), channel_id=1, source_target_pairs={{0,64},{32,96},{64,0},{96,32},{1,65},{33,97},{65,1},{97,33},{2,66}... | collective-permute-start | bytes 393224 | tf_op jit(solution)/shard_map/ppermute | solution.py:463
  68.2 0.8 collective-permute-start.1
  69.0 0.7 collective-permute-start
  69.7 1.7 %collective-permute-done.2.refs_5_ = f32[256,128]{1,0:T(8,128)S(1)} collective-permute-done((f32[256,128]{1,0:T(8,128)S(1)}, f32[256,128]{1,0:T(8,128)S(1)}, u32[]{:S(2)}, u32[]{:S(2)}) %collective-permute-start.2) | collective-permute-done | bytes 131104 | tf_op jit(solution)/shard_map/ppermute | solution.py:463
  71.4 3.1 %collective-permute-done.1.refs_4_ = f32[256,128]{1,0:T(8,128)S(1)} collective-permute-done((f32[256,128]{1,0:T(8,128)S(1)}, f32[256,128]{1,0:T(8,128)S(1)}, u32[]{:S(2)}, u32[]{:S(2)}) %collective-permute-start.1) | collective-permute-done | bytes 131104 | tf_op jit(solution)/shard_map/ppermute | solution.py:463
  74.5 0.0 collective-permute-done.refs_3_
  74.5 6.3 %adjoint.1 = (f32[1856,128]{1,0:T(8,128)S(1)}, f32[256,128]{1,0:T(8,128)S(1)}) custom-call(s32[32]{0:T(128)S(1)} %bitcast.22, s32[272]{0:T(512)S(1)} %get-tuple-element.9.refs_0_.refs_1_, f32[256,128]{1,0:T(8,128)S(1)} %observe.1.refs_2_, f32[256,128]{1,0:T(8,128)S(1)} %collective-permute-done.refs_3_, f32[256,128]{1,0:T(8,128)S(1)} %collective-permute-done.1.refs_4_, ...), custom_call_target="tpu_custom_call" | custom-call | tf_op jit(solution)/shard_map/adjoint/pallas_call | solution.py:465
  80.8 22.9 %all_to_all.20 = f32[32,29,2,128]{3,2,1,0:T(2,128)S(1)} all-to-all(f32[32,29,2,128]{3,2,1,0:T(2,128)S(1)} %bitcast.16), channel_id=1, replica_groups=mesh['member'=4,'tile'=32] {'tile'}, dimensions={0} | all-to-all | bytes 1900544 | tf_op jit(solution)/shard_map/all_to_all | solution.py:407
  103.7 0.0 copy-start.1
  103.7 4.5 %diffuse.1 = f32[1856,128]{1,0:T(8,128)} custom-call(s32[1]{0:T(128)} %dynamic_slice.3.steps_ref, f32[1856,128]{1,0:T(8,128)S(1)} %bitcast.15), custom_call_target="tpu_custom_call" | custom-call | tf_op jit(solution)/shard_map/diffuse/pallas_call | solution.py:481
  108.3 3.8 %all-to-all-start.3 = ((f32[32,29,2,128]{3,2,1,0:T(2,128)}), f32[32,29,2,128]{3,2,1,0:T(2,128)S(1)}, u32[]{:S(2)}, u32[]{:S(2)}) async-start(f32[32,29,2,128]{3,2,1,0:T(2,128)} %bitcast.11), calls=%async_computation.3 | async-start | bytes 1900544 | tf_op jit(solution)/shard_map/all_to_all | solution.py:407
  112.1 0.7 reshape.51
  112.8 15.1 %all-to-all-done.3 = f32[32,29,2,128]{3,2,1,0:T(2,128)S(1)} async-done(((f32[32,29,2,128]{3,2,1,0:T(2,128)}), f32[32,29,2,128]{3,2,1,0:T(2,128)S(1)}, u32[]{:S(2)}, u32[]{:S(2)}) %all-to-all-start.3) | async-done | bytes 950304 | tf_op jit(solution)/shard_map/all_to_all | solution.py:407
  127.9 0.0 copy-done.1
  127.9 1.4 %gradient.1 = f32[20,4,2,1440]{3,2,1,0:T(2,128)} custom-call(f32[20,4,2,1440]{3,2,1,0:T(2,128)S(1)} %copy-done.1, f32[1856,128]{1,0:T(8,128)S(1)} %bitcast.14), custom_call_target="tpu_custom_call" | custom-call | tf_op jit(solution)/shard_map/gradient/pallas_call | solution.py:492
Async XLA Ops:
  0.6 1.2 copy-start
  1.8 0.9 copy-start.4
  2.7 0.9 copy-start.5
  3.6 10.9 %copy-start.8 = (s32[4]{0:T(128)S(1)}, s32[4]{0:T(128)}, u32[]{:S(2)}) copy-start(s32[4]{0:T(128)} %param.10) | copy-start | bytes 52
  5.1 28.2 %all-to-all-start = ((f32[32,37,2,128]{3,2,1,0:T(2,128)}), f32[32,37,2,128]{3,2,1,0:T(2,128)S(1)}, u32[]{:S(2)}, u32[]{:S(2)}) async-start(f32[32,37,2,128]{3,2,1,0:T(2,128)} %bitcast.5), calls=%async_computation | async-start | bytes 2424832 | tf_op jit(solution)/shard_map/all_to_all | solution.py:407
  14.5 27.6 %copy-start.7 = (bf16[20,4,4,2,1440]{4,3,2,1,0:T(2,128)(2,1)S(1)}, bf16[20,4,4,2,1440]{4,3,2,1,0:T(2,128)(2,1)}, u32[]{:S(2)}) copy-start(bf16[20,4,4,2,1440]{4,3,2,1,0:T(2,128)(2,1)} %param.9) | copy-start | bytes 5529604
  37.7 20.3 %all-to-all-start.1 = ((f32[32,29,2,128]{3,2,1,0:T(2,128)}), f32[32,29,2,128]{3,2,1,0:T(2,128)}, u32[]{:S(2)}, u32[]{:S(2)}) async-start(f32[32,29,2,128]{3,2,1,0:T(2,128)} %bitcast.7), calls=%async_computation.1 | async-start | bytes 1900544 | tf_op jit(solution)/shard_map/all_to_all | solution.py:407
  44.7 1.8 %copy-start.2 = (s32[1,32,4,1024]{3,2,1,0:T(4,128)S(1)}, s32[1,32,4,1024]{3,2,1,0:T(4,128)}, u32[]{:S(2)}) copy-start(s32[1,32,4,1024]{3,2,1,0:T(4,128)} %param.11) | copy-start | bytes 1572868
  44.7 1.8 %copy-start.3 = (f32[1,32,4,1024]{3,2,1,0:T(4,128)S(1)}, f32[1,32,4,1024]{3,2,1,0:T(4,128)}, u32[]{:S(2)}) copy-start(f32[1,32,4,1024]{3,2,1,0:T(4,128)} %param.12) | copy-start | bytes 1572868
  44.7 1.9 %copy-start.6 = (s32[1,32]{1,0:T(1,128)S(1)}, s32[1,32]{1,0:T(1,128)}, u32[]{:S(2)}) copy-start(s32[1,32]{1,0:T(1,128)} %param.13) | copy-start | bytes 388
  65.2 6.1 %collective-permute-start.2 = (f32[256,128]{1,0:T(8,128)S(1)}, f32[256,128]{1,0:T(8,128)S(1)}, u32[]{:S(2)}, u32[]{:S(2)}) collective-permute-start(f32[256,128]{1,0:T(8,128)S(1)} %observe.1.refs_2_), channel_id=1, source_target_pairs={{0,64},{32,96},{64,0},{96,32},{1,65},{33,97},{65,1},{97,33},{2,66}... | collective-permute-start | bytes 393224 | tf_op jit(solution)/shard_map/ppermute | solution.py:463
  68.2 6.3 %collective-permute-start.1 = (f32[256,128]{1,0:T(8,128)S(1)}, f32[256,128]{1,0:T(8,128)S(1)}, u32[]{:S(2)}, u32[]{:S(2)}) collective-permute-start(f32[256,128]{1,0:T(8,128)S(1)} %observe.1.refs_2_), channel_id=1, source_target_pairs={{0,96},{32,0},{64,32},{96,64},{1,97},{33,1},{65,33},{97,65},{2,98}... | collective-permute-start | bytes 393224 | tf_op jit(solution)/shard_map/ppermute | solution.py:463
  69.0 5.5 %collective-permute-start = (f32[256,128]{1,0:T(8,128)S(1)}, f32[256,128]{1,0:T(8,128)S(1)}, u32[]{:S(2)}, u32[]{:S(2)}) collective-permute-start(f32[256,128]{1,0:T(8,128)S(1)} %observe.1.refs_2_), channel_id=1, source_target_pairs={{0,32},{32,64},{64,96},{96,0},{1,33},{33,65},{65,97},{97,1},{2,34}... | collective-permute-start | bytes 393224 | tf_op jit(solution)/shard_map/ppermute | solution.py:463
  103.7 24.2 %copy-start.1 = (f32[20,4,2,1440]{3,2,1,0:T(2,128)S(1)}, f32[20,4,2,1440]{3,2,1,0:T(2,128)}, u32[]{:S(2)}) copy-start(f32[20,4,2,1440]{3,2,1,0:T(2,128)} %alpha_ref.3) | copy-start | bytes 2764804
  108.3 19.6 %all-to-all-start.3 = ((f32[32,29,2,128]{3,2,1,0:T(2,128)}), f32[32,29,2,128]{3,2,1,0:T(2,128)S(1)}, u32[]{:S(2)}, u32[]{:S(2)}) async-start(f32[32,29,2,128]{3,2,1,0:T(2,128)} %bitcast.11), calls=%async_computation.3 | async-start | bytes 1900544 | tf_op jit(solution)/shard_map/all_to_all | solution.py:407

commit v5 on v4

--- a/solution.py
+++ b/solution.py
@@ -21,7 +21,8 @@
 LINE = -(-PIECES * PIECE // LANES)
 COLS = -(-LON // LANES)
 OBS_ROWS = SLOT // LANES
-THERE, BACK = LINE + OBS_ROWS, LINE
+HALF_VAR = OBS_ROWS // ROWS
+THERE, BACK = LINE + HALF_VAR + 1, LINE
 DEEP, WIDE = 16, 32
 
 CHUNK = 90
@@ -34,6 +35,7 @@
 F32, BF16, I32 = jnp.float32, jnp.bfloat16, jnp.int32
 VMEM = pl.BlockSpec(memory_space=pltpu.VMEM)
 SMEM = pl.BlockSpec(memory_space=pltpu.SMEM)
+HBM = pl.BlockSpec(memory_space=pltpu.HBM)
 
 
 def params(mib):
@@ -65,9 +67,9 @@
     return value
 
 
-def pack_rows(fetch, store, line):
-    for mgrp in range(MGRP):
-        for half in range(2):
+def pack_rows(fetch, store, line, halves=range(2)):
+    for half in halves:
+        for mgrp in range(MGRP):
             cache = {}
             for j in range(LINE):
 
@@ -99,7 +101,14 @@
     return assemble(fetch, where_from, cache)
 
 
-def pack_kernel(alpha_ref, value_ref, var_ref, out_ref):
+def pack_kernel(member_ref, alpha_hbm, value_hbm, var_hbm, out_hbm, alpha_ref, value_ref, var_ref, out_ref, sems):
+    loads = [
+        pltpu.make_async_copy(src, dst, sems.at[k])
+        for k, (src, dst) in enumerate(((alpha_hbm, alpha_ref), (value_hbm, value_ref), (var_hbm, var_ref)))
+    ]
+    for load in loads:
+        load.start()
+
     def fetch(member, t):
         width = min(LANES, LON - t * LANES)
         tile = alpha_ref[member, :, :, t * LANES : t * LANES + width].reshape(8, width)
@@ -110,11 +119,27 @@
     def store(row, tile):
         out_ref[pl.ds(row, 8, stride=THERE), :] = tile
 
-    pack_rows(fetch, store, THERE)
-    for d in range(TILES):
-        for r, ref in enumerate((value_ref, var_ref)):
-            at = (d * 2 + r) * THERE + LINE
-            out_ref[at : at + OBS_ROWS, :] = ref[d * OBS_ROWS : (d + 1) * OBS_ROWS, :]
+    loads[0].wait()
+    rows = TILES * THERE
+    stores = []
+    for half in range(2):
+        pack_rows(fetch, store, THERE, (half,))
+        if half == 0:
+            loads[1].wait()
+            loads[2].wait()
+        for d in range(half * TILES // 2, (half + 1) * TILES // 2):
+            for r in range(ROWS):
+                at, var_at = (d * 2 + r) * THERE + LINE, d * OBS_ROWS + r * HALF_VAR
+                out_ref[at : at + HALF_VAR, :] = var_ref[var_at : var_at + HALF_VAR, :]
+        for d in range(half * TILES // 2, (half + 1) * TILES // 2, 8):
+            for r in range(ROWS):
+                quarter = value_ref[pl.ds(d * OBS_ROWS + member_ref[0] * 2 + r, 8, stride=OBS_ROWS), :]
+                out_ref[pl.ds((d * 2 + r) * THERE + THERE - 1, 8, stride=2 * THERE), :] = quarter
+        at = slice(half * rows, (half + 1) * rows)
+        stores.append(pltpu.make_async_copy(out_ref.at[at], out_hbm.at[at], sems.at[3 + half]))
+        stores[-1].start()
+    for done in stores:
+        done.wait()
 
 
 def diffuse_step(src, dst):
@@ -187,10 +212,11 @@
 
 def diffuse_first_kernel(steps_ref, in_ref, out_ref, value_ref, var_ref, one, two, turned):
     diffuse_body(steps_ref, in_ref, out_ref, one, two, turned, THERE)
-    for t in range(TILES):
-        for r, ref in enumerate((value_ref, var_ref)):
-            at = (t * 2 + r) * THERE + LINE
-            ref[t * OBS_ROWS : (t + 1) * OBS_ROWS, :] = in_ref[at : at + OBS_ROWS, :]
+    for row in range(LAT):
+        at = row * THERE + LINE
+        var_ref[row * HALF_VAR : (row + 1) * HALF_VAR, :] = in_ref[at : at + HALF_VAR, :]
+    for row in range(0, LAT, 8):
+        value_ref[row : row + 8, :] = in_ref[pl.ds(row * THERE + THERE - 1, 8, stride=THERE), :]
 
 
 def diffuse_kernel(steps_ref, in_ref, out_ref, one, two, turned):
@@ -274,11 +300,12 @@
 LISTED = BLOCKS + 16
 
 
-def observe_kernel(scale, list_ref, got_ref, ens_ref, slot_ref, out_ref, inc_ref, table_ref):
+def observe_kernel(scale, member_ref, list_ref, got_ref, ens_ref, slot_ref, value_ref, out_ref, inc_ref, table_ref):
+    caches = [{} for m in range(GROUP)]
     for t in range(COLS):
         total = [jnp.zeros((8, LANES), F32) for f in range(FLD)]
         for m in range(GROUP):
-            local = unpack_tile(got_ref, m, t, {})
+            local = unpack_tile(got_ref, m, t, caches[m])
             for pair in range(FLD // 2):
                 ens = ens_ref[m, pair, :, t * LANES : (t + 1) * LANES].astype(F32)
                 total[2 * pair] += ens[:8] * local
@@ -320,15 +347,19 @@
                 out_ref[pl.ds(pair[h], 1), :] = value[:, h * LANES : (h + 1) * LANES]
 
     over_live(n, body)
-
-
-def adjoint_kernel(scale, count_ref, list_ref, m0, m1, m2, m3, value_ref, var_ref, slot_ref, ens_ref, out_ref, dep_ref,
+    for t in range(0, TILES, 8):
+        for r in range(ROWS):
+            at = pl.ds(t * OBS_ROWS + member_ref[0] * 2 + r, 8, stride=OBS_ROWS)
+            out_ref[at, :] = out_ref[at, :] - value_ref[pl.ds(t * 2 + r, 8, stride=2), :]
+
+
+def adjoint_kernel(scale, count_ref, list_ref, m0, m1, m2, m3, var_ref, slot_ref, ens_ref, out_ref, dep_ref,
                    acc_ref, table_ref, adj_ref, proj_ref):
     slot_at = lax.broadcasted_iota(I32, (OBS_ROWS, LANES), 0) * LANES + lax.broadcasted_iota(I32, (OBS_ROWS, LANES), 1)
     for s in range(TILES):
         at = slice(s * OBS_ROWS, (s + 1) * OBS_ROWS)
-        model = (m0[at, :] + m1[at, :]) + (m2[at, :] + m3[at, :])
-        weighted = var_ref[at, :] * (value_ref[at, :] - model)
+        excess = (m0[at, :] + m1[at, :]) + (m2[at, :] + m3[at, :])
+        weighted = var_ref[at, :] * -excess
         dep_ref[at, :] = jnp.where(slot_at < count_ref[s], weighted, 0.0)
     acc_ref[...] = jnp.zeros_like(acc_ref)
     n = list_ref[LISTED - 1]
@@ -413,6 +444,7 @@
     me = lax.axis_index("tile")
     steps = lax.dynamic_slice(step_count, (lax.rem(me, LEV),), (1,))
     counts = obs_count[0]
+    member = lax.axis_index("member").reshape(1)
     wide = ((0, 0), (0, COLS * LANES - LON))
     ens = jnp.pad(ensemble.reshape(GROUP, 2, 16, LON), ((0, 0), (0, 0)) + wide)
     value = obs_value.reshape(TILES * OBS_ROWS, LANES)
@@ -422,11 +454,18 @@
     sent = pl.pallas_call(
         pack_kernel,
         out_shape=shape(LAT * THERE, LANES),
-        in_specs=[VMEM] * 3,
-        out_specs=VMEM,
-        compiler_params=params(16),
+        in_specs=[SMEM] + [HBM] * 3,
+        out_specs=HBM,
+        scratch_shapes=[
+            pltpu.VMEM(alpha.shape, F32),
+            pltpu.VMEM(value.shape, F32),
+            pltpu.VMEM(var.shape, F32),
+            pltpu.VMEM((LAT * THERE, LANES), F32),
+            pltpu.SemaphoreType.DMA((5,)),
+        ],
+        compiler_params=params(63),
         name="pack",
-    )(alpha, value, var)
+    )(member, alpha, value, var)
     got = exchange(sent)
 
     slots, listed = pl.pallas_call(
@@ -442,7 +481,7 @@
     buf = [pltpu.VMEM((DEEP, DEEP, 8, LANES), F32)] * 2 + [pltpu.VMEM((DEEP, LANES, LANES), F32)]
     moved, value, var = pl.pallas_call(
         diffuse_first_kernel,
-        out_shape=(shape(LAT * BACK, LANES), flat, flat),
+        out_shape=(shape(LAT * BACK, LANES), shape(LAT, LANES), flat),
         in_specs=[SMEM, VMEM],
         out_specs=[VMEM] * 3,
         scratch_shapes=buf,
@@ -454,18 +493,18 @@
     mine = pl.pallas_call(
         lambda *refs: observe_kernel(scale, *refs),
         out_shape=flat,
-        in_specs=[SMEM] + [VMEM] * 3,
+        in_specs=[SMEM] * 2 + [VMEM] * 4,
         out_specs=VMEM,
         scratch_shapes=[pltpu.VMEM((COLS, 32, LANES), F32), pltpu.VMEM((2 * HI, LANES), F32)],
         compiler_params=params(16),
         name="observe",
-    )(listed, got, ens, slots)
+    )(member, listed, got, ens, slots, value)
     others = [lax.ppermute(mine, "member", [(i, (i + k) % 4) for i in range(4)]) for k in (1, 3, 2)]
 
     sent, departure = pl.pallas_call(
         lambda *refs: adjoint_kernel(scale, *refs),
         out_shape=(shape(LAT * BACK, LANES), flat),
-        in_specs=[SMEM] * 2 + [VMEM] * 8,
+        in_specs=[SMEM] * 2 + [VMEM] * 7,
         out_specs=[VMEM] * 2,
         scratch_shapes=[
             pltpu.VMEM((4 * LO, HI), F32),
@@ -475,7 +514,7 @@
         ],
         compiler_params=params(24),
         name="adjoint",
-    )(counts, listed, mine, *others, value, var, slots, ens)
+    )(counts, listed, mine, *others, var, slots, ens)
     got = exchange(sent)
 
     moved = pl.pallas_call(

time: 130 us -> 126 us (0.969)
  waiting for transfers between devices: 45.5 us -> 41 us
  Pallas kernels: 29.4 us -> 31.2 us
    all_to_all x3, waiting for transfers between devices: 40.7 us -> 36.1 us  [exchange(): lax.all_to_all(x, 'tile', 0, 0, tiled=True).reshape(TILES * rows, LANES)]
    unnamed x18 -> x10, local copies, waits for them, and re-layouts: 3.03 us -> 0.02 us
    reshape x1, local copies, waits for them, and re-layouts: 2.48 us -> 5.23 us  [shards(): ens = jnp.pad(ensemble.reshape(GROUP, 2, 16, LON), ((0, 0), (0, 0)) + wide)]
  transfers between devices with their start and end apart: 6 -> 6, of which waited for: 5 -> 5; matrix products, arithmetic and copies ran while one was open for 4% -> 7% of each run, Pallas kernels for 3% -> 3%
where the time goes in v5:
time: 126 us; the launch traced here: 125 us
  waiting for transfers between devices  41 us (33%)
  Pallas kernels  31.2 us (25%)
  starting transfers between devices  22 us (17%)
  blocking collectives  21.7 us (17%)
  local copies, waits for them, and re-layouts  8.33 us (7%)
    all_to_all x3, waiting for transfers between devices, exchange(): lax.all_to_all(x, 'tile', 0, 0, tiled=True).reshape(TILES * rows, LANES)  36.1 us
    all_to_all x1, blocking collectives, exchange(): lax.all_to_all(x, 'tile', 0, 0, tiled=True).reshape(TILES * rows, LANES)  21.7 us
    all_to_all x3, starting transfers between devices, exchange(): lax.all_to_all(x, 'tile', 0, 0, tiled=True).reshape(TILES * rows, LANES)  17.6 us
    pallas_call x1, Pallas kernels, shards(): pl.pallas_call(lambda *refs: observe_kernel(scale, *refs), out_shape=flat...  7.43 us
    pallas_call x1, Pallas kernels, shards(): pl.pallas_call(lambda *refs: adjoint_kernel(scale, *refs), out_shape=(sha...  6.74 us
    reshape x1, local copies, waits for them, and re-layouts, shards(): ens = jnp.pad(ensemble.reshape(GROUP, 2, 16, LON), ((0, 0), (0, 0)) + wide)  5.23 us
    ppermute x3, waiting for transfers between devices, shards(): lax.ppermute(mine, 'member', [(i, (i + k) % 4) for i in range(4)])  4.86 us
    pallas_call x1, Pallas kernels, shards(): pl.pallas_call(diffuse_kernel, out_shape=shape(LAT * BACK, LANES), in_spe...  4.54 us
  transfers between devices with their start and end apart: 6, of which 5 were waited for; matrix products, arithmetic and copies ran while one was open for 7% of the time, Pallas kernels for 3%

profile of v5, /device:TPU:1, one launch (start us, length us, event | category | flops | bytes accessed | tf_op | source)
XLA Modules:
  0.0 125.0 jit_solution(5083021853362640488)
XLA Ops:
  0.6 0.0 copy-start.4
  0.6 2.6 %pack.1 = f32[2176,128]{1,0:T(8,128)} custom-call(s32[1]{0:T(128)} %bitcast.3.member_ref.refs_0_, f32[20,4,2,1440]{3,2,1,0:T(2,128)} %alpha_ref.1, f32[256,128]{1,0:T(8,128)} %bitcast.23, f32[256,128]{1,0:T(8,128)} %bitcast.24), custom_call_target="tpu_custom_call" | custom-call | tf_op jit(solution)/shard_map/pack/pallas_call | solution.py:454
  3.2 9.4 %all-to-all-start = ((f32[32,34,2,128]{3,2,1,0:T(2,128)}), f32[32,34,2,128]{3,2,1,0:T(2,128)S(1)}, u32[]{:S(2)}, u32[]{:S(2)}) async-start(f32[32,34,2,128]{3,2,1,0:T(2,128)} %bitcast.22), calls=%async_computation | async-start | bytes 2228224 | tf_op jit(solution)/shard_map/all_to_all | solution.py:438
  12.7 0.0 copy-done.4
  12.7 0.6 dynamic_slice.3.steps_ref
  13.3 17.0 %all-to-all-done = f32[32,34,2,128]{3,2,1,0:T(2,128)S(1)} async-done(((f32[32,34,2,128]{3,2,1,0:T(2,128)}), f32[32,34,2,128]{3,2,1,0:T(2,128)S(1)}, u32[]{:S(2)}, u32[]{:S(2)}) %all-to-all-start) | async-done | bytes 1114144 | tf_op jit(solution)/shard_map/all_to_all | solution.py:438
  30.3 4.5 %diffuse_first.1 = (f32[1856,128]{1,0:T(8,128)}, f32[64,128]{1,0:T(8,128)S(1)}, f32[256,128]{1,0:T(8,128)S(1)}) custom-call(s32[1]{0:T(128)} %dynamic_slice.3.steps_ref, f32[2176,128]{1,0:T(8,128)S(1)} %bitcast.14), custom_call_target="tpu_custom_call" | custom-call | tf_op jit(solution)/shard_map/diffuse_first/pallas_call | solution.py:482
  34.8 4.4 %all-to-all-start.1 = ((f32[32,29,2,128]{3,2,1,0:T(2,128)}), f32[32,29,2,128]{3,2,1,0:T(2,128)}, u32[]{:S(2)}, u32[]{:S(2)}) async-start(f32[32,29,2,128]{3,2,1,0:T(2,128)} %bitcast.8), calls=%async_computation.1 | async-start | bytes 1900544 | tf_op jit(solution)/shard_map/all_to_all | solution.py:438
  39.2 5.2 %reshape.50 = bf16[20,2,16,1440]{3,2,1,0:T(8,128)(2,1)} reshape(bf16[20,4,4,2,1440]{4,3,2,1,0:T(2,128)(2,1)} %param.9) | data formatting | bytes 3686400 | tf_op jit(solution)/shard_map/reshape | solution.py:449
  44.5 0.0 copy-start.1
  44.5 0.0 copy-start.2
  44.5 0.0 copy-start.3
  44.5 1.8 %pad.4.refs_3_.refs_8_ = bf16[20,2,16,1536]{3,2,1,0:T(8,128)(2,1)S(1)} pad(bf16[20,2,16,1440]{3,2,1,0:T(8,128)(2,1)} %reshape.50, bf16[]{:T(256)} %constant.17.clone.1), padding=0_0x0_0x0_0x0_96 | pad | bytes 3809282 | tf_op jit(solution)/shard_map/jit(_pad)/pad | solution.py:449
  46.3 0.0 copy-done.1
  46.3 0.0 copy-done.2
  46.3 0.0 copy-done.3
  46.3 4.1 %slots.1 = (f32[256,8,128]{2,1,0:T(8,128)S(1)}, s32[272]{0:T(512)S(1)}) custom-call(s32[32]{0:T(128)S(1)} %bitcast.20, s32[32,4,1024]{2,1,0:T(4,128)S(1)} %bitcast.18, f32[32,4,1024]{2,1,0:T(4,128)S(1)} %bitcast.19), custom_call_target="tpu_custom_call" | custom-call | flops 8000000 | bytes 2097152 | tf_op jit(solution)/shard_map/slots/pallas_call | solution.py:471
  50.4 4.1 %all-to-all-done.1 = f32[32,29,2,128]{3,2,1,0:T(2,128)} async-done(((f32[32,29,2,128]{3,2,1,0:T(2,128)}), f32[32,29,2,128]{3,2,1,0:T(2,128)}, u32[]{:S(2)}, u32[]{:S(2)}) %all-to-all-start.1) | async-done | bytes 950304 | tf_op jit(solution)/shard_map/all_to_all | solution.py:438
  54.5 7.4 %observe.1.refs_2_ = f32[256,128]{1,0:T(8,128)S(1)} custom-call(s32[1]{0:T(128)} %bitcast.3.member_ref.refs_0_, s32[272]{0:T(512)S(1)} %get-tuple-element.9.refs_1_, f32[1856,128]{1,0:T(8,128)} %bitcast.9.refs_2_, bf16[20,2,16,1536]{3,2,1,0:T(8,128)(2,1)S(1)} %pad.4.refs_3_.refs_8_, f32[256,8,128]{2,1,0:T(8,128)S(1)} %get-tuple-element.11.refs_4_.refs_7_, ...), custom_call_target="tpu_custom_call" | custom-call | tf_op jit(solution)/shard_map/observe/pallas_call | solution.py:493
  62.0 3.0 %collective-permute-start.2 = (f32[256,128]{1,0:T(8,128)S(1)}, f32[256,128]{1,0:T(8,128)S(1)}, u32[]{:S(2)}, u32[]{:S(2)}) collective-permute-start(f32[256,128]{1,0:T(8,128)S(1)} %observe.1.refs_2_), channel_id=1, source_target_pairs={{0,64},{32,96},{64,0},{96,32},{1,65},{33,97},{65,1},{97,33},{2,66}... | collective-permute-start | bytes 393224 | tf_op jit(solution)/shard_map/ppermute | solution.py:502
  65.0 0.8 collective-permute-start.1
  65.7 0.7 collective-permute-start
  66.4 1.7 %collective-permute-done.2.refs_5_ = f32[256,128]{1,0:T(8,128)S(1)} collective-permute-done((f32[256,128]{1,0:T(8,128)S(1)}, f32[256,128]{1,0:T(8,128)S(1)}, u32[]{:S(2)}, u32[]{:S(2)}) %collective-permute-start.2) | collective-permute-done | bytes 131104 | tf_op jit(solution)/shard_map/ppermute | solution.py:502
  68.1 3.2 %collective-permute-done.1.refs_4_ = f32[256,128]{1,0:T(8,128)S(1)} collective-permute-done((f32[256,128]{1,0:T(8,128)S(1)}, f32[256,128]{1,0:T(8,128)S(1)}, u32[]{:S(2)}, u32[]{:S(2)}) %collective-permute-start.1) | collective-permute-done | bytes 131104 | tf_op jit(solution)/shard_map/ppermute | solution.py:502
  71.3 0.0 collective-permute-done.refs_3_
  71.3 6.7 %adjoint.1 = (f32[1856,128]{1,0:T(8,128)S(1)}, f32[256,128]{1,0:T(8,128)S(1)}) custom-call(s32[32]{0:T(128)S(1)} %bitcast.21, s32[272]{0:T(512)S(1)} %get-tuple-element.9.refs_1_, f32[256,128]{1,0:T(8,128)S(1)} %observe.1.refs_2_, f32[256,128]{1,0:T(8,128)S(1)} %collective-permute-done.refs_3_, f32[256,128]{1,0:T(8,128)S(1)} %collective-permute-done.1.refs_4_, ...), custom_call_target="tpu_custom_call" | custom-call | tf_op jit(solution)/shard_map/adjoint/pallas_call | solution.py:504
  78.0 21.7 %all_to_all.20 = f32[32,29,2,128]{3,2,1,0:T(2,128)S(1)} all-to-all(f32[32,29,2,128]{3,2,1,0:T(2,128)S(1)} %bitcast.17), channel_id=1, replica_groups=mesh['member'=4,'tile'=32] {'tile'}, dimensions={0} | all-to-all | bytes 1900544 | tf_op jit(solution)/shard_map/all_to_all | solution.py:438
  99.7 0.0 copy-start
  99.7 4.5 %diffuse.1 = f32[1856,128]{1,0:T(8,128)} custom-call(s32[1]{0:T(128)} %dynamic_slice.3.steps_ref, f32[1856,128]{1,0:T(8,128)S(1)} %bitcast.16), custom_call_target="tpu_custom_call" | custom-call | tf_op jit(solution)/shard_map/diffuse/pallas_call | solution.py:520
  104.2 3.7 %all-to-all-start.3 = ((f32[32,29,2,128]{3,2,1,0:T(2,128)}), f32[32,29,2,128]{3,2,1,0:T(2,128)S(1)}, u32[]{:S(2)}, u32[]{:S(2)}) async-start(f32[32,29,2,128]{3,2,1,0:T(2,128)} %bitcast.12), calls=%async_computation.3 | async-start | bytes 1900544 | tf_op jit(solution)/shard_map/all_to_all | solution.py:438
  108.0 0.7 reshape.55
  108.6 14.9 %all-to-all-done.3 = f32[32,29,2,128]{3,2,1,0:T(2,128)S(1)} async-done(((f32[32,29,2,128]{3,2,1,0:T(2,128)}), f32[32,29,2,128]{3,2,1,0:T(2,128)S(1)}, u32[]{:S(2)}, u32[]{:S(2)}) %all-to-all-start.3) | async-done | bytes 950304 | tf_op jit(solution)/shard_map/all_to_all | solution.py:438
  123.6 0.0 copy-done
  123.6 1.4 %gradient.1 = f32[20,4,2,1440]{3,2,1,0:T(2,128)} custom-call(f32[20,4,2,1440]{3,2,1,0:T(2,128)S(1)} %copy-done, f32[1856,128]{1,0:T(8,128)S(1)} %bitcast.15), custom_call_target="tpu_custom_call" | custom-call | tf_op jit(solution)/shard_map/gradient/pallas_call | solution.py:531
Async XLA Ops:
  0.6 12.1 %copy-start.4 = (s32[4]{0:T(128)S(1)}, s32[4]{0:T(128)}, u32[]{:S(2)}) copy-start(s32[4]{0:T(128)} %param.10) | copy-start | bytes 52
  3.2 27.1 %all-to-all-start = ((f32[32,34,2,128]{3,2,1,0:T(2,128)}), f32[32,34,2,128]{3,2,1,0:T(2,128)S(1)}, u32[]{:S(2)}, u32[]{:S(2)}) async-start(f32[32,34,2,128]{3,2,1,0:T(2,128)} %bitcast.22), calls=%async_computation | async-start | bytes 2228224 | tf_op jit(solution)/shard_map/all_to_all | solution.py:438
  34.8 19.7 %all-to-all-start.1 = ((f32[32,29,2,128]{3,2,1,0:T(2,128)}), f32[32,29,2,128]{3,2,1,0:T(2,128)}, u32[]{:S(2)}, u32[]{:S(2)}) async-start(f32[32,29,2,128]{3,2,1,0:T(2,128)} %bitcast.8), calls=%async_computation.1 | async-start | bytes 1900544 | tf_op jit(solution)/shard_map/all_to_all | solution.py:438
  44.5 1.8 %copy-start.1 = (s32[1,32,4,1024]{3,2,1,0:T(4,128)S(1)}, s32[1,32,4,1024]{3,2,1,0:T(4,128)}, u32[]{:S(2)}) copy-start(s32[1,32,4,1024]{3,2,1,0:T(4,128)} %param.11) | copy-start | bytes 1572868
  44.5 1.8 %copy-start.2 = (f32[1,32,4,1024]{3,2,1,0:T(4,128)S(1)}, f32[1,32,4,1024]{3,2,1,0:T(4,128)}, u32[]{:S(2)}) copy-start(f32[1,32,4,1024]{3,2,1,0:T(4,128)} %param.12) | copy-start | bytes 1572868
  44.5 1.9 %copy-start.3 = (s32[1,32]{1,0:T(1,128)S(1)}, s32[1,32]{1,0:T(1,128)}, u32[]{:S(2)}) copy-start(s32[1,32]{1,0:T(1,128)} %param.13) | copy-start | bytes 388
  62.0 6.2 %collective-permute-start.2 = (f32[256,128]{1,0:T(8,128)S(1)}, f32[256,128]{1,0:T(8,128)S(1)}, u32[]{:S(2)}, u32[]{:S(2)}) collective-permute-start(f32[256,128]{1,0:T(8,128)S(1)} %observe.1.refs_2_), channel_id=1, source_target_pairs={{0,64},{32,96},{64,0},{96,32},{1,65},{33,97},{65,1},{97,33},{2,66}... | collective-permute-start | bytes 393224 | tf_op jit(solution)/shard_map/ppermute | solution.py:502
  65.0 6.3 %collective-permute-start.1 = (f32[256,128]{1,0:T(8,128)S(1)}, f32[256,128]{1,0:T(8,128)S(1)}, u32[]{:S(2)}, u32[]{:S(2)}) collective-permute-start(f32[256,128]{1,0:T(8,128)S(1)} %observe.1.refs_2_), channel_id=1, source_target_pairs={{0,96},{32,0},{64,32},{96,64},{1,97},{33,1},{65,33},{97,65},{2,98}... | collective-permute-start | bytes 393224 | tf_op jit(solution)/shard_map/ppermute | solution.py:502
  65.7 5.6 %collective-permute-start = (f32[256,128]{1,0:T(8,128)S(1)}, f32[256,128]{1,0:T(8,128)S(1)}, u32[]{:S(2)}, u32[]{:S(2)}) collective-permute-start(f32[256,128]{1,0:T(8,128)S(1)} %observe.1.refs_2_), channel_id=1, source_target_pairs={{0,32},{32,64},{64,96},{96,0},{1,33},{33,65},{65,97},{97,1},{2,34}... | collective-permute-start | bytes 393224 | tf_op jit(solution)/shard_map/ppermute | solution.py:502
  99.7 23.9 %copy-start = (f32[20,4,2,1440]{3,2,1,0:T(2,128)S(1)}, f32[20,4,2,1440]{3,2,1,0:T(2,128)}, u32[]{:S(2)}) copy-start(f32[20,4,2,1440]{3,2,1,0:T(2,128)} %alpha_ref.1) | copy-start | bytes 2764804
  104.2 19.3 %all-to-all-start.3 = ((f32[32,29,2,128]{3,2,1,0:T(2,128)}), f32[32,29,2,128]{3,2,1,0:T(2,128)S(1)}, u32[]{:S(2)}, u32[]{:S(2)}) async-start(f32[32,29,2,128]{3,2,1,0:T(2,128)} %bitcast.12), calls=%async_computation.3 | async-start | bytes 1900544 | tf_op jit(solution)/shard_map/all_to_all | solution.py:438

commit v6 on v5

--- a/solution.py
+++ b/solution.py
@@ -163,7 +163,7 @@
         line = [west] + here + [east]
         for a in range(DEEP):
             near = (above[a] + below[a]) + (line[a] + line[a + 2])
-            dst[g, a] = 0.2 * near + (1.0 - 4.0 * 0.2) * here[a]
+            dst[g, a] = near + here[a]
         above, here = here, below
 
 
@@ -188,26 +188,20 @@
 
     lax.fori_loop(0, lax.div(count, 2), pair, 0)
 
-    def put(src):
-        for g in range(DEEP):
-            for a in range(DEEP):
-                turned[g, pl.ds(a, 8, stride=DEEP), :] = src[g, a]
-        for g in range(DEEP):
-            lines = turned[g].T
-            for q in range(blocks):
-                at = (DEEP * q + g) * BACK
-                out_ref[at : at + LINE, :] = lines[q * WIDE : q * WIDE + LINE]
-
-    odd = lax.rem(count, 2)
-
-    @pl.when(odd == 1)
+    @pl.when(lax.rem(count, 2) == 1)
     def _():
         diffuse_step(one, two)
-        put(two)
-
-    @pl.when(odd == 0)
-    def _():
-        put(one)
+        one[...] = two[...]
+
+    factor = lax.fori_loop(0, count, lambda k, x: x * 0.2, jnp.float32(1.0))
+    for g in range(DEEP):
+        for a in range(DEEP):
+            turned[g, pl.ds(a, 8, stride=DEEP), :] = one[g, a] * factor
+    for g in range(DEEP):
+        lines = turned[g].T
+        for q in range(blocks):
+            at = (DEEP * q + g) * BACK
+            out_ref[at : at + LINE, :] = lines[q * WIDE : q * WIDE + LINE]
 
 
 def diffuse_first_kernel(steps_ref, in_ref, out_ref, value_ref, var_ref, one, two, turned):
@@ -418,7 +412,8 @@
     pack_rows(lambda m, t: proj_ref[t, m * 8 : m * 8 + 8, :], store, BACK)
 
 
-def gradient_kernel(alpha_ref, got_ref, out_ref):
+def gradient_kernel(alpha_ref, got_ref, out_hbm, out_ref, sems):
+    stores = []
     for m in range(GROUP):
         cache = {}
         for t in range(COLS):
@@ -426,6 +421,12 @@
             tile = unpack_tile(got_ref, m, t, cache)
             at = (m, slice(None), slice(None), slice(t * LANES, t * LANES + width))
             out_ref[at] = alpha_ref[at] - tile[:, :width].reshape(LEV, ROWS, width)
+        if m % MGRP == MGRP - 1:
+            at = slice(m + 1 - MGRP, m + 1)
+            stores.append(pltpu.make_async_copy(out_ref.at[at], out_hbm.at[at], sems.at[len(stores)]))
+            stores[-1].start()
+    for done in stores:
+        done.wait()
 
 
 def shape(*dims, dtype=F32):
@@ -532,7 +533,8 @@
         gradient_kernel,
         out_shape=shape(*alpha.shape),
         in_specs=[VMEM] * 2,
-        out_specs=VMEM,
+        out_specs=HBM,
+        scratch_shapes=[pltpu.VMEM(alpha.shape, F32), pltpu.SemaphoreType.DMA((PIECES,))],
         compiler_params=params(16),
         name="gradient",
     )(alpha, got)

time: 126 us -> 124 us (0.984)
  Pallas kernels: 31.2 us -> 29.5 us
where the time goes in v6:
time: 124 us; the launch traced here: 123 us
  waiting for transfers between devices  40.6 us (33%)
  Pallas kernels  29.5 us (24%)
  starting transfers between devices  22 us (18%)
  blocking collectives  22 us (18%)
  local copies, waits for them, and re-layouts  8.33 us (7%)
    all_to_all x3, waiting for transfers between devices, exchange(): lax.all_to_all(x, 'tile', 0, 0, tiled=True).reshape(TILES * rows, LANES)  36.1 us
    all_to_all x1, blocking collectives, exchange(): lax.all_to_all(x, 'tile', 0, 0, tiled=True).reshape(TILES * rows, LANES)  22 us
    all_to_all x3, starting transfers between devices, exchange(): lax.all_to_all(x, 'tile', 0, 0, tiled=True).reshape(TILES * rows, LANES)  17.6 us
    pallas_call x1, Pallas kernels, shards(): pl.pallas_call(lambda *refs: observe_kernel(scale, *refs), out_shape=flat...  7.08 us
    pallas_call x1, Pallas kernels, shards(): pl.pallas_call(lambda *refs: adjoint_kernel(scale, *refs), out_shape=(sha...  6.43 us
    reshape x1, local copies, waits for them, and re-layouts, shards(): ens = jnp.pad(ensemble.reshape(GROUP, 2, 16, LON), ((0, 0), (0, 0)) + wide)  5.23 us
    ppermute x3, waiting for transfers between devices, shards(): lax.ppermute(mine, 'member', [(i, (i + k) % 4) for i in range(4)])  4.55 us
    ppermute x3, starting transfers between devices, shards(): lax.ppermute(mine, 'member', [(i, (i + k) % 4) for i in range(4)])  4.46 us
  transfers between devices with their start and end apart: 6, of which 5 were waited for; matrix products, arithmetic and copies ran while one was open for 7% of the time, Pallas kernels for 3%

profile of v6, /device:TPU:1, one launch (start us, length us, event | category | flops | bytes accessed | tf_op | source)
XLA Modules:
  0.0 123.4 jit_solution(7506679267709947368)
XLA Ops:
  0.6 0.0 copy-start.4
  0.6 2.6 %pack.1 = f32[2176,128]{1,0:T(8,128)} custom-call(s32[1]{0:T(128)} %bitcast.3.member_ref.refs_0_, f32[20,4,2,1440]{3,2,1,0:T(2,128)} %alpha_ref.1, f32[256,128]{1,0:T(8,128)} %bitcast.23, f32[256,128]{1,0:T(8,128)} %bitcast.24), custom_call_target="tpu_custom_call" | custom-call | tf_op jit(solution)/shard_map/pack/pallas_call | solution.py:455
  3.2 9.4 %all-to-all-start = ((f32[32,34,2,128]{3,2,1,0:T(2,128)}), f32[32,34,2,128]{3,2,1,0:T(2,128)S(1)}, u32[]{:S(2)}, u32[]{:S(2)}) async-start(f32[32,34,2,128]{3,2,1,0:T(2,128)} %bitcast.22), calls=%async_computation | async-start | bytes 2228224 | tf_op jit(solution)/shard_map/all_to_all | solution.py:439
  12.7 0.0 copy-done.4
  12.7 0.6 dynamic_slice.3.steps_ref
  13.3 17.0 %all-to-all-done = f32[32,34,2,128]{3,2,1,0:T(2,128)S(1)} async-done(((f32[32,34,2,128]{3,2,1,0:T(2,128)}), f32[32,34,2,128]{3,2,1,0:T(2,128)S(1)}, u32[]{:S(2)}, u32[]{:S(2)}) %all-to-all-start) | async-done | bytes 1114144 | tf_op jit(solution)/shard_map/all_to_all | solution.py:439
  30.3 4.0 %diffuse_first.1 = (f32[1856,128]{1,0:T(8,128)}, f32[64,128]{1,0:T(8,128)S(1)}, f32[256,128]{1,0:T(8,128)S(1)}) custom-call(s32[1]{0:T(128)} %dynamic_slice.3.steps_ref, f32[2176,128]{1,0:T(8,128)S(1)} %bitcast.14), custom_call_target="tpu_custom_call" | custom-call | tf_op jit(solution)/shard_map/diffuse_first/pallas_call | solution.py:483
  34.4 4.4 %all-to-all-start.1 = ((f32[32,29,2,128]{3,2,1,0:T(2,128)}), f32[32,29,2,128]{3,2,1,0:T(2,128)}, u32[]{:S(2)}, u32[]{:S(2)}) async-start(f32[32,29,2,128]{3,2,1,0:T(2,128)} %bitcast.8), calls=%async_computation.1 | async-start | bytes 1900544 | tf_op jit(solution)/shard_map/all_to_all | solution.py:439
  38.8 5.2 %reshape.50 = bf16[20,2,16,1440]{3,2,1,0:T(8,128)(2,1)} reshape(bf16[20,4,4,2,1440]{4,3,2,1,0:T(2,128)(2,1)} %param.9) | data formatting | bytes 3686400 | tf_op jit(solution)/shard_map/reshape | solution.py:450
  44.0 0.0 copy-start.1
  44.0 0.0 copy-start.2
  44.0 0.0 copy-start.3
  44.0 1.8 %pad.4.refs_3_.refs_8_ = bf16[20,2,16,1536]{3,2,1,0:T(8,128)(2,1)S(1)} pad(bf16[20,2,16,1440]{3,2,1,0:T(8,128)(2,1)} %reshape.50, bf16[]{:T(256)} %constant.17.clone.1), padding=0_0x0_0x0_0x0_96 | pad | bytes 3809282 | tf_op jit(solution)/shard_map/jit(_pad)/pad | solution.py:450
  45.9 0.0 copy-done.1
  45.9 0.0 copy-done.2
  45.9 0.0 copy-done.3
  45.9 4.1 %slots.1 = (f32[256,8,128]{2,1,0:T(8,128)S(1)}, s32[272]{0:T(512)S(1)}) custom-call(s32[32]{0:T(128)S(1)} %bitcast.20, s32[32,4,1024]{2,1,0:T(4,128)S(1)} %bitcast.18, f32[32,4,1024]{2,1,0:T(4,128)S(1)} %bitcast.19), custom_call_target="tpu_custom_call" | custom-call | flops 8000000 | bytes 2097152 | tf_op jit(solution)/shard_map/slots/pallas_call | solution.py:472
  50.0 3.9 %all-to-all-done.1 = f32[32,29,2,128]{3,2,1,0:T(2,128)} async-done(((f32[32,29,2,128]{3,2,1,0:T(2,128)}), f32[32,29,2,128]{3,2,1,0:T(2,128)}, u32[]{:S(2)}, u32[]{:S(2)}) %all-to-all-start.1) | async-done | bytes 950304 | tf_op jit(solution)/shard_map/all_to_all | solution.py:439
  53.9 7.1 %observe.1.refs_2_ = f32[256,128]{1,0:T(8,128)S(1)} custom-call(s32[1]{0:T(128)} %bitcast.3.member_ref.refs_0_, s32[272]{0:T(512)S(1)} %get-tuple-element.9.refs_1_, f32[1856,128]{1,0:T(8,128)} %bitcast.9.refs_2_, bf16[20,2,16,1536]{3,2,1,0:T(8,128)(2,1)S(1)} %pad.4.refs_3_.refs_8_, f32[256,8,128]{2,1,0:T(8,128)S(1)} %get-tuple-element.11.refs_4_.refs_7_, ...), custom_call_target="tpu_custom_call" | custom-call | tf_op jit(solution)/shard_map/observe/pallas_call | solution.py:494
  61.0 3.0 %collective-permute-start.2 = (f32[256,128]{1,0:T(8,128)S(1)}, f32[256,128]{1,0:T(8,128)S(1)}, u32[]{:S(2)}, u32[]{:S(2)}) collective-permute-start(f32[256,128]{1,0:T(8,128)S(1)} %observe.1.refs_2_), channel_id=1, source_target_pairs={{0,64},{32,96},{64,0},{96,32},{1,65},{33,97},{65,1},{97,33},{2,66}... | collective-permute-start | bytes 393224 | tf_op jit(solution)/shard_map/ppermute | solution.py:503
  64.0 0.8 collective-permute-start.1
  64.7 0.7 collective-permute-start
  65.4 1.4 %collective-permute-done.2.refs_5_ = f32[256,128]{1,0:T(8,128)S(1)} collective-permute-done((f32[256,128]{1,0:T(8,128)S(1)}, f32[256,128]{1,0:T(8,128)S(1)}, u32[]{:S(2)}, u32[]{:S(2)}) %collective-permute-start.2) | collective-permute-done | bytes 131104 | tf_op jit(solution)/shard_map/ppermute | solution.py:503
  66.8 3.2 %collective-permute-done.1.refs_4_ = f32[256,128]{1,0:T(8,128)S(1)} collective-permute-done((f32[256,128]{1,0:T(8,128)S(1)}, f32[256,128]{1,0:T(8,128)S(1)}, u32[]{:S(2)}, u32[]{:S(2)}) %collective-permute-start.1) | collective-permute-done | bytes 131104 | tf_op jit(solution)/shard_map/ppermute | solution.py:503
  70.0 0.0 collective-permute-done.refs_3_
  70.0 6.4 %adjoint.1 = (f32[1856,128]{1,0:T(8,128)S(1)}, f32[256,128]{1,0:T(8,128)S(1)}) custom-call(s32[32]{0:T(128)S(1)} %bitcast.21, s32[272]{0:T(512)S(1)} %get-tuple-element.9.refs_1_, f32[256,128]{1,0:T(8,128)S(1)} %observe.1.refs_2_, f32[256,128]{1,0:T(8,128)S(1)} %collective-permute-done.refs_3_, f32[256,128]{1,0:T(8,128)S(1)} %collective-permute-done.1.refs_4_, ...), custom_call_target="tpu_custom_call" | custom-call | tf_op jit(solution)/shard_map/adjoint/pallas_call | solution.py:505
  76.4 22.0 %all_to_all.20 = f32[32,29,2,128]{3,2,1,0:T(2,128)S(1)} all-to-all(f32[32,29,2,128]{3,2,1,0:T(2,128)S(1)} %bitcast.17), channel_id=1, replica_groups=mesh['member'=4,'tile'=32] {'tile'}, dimensions={0} | all-to-all | bytes 1900544 | tf_op jit(solution)/shard_map/all_to_all | solution.py:439
  98.4 0.0 copy-start
  98.4 4.1 %diffuse.1 = f32[1856,128]{1,0:T(8,128)} custom-call(s32[1]{0:T(128)} %dynamic_slice.3.steps_ref, f32[1856,128]{1,0:T(8,128)S(1)} %bitcast.16), custom_call_target="tpu_custom_call" | custom-call | tf_op jit(solution)/shard_map/diffuse/pallas_call | solution.py:521
  102.5 3.7 %all-to-all-start.3 = ((f32[32,29,2,128]{3,2,1,0:T(2,128)}), f32[32,29,2,128]{3,2,1,0:T(2,128)S(1)}, u32[]{:S(2)}, u32[]{:S(2)}) async-start(f32[32,29,2,128]{3,2,1,0:T(2,128)} %bitcast.12), calls=%async_computation.3 | async-start | bytes 1900544 | tf_op jit(solution)/shard_map/all_to_all | solution.py:439
  106.3 0.7 reshape.55
  106.9 15.1 %all-to-all-done.3 = f32[32,29,2,128]{3,2,1,0:T(2,128)S(1)} async-done(((f32[32,29,2,128]{3,2,1,0:T(2,128)}), f32[32,29,2,128]{3,2,1,0:T(2,128)S(1)}, u32[]{:S(2)}, u32[]{:S(2)}) %all-to-all-start.3) | async-done | bytes 950304 | tf_op jit(solution)/shard_map/all_to_all | solution.py:439
  122.1 0.0 copy-done
  122.1 1.2 gradient.1
Async XLA Ops:
  0.6 12.1 %copy-start.4 = (s32[4]{0:T(128)S(1)}, s32[4]{0:T(128)}, u32[]{:S(2)}) copy-start(s32[4]{0:T(128)} %param.10) | copy-start | bytes 52
  3.2 27.1 %all-to-all-start = ((f32[32,34,2,128]{3,2,1,0:T(2,128)}), f32[32,34,2,128]{3,2,1,0:T(2,128)S(1)}, u32[]{:S(2)}, u32[]{:S(2)}) async-start(f32[32,34,2,128]{3,2,1,0:T(2,128)} %bitcast.22), calls=%async_computation | async-start | bytes 2228224 | tf_op jit(solution)/shard_map/all_to_all | solution.py:439
  34.4 19.5 %all-to-all-start.1 = ((f32[32,29,2,128]{3,2,1,0:T(2,128)}), f32[32,29,2,128]{3,2,1,0:T(2,128)}, u32[]{:S(2)}, u32[]{:S(2)}) async-start(f32[32,29,2,128]{3,2,1,0:T(2,128)} %bitcast.8), calls=%async_computation.1 | async-start | bytes 1900544 | tf_op jit(solution)/shard_map/all_to_all | solution.py:439
  44.0 1.8 %copy-start.1 = (s32[1,32,4,1024]{3,2,1,0:T(4,128)S(1)}, s32[1,32,4,1024]{3,2,1,0:T(4,128)}, u32[]{:S(2)}) copy-start(s32[1,32,4,1024]{3,2,1,0:T(4,128)} %param.11) | copy-start | bytes 1572868
  44.0 1.8 %copy-start.2 = (f32[1,32,4,1024]{3,2,1,0:T(4,128)S(1)}, f32[1,32,4,1024]{3,2,1,0:T(4,128)}, u32[]{:S(2)}) copy-start(f32[1,32,4,1024]{3,2,1,0:T(4,128)} %param.12) | copy-start | bytes 1572868
  44.0 1.9 %copy-start.3 = (s32[1,32]{1,0:T(1,128)S(1)}, s32[1,32]{1,0:T(1,128)}, u32[]{:S(2)}) copy-start(s32[1,32]{1,0:T(1,128)} %param.13) | copy-start | bytes 388
  61.0 5.8 %collective-permute-start.2 = (f32[256,128]{1,0:T(8,128)S(1)}, f32[256,128]{1,0:T(8,128)S(1)}, u32[]{:S(2)}, u32[]{:S(2)}) collective-permute-start(f32[256,128]{1,0:T(8,128)S(1)} %observe.1.refs_2_), channel_id=1, source_target_pairs={{0,64},{32,96},{64,0},{96,32},{1,65},{33,97},{65,1},{97,33},{2,66}... | collective-permute-start | bytes 393224 | tf_op jit(solution)/shard_map/ppermute | solution.py:503
  64.0 6.0 %collective-permute-start.1 = (f32[256,128]{1,0:T(8,128)S(1)}, f32[256,128]{1,0:T(8,128)S(1)}, u32[]{:S(2)}, u32[]{:S(2)}) collective-permute-start(f32[256,128]{1,0:T(8,128)S(1)} %observe.1.refs_2_), channel_id=1, source_target_pairs={{0,96},{32,0},{64,32},{96,64},{1,97},{33,1},{65,33},{97,65},{2,98}... | collective-permute-start | bytes 393224 | tf_op jit(solution)/shard_map/ppermute | solution.py:503
  64.7 5.2 %collective-permute-start = (f32[256,128]{1,0:T(8,128)S(1)}, f32[256,128]{1,0:T(8,128)S(1)}, u32[]{:S(2)}, u32[]{:S(2)}) collective-permute-start(f32[256,128]{1,0:T(8,128)S(1)} %observe.1.refs_2_), channel_id=1, source_target_pairs={{0,32},{32,64},{64,96},{96,0},{1,33},{33,65},{65,97},{97,1},{2,34}... | collective-permute-start | bytes 393224 | tf_op jit(solution)/shard_map/ppermute | solution.py:503
  98.4 23.7 %copy-start = (f32[20,4,2,1440]{3,2,1,0:T(2,128)S(1)}, f32[20,4,2,1440]{3,2,1,0:T(2,128)}, u32[]{:S(2)}) copy-start(f32[20,4,2,1440]{3,2,1,0:T(2,128)} %alpha_ref.1) | copy-start | bytes 2764804
  102.5 19.5 %all-to-all-start.3 = ((f32[32,29,2,128]{3,2,1,0:T(2,128)}), f32[32,29,2,128]{3,2,1,0:T(2,128)S(1)}, u32[]{:S(2)}, u32[]{:S(2)}) async-start(f32[32,29,2,128]{3,2,1,0:T(2,128)} %bitcast.12), calls=%async_computation.3 | async-start | bytes 1900544 | tf_op jit(solution)/shard_map/all_to_all | solution.py:439

commit v7 on v6

--- a/solution.py
+++ b/solution.py
@@ -290,7 +290,7 @@
     return high, (x - high.astype(F32)).astype(BF16)
 
 
-SIZES = (16, 8, 4, 2)
+SIZES = (32, 16, 8, 4, 2)
 LISTED = BLOCKS + 16
 
 
@@ -513,7 +513,7 @@
             pltpu.VMEM((COLS, 32, LANES), F32),
             pltpu.VMEM((COLS, GROUP * 8, LANES), F32),
         ],
-        compiler_params=params(24),
+        compiler_params=params(32),
         name="adjoint",
     )(counts, listed, mine, *others, var, slots, ens)
     got = exchange(sent)

time: 124 us -> 124 us (level)
  Pallas kernels: 29.5 us -> 25.5 us
  starting transfers between devices: 22 us -> 24.4 us
  blocking collectives: 22 us -> 23.9 us
    all_to_all x3, starting transfers between devices: 17.6 us -> 20 us  [exchange(): lax.all_to_all(x, 'tile', 0, 0, tiled=True).reshape(TILES * rows, LANES)]
    all_to_all x1, blocking collectives: 22 us -> 23.9 us  [exchange(): lax.all_to_all(x, 'tile', 0, 0, tiled=True).reshape(TILES * rows, LANES)]
    pallas_call x1, Pallas kernels: 4.04 us -> 2.77 us  [shards(): pl.pallas_call(diffuse_first_kernel, out_shape=(shape(LAT * BACK, LANES),...]
    pallas_call x1, Pallas kernels: 4.13 us -> 2.86 us  [shards(): pl.pallas_call(diffuse_kernel, out_shape=shape(LAT * BACK, LANES), in_spe...]
where the time goes in v7:
time: 124 us
  waiting for transfers between devices  41.5 us (33%)
  Pallas kernels  25.5 us (21%)
  starting transfers between devices  24.4 us (20%)
  blocking collectives  23.9 us (19%)
  local copies, waits for them, and re-layouts  8.33 us (7%)
    all_to_all x3, waiting for transfers between devices, exchange(): lax.all_to_all(x, 'tile', 0, 0, tiled=True).reshape(TILES * rows, LANES)  37 us
    all_to_all x1, blocking collectives, exchange(): lax.all_to_all(x, 'tile', 0, 0, tiled=True).reshape(TILES * rows, LANES)  23.9 us
    all_to_all x3, starting transfers between devices, exchange(): lax.all_to_all(x, 'tile', 0, 0, tiled=True).reshape(TILES * rows, LANES)  20 us
    pallas_call x1, Pallas kernels, shards(): pl.pallas_call(lambda *refs: observe_kernel(scale, *refs), out_shape=flat...  6.51 us
    pallas_call x1, Pallas kernels, shards(): pl.pallas_call(lambda *refs: adjoint_kernel(scale, *refs), out_shape=(sha...  5.5 us
    reshape x1, local copies, waits for them, and re-layouts, shards(): ens = jnp.pad(ensemble.reshape(GROUP, 2, 16, LON), ((0, 0), (0, 0)) + wide)  5.23 us
    ppermute x3, waiting for transfers between devices, shards(): lax.ppermute(mine, 'member', [(i, (i + k) % 4) for i in range(4)])  4.48 us
    ppermute x3, starting transfers between devices, shards(): lax.ppermute(mine, 'member', [(i, (i + k) % 4) for i in range(4)])  4.46 us
  transfers between devices with their start and end apart: 6, of which 5 were waited for; matrix products, arithmetic and copies ran while one was open for 7% of the time, Pallas kernels for 3%

profile of v7, /device:TPU:1, one launch (start us, length us, event | category | flops | bytes accessed | tf_op | source)
XLA Modules:
  0.0 124.5 jit_solution(4368311943993500527)
XLA Ops:
  0.6 0.0 copy-start.4
  0.6 2.6 %pack.1 = f32[2176,128]{1,0:T(8,128)} custom-call(s32[1]{0:T(128)} %bitcast.3.member_ref.refs_0_, f32[20,4,2,1440]{3,2,1,0:T(2,128)} %alpha_ref.1, f32[256,128]{1,0:T(8,128)} %bitcast.23, f32[256,128]{1,0:T(8,128)} %bitcast.24), custom_call_target="tpu_custom_call" | custom-call | tf_op jit(solution)/shard_map/pack/pallas_call | solution.py:455
  3.2 9.4 %all-to-all-start = ((f32[32,34,2,128]{3,2,1,0:T(2,128)}), f32[32,34,2,128]{3,2,1,0:T(2,128)S(1)}, u32[]{:S(2)}, u32[]{:S(2)}) async-start(f32[32,34,2,128]{3,2,1,0:T(2,128)} %bitcast.22), calls=%async_computation | async-start | bytes 2228224 | tf_op jit(solution)/shard_map/all_to_all | solution.py:439
  12.7 0.0 copy-done.4
  12.7 0.6 dynamic_slice.3.steps_ref
  13.3 17.0 %all-to-all-done = f32[32,34,2,128]{3,2,1,0:T(2,128)S(1)} async-done(((f32[32,34,2,128]{3,2,1,0:T(2,128)}), f32[32,34,2,128]{3,2,1,0:T(2,128)S(1)}, u32[]{:S(2)}, u32[]{:S(2)}) %all-to-all-start) | async-done | bytes 1114144 | tf_op jit(solution)/shard_map/all_to_all | solution.py:439
  30.3 2.8 %diffuse_first.1 = (f32[1856,128]{1,0:T(8,128)}, f32[64,128]{1,0:T(8,128)S(1)}, f32[256,128]{1,0:T(8,128)S(1)}) custom-call(s32[1]{0:T(128)} %dynamic_slice.3.steps_ref, f32[2176,128]{1,0:T(8,128)S(1)} %bitcast.14), custom_call_target="tpu_custom_call" | custom-call | tf_op jit(solution)/shard_map/diffuse_first/pallas_call | solution.py:483
  33.1 5.3 %all-to-all-start.1 = ((f32[32,29,2,128]{3,2,1,0:T(2,128)}), f32[32,29,2,128]{3,2,1,0:T(2,128)}, u32[]{:S(2)}, u32[]{:S(2)}) async-start(f32[32,29,2,128]{3,2,1,0:T(2,128)} %bitcast.8), calls=%async_computation.1 | async-start | bytes 1900544 | tf_op jit(solution)/shard_map/all_to_all | solution.py:439
  38.4 5.2 %reshape.50 = bf16[20,2,16,1440]{3,2,1,0:T(8,128)(2,1)} reshape(bf16[20,4,4,2,1440]{4,3,2,1,0:T(2,128)(2,1)} %param.9) | data formatting | bytes 3686400 | tf_op jit(solution)/shard_map/reshape | solution.py:450
  43.7 0.0 copy-start.1
  43.7 0.0 copy-start.2
  43.7 0.0 copy-start.3
  43.7 1.8 %pad.4.refs_3_.refs_8_ = bf16[20,2,16,1536]{3,2,1,0:T(8,128)(2,1)S(1)} pad(bf16[20,2,16,1440]{3,2,1,0:T(8,128)(2,1)} %reshape.50, bf16[]{:T(256)} %constant.17.clone.1), padding=0_0x0_0x0_0x0_96 | pad | bytes 3809282 | tf_op jit(solution)/shard_map/jit(_pad)/pad | solution.py:450
  45.5 0.0 copy-done.1
  45.5 0.0 copy-done.2
  45.5 0.0 copy-done.3
  45.5 4.1 %slots.1 = (f32[256,8,128]{2,1,0:T(8,128)S(1)}, s32[272]{0:T(512)S(1)}) custom-call(s32[32]{0:T(128)S(1)} %bitcast.20, s32[32,4,1024]{2,1,0:T(4,128)S(1)} %bitcast.18, f32[32,4,1024]{2,1,0:T(4,128)S(1)} %bitcast.19), custom_call_target="tpu_custom_call" | custom-call | flops 8000000 | bytes 2097152 | tf_op jit(solution)/shard_map/slots/pallas_call | solution.py:472
  49.6 4.8 %all-to-all-done.1 = f32[32,29,2,128]{3,2,1,0:T(2,128)} async-done(((f32[32,29,2,128]{3,2,1,0:T(2,128)}), f32[32,29,2,128]{3,2,1,0:T(2,128)}, u32[]{:S(2)}, u32[]{:S(2)}) %all-to-all-start.1) | async-done | bytes 950304 | tf_op jit(solution)/shard_map/all_to_all | solution.py:439
  54.4 6.5 %observe.1.refs_2_ = f32[256,128]{1,0:T(8,128)S(1)} custom-call(s32[1]{0:T(128)} %bitcast.3.member_ref.refs_0_, s32[272]{0:T(512)S(1)} %get-tuple-element.9.refs_1_, f32[1856,128]{1,0:T(8,128)} %bitcast.9.refs_2_, bf16[20,2,16,1536]{3,2,1,0:T(8,128)(2,1)S(1)} %pad.4.refs_3_.refs_8_, f32[256,8,128]{2,1,0:T(8,128)S(1)} %get-tuple-element.11.refs_4_.refs_7_, ...), custom_call_target="tpu_custom_call" | custom-call | tf_op jit(solution)/shard_map/observe/pallas_call | solution.py:494
  60.9 3.0 %collective-permute-start.2 = (f32[256,128]{1,0:T(8,128)S(1)}, f32[256,128]{1,0:T(8,128)S(1)}, u32[]{:S(2)}, u32[]{:S(2)}) collective-permute-start(f32[256,128]{1,0:T(8,128)S(1)} %observe.1.refs_2_), channel_id=1, source_target_pairs={{0,64},{32,96},{64,0},{96,32},{1,65},{33,97},{65,1},{97,33},{2,66}... | collective-permute-start | bytes 393224 | tf_op jit(solution)/shard_map/ppermute | solution.py:503
  63.9 0.8 collective-permute-start.1
  64.7 0.7 collective-permute-start
  65.4 1.3 %collective-permute-done.2.refs_5_ = f32[256,128]{1,0:T(8,128)S(1)} collective-permute-done((f32[256,128]{1,0:T(8,128)S(1)}, f32[256,128]{1,0:T(8,128)S(1)}, u32[]{:S(2)}, u32[]{:S(2)}) %collective-permute-start.2) | collective-permute-done | bytes 131104 | tf_op jit(solution)/shard_map/ppermute | solution.py:503
  66.7 3.2 %collective-permute-done.1.refs_4_ = f32[256,128]{1,0:T(8,128)S(1)} collective-permute-done((f32[256,128]{1,0:T(8,128)S(1)}, f32[256,128]{1,0:T(8,128)S(1)}, u32[]{:S(2)}, u32[]{:S(2)}) %collective-permute-start.1) | collective-permute-done | bytes 131104 | tf_op jit(solution)/shard_map/ppermute | solution.py:503
  69.9 0.0 collective-permute-done.refs_3_
  69.9 5.5 %adjoint.1 = (f32[1856,128]{1,0:T(8,128)S(1)}, f32[256,128]{1,0:T(8,128)S(1)}) custom-call(s32[32]{0:T(128)S(1)} %bitcast.21, s32[272]{0:T(512)S(1)} %get-tuple-element.9.refs_1_, f32[256,128]{1,0:T(8,128)S(1)} %observe.1.refs_2_, f32[256,128]{1,0:T(8,128)S(1)} %collective-permute-done.refs_3_, f32[256,128]{1,0:T(8,128)S(1)} %collective-permute-done.1.refs_4_, ...), custom_call_target="tpu_custom_call" | custom-call | tf_op jit(solution)/shard_map/adjoint/pallas_call | solution.py:505
  75.4 23.9 %all_to_all.20 = f32[32,29,2,128]{3,2,1,0:T(2,128)S(1)} all-to-all(f32[32,29,2,128]{3,2,1,0:T(2,128)S(1)} %bitcast.17), channel_id=1, replica_groups=mesh['member'=4,'tile'=32] {'tile'}, dimensions={0} | all-to-all | bytes 1900544 | tf_op jit(solution)/shard_map/all_to_all | solution.py:439
  99.3 0.0 copy-start
  99.3 2.9 %diffuse.1 = f32[1856,128]{1,0:T(8,128)} custom-call(s32[1]{0:T(128)} %dynamic_slice.3.steps_ref, f32[1856,128]{1,0:T(8,128)S(1)} %bitcast.16), custom_call_target="tpu_custom_call" | custom-call | tf_op jit(solution)/shard_map/diffuse/pallas_call | solution.py:521
  102.1 5.2 %all-to-all-start.3 = ((f32[32,29,2,128]{3,2,1,0:T(2,128)}), f32[32,29,2,128]{3,2,1,0:T(2,128)S(1)}, u32[]{:S(2)}, u32[]{:S(2)}) async-start(f32[32,29,2,128]{3,2,1,0:T(2,128)} %bitcast.12), calls=%async_computation.3 | async-start | bytes 1900544 | tf_op jit(solution)/shard_map/all_to_all | solution.py:439
  107.3 0.7 reshape.55
  108.0 15.1 %all-to-all-done.3 = f32[32,29,2,128]{3,2,1,0:T(2,128)S(1)} async-done(((f32[32,29,2,128]{3,2,1,0:T(2,128)}), f32[32,29,2,128]{3,2,1,0:T(2,128)S(1)}, u32[]{:S(2)}, u32[]{:S(2)}) %all-to-all-start.3) | async-done | bytes 950304 | tf_op jit(solution)/shard_map/all_to_all | solution.py:439
  123.2 0.0 copy-done
  123.2 1.2 gradient.1
Async XLA Ops:
  0.6 12.1 %copy-start.4 = (s32[4]{0:T(128)S(1)}, s32[4]{0:T(128)}, u32[]{:S(2)}) copy-start(s32[4]{0:T(128)} %param.10) | copy-start | bytes 52
  3.2 27.1 %all-to-all-start = ((f32[32,34,2,128]{3,2,1,0:T(2,128)}), f32[32,34,2,128]{3,2,1,0:T(2,128)S(1)}, u32[]{:S(2)}, u32[]{:S(2)}) async-start(f32[32,34,2,128]{3,2,1,0:T(2,128)} %bitcast.22), calls=%async_computation | async-start | bytes 2228224 | tf_op jit(solution)/shard_map/all_to_all | solution.py:439
  33.1 21.3 %all-to-all-start.1 = ((f32[32,29,2,128]{3,2,1,0:T(2,128)}), f32[32,29,2,128]{3,2,1,0:T(2,128)}, u32[]{:S(2)}, u32[]{:S(2)}) async-start(f32[32,29,2,128]{3,2,1,0:T(2,128)} %bitcast.8), calls=%async_computation.1 | async-start | bytes 1900544 | tf_op jit(solution)/shard_map/all_to_all | solution.py:439
  43.7 1.8 %copy-start.1 = (s32[1,32,4,1024]{3,2,1,0:T(4,128)S(1)}, s32[1,32,4,1024]{3,2,1,0:T(4,128)}, u32[]{:S(2)}) copy-start(s32[1,32,4,1024]{3,2,1,0:T(4,128)} %param.11) | copy-start | bytes 1572868
  43.7 1.8 %copy-start.2 = (f32[1,32,4,1024]{3,2,1,0:T(4,128)S(1)}, f32[1,32,4,1024]{3,2,1,0:T(4,128)}, u32[]{:S(2)}) copy-start(f32[1,32,4,1024]{3,2,1,0:T(4,128)} %param.12) | copy-start | bytes 1572868
  43.7 1.9 %copy-start.3 = (s32[1,32]{1,0:T(1,128)S(1)}, s32[1,32]{1,0:T(1,128)}, u32[]{:S(2)}) copy-start(s32[1,32]{1,0:T(1,128)} %param.13) | copy-start | bytes 388
  60.9 5.8 %collective-permute-start.2 = (f32[256,128]{1,0:T(8,128)S(1)}, f32[256,128]{1,0:T(8,128)S(1)}, u32[]{:S(2)}, u32[]{:S(2)}) collective-permute-start(f32[256,128]{1,0:T(8,128)S(1)} %observe.1.refs_2_), channel_id=1, source_target_pairs={{0,64},{32,96},{64,0},{96,32},{1,65},{33,97},{65,1},{97,33},{2,66}... | collective-permute-start | bytes 393224 | tf_op jit(solution)/shard_map/ppermute | solution.py:503
  63.9 5.9 %collective-permute-start.1 = (f32[256,128]{1,0:T(8,128)S(1)}, f32[256,128]{1,0:T(8,128)S(1)}, u32[]{:S(2)}, u32[]{:S(2)}) collective-permute-start(f32[256,128]{1,0:T(8,128)S(1)} %observe.1.refs_2_), channel_id=1, source_target_pairs={{0,96},{32,0},{64,32},{96,64},{1,97},{33,1},{65,33},{97,65},{2,98}... | collective-permute-start | bytes 393224 | tf_op jit(solution)/shard_map/ppermute | solution.py:503
  64.7 5.2 %collective-permute-start = (f32[256,128]{1,0:T(8,128)S(1)}, f32[256,128]{1,0:T(8,128)S(1)}, u32[]{:S(2)}, u32[]{:S(2)}) collective-permute-start(f32[256,128]{1,0:T(8,128)S(1)} %observe.1.refs_2_), channel_id=1, source_target_pairs={{0,32},{32,64},{64,96},{96,0},{1,33},{33,65},{65,97},{97,1},{2,34}... | collective-permute-start | bytes 393224 | tf_op jit(solution)/shard_map/ppermute | solution.py:503
  99.3 23.9 %copy-start = (f32[20,4,2,1440]{3,2,1,0:T(2,128)S(1)}, f32[20,4,2,1440]{3,2,1,0:T(2,128)}, u32[]{:S(2)}) copy-start(f32[20,4,2,1440]{3,2,1,0:T(2,128)} %alpha_ref.1) | copy-start | bytes 2764804
  102.1 21.0 %all-to-all-start.3 = ((f32[32,29,2,128]{3,2,1,0:T(2,128)}), f32[32,29,2,128]{3,2,1,0:T(2,128)S(1)}, u32[]{:S(2)}, u32[]{:S(2)}) async-start(f32[32,29,2,128]{3,2,1,0:T(2,128)} %bitcast.12), calls=%async_computation.3 | async-start | bytes 1900544 | tf_op jit(solution)/shard_map/all_to_all | solution.py:439
